TPU v7x, 32 devices: a whole 2x2x4 slice. The times are simulated.
32 devices in a mesh: dp: 8 (over z, y), fsdp: 4 (over x, core).
Axes of the slice: x: 2, y: 2, z: 4, core: 2. Of those that a mesh axis runs over, the one named last changes fastest.
Arguments:
- tokens: bfloat16 [4096, 2048], P(('dp', 'fsdp')), may hold values from -6 to 6
- upstream: bfloat16 [4096, 512], P(('dp', 'fsdp')), may hold values from -6 to 6
- value_weight: bfloat16 [2048, 512], P('fsdp'), may hold values from -0.125 to 0.125
- forget_label: int32 [8], P('dp'), may hold values 0 or 1
- copy_index: int32 [8], P('dp'), may hold values from 0 to 1, as said below
- adv_rate: float32 [2], replicated, may hold values from 0.5 to 2
Outputs:
- meta_grad: float32 [2048, 512], P('fsdp')
Inputs may be any that keep to these rules, and one draw needn't show every extreme that they name: `copy_index`: each of the 2 copies is named by exactly 4 sequences.
All inputs are finite; a program needn't handle non-finite values. No bound on the sum of `forget_label` on one device may be relied on, other than what follows from the above.
Results may differ from a plain program's by a relative error of at most 0.0056.
Values may be sent and summed in bfloat16 or wider, within the bound.
No kernel may reach another device: no remote copies, remote signals or barrier semaphores. Data moves between devices by JAX's collectives and lax.ppermute only.
A program may use at most 64 MiB of HBM per device.

v0:
```python
import jax
import jax.numpy as jnp
from jax import lax
from jax.sharding import PartitionSpec as P


def first_slope(value):
    sig = jax.nn.sigmoid(value)
    return sig * (1.0 + value * (1.0 - sig))


def second_slope(value):
    sig = jax.nn.sigmoid(value)
    return sig * (1.0 - sig) * (2.0 + value * (1.0 - 2.0 * sig))


def local(tokens, upstream, value_weight, forget_label, copy_index, adv_rate):
    groups = lax.axis_size("fsdp")
    seq_count = lax.axis_size("dp")
    seq_length = tokens.shape[0] * groups
    forget = forget_label[0].astype(jnp.float32)
    onehot = (jnp.arange(adv_rate.shape[0], dtype=jnp.int32) == copy_index[0]).astype(jnp.float32)
    own_rate = jnp.sum(onehot * adv_rate)
    upward = upstream.astype(jnp.float32)

    def project(piece):
        return jnp.dot(tokens, piece, preferred_element_type=jnp.float32)

    primal = project(lax.all_gather(value_weight, "fsdp", axis=0, tiled=True))
    columns = lax.all_to_all(tokens, "fsdp", split_axis=1, concat_axis=0, tiled=True)

    def contract(piece):
        return lax.dot_general(
            columns, piece, (((0,), (0,)), ((), ())), preferred_element_type=jnp.float32
        )

    delta_adv = (forget * upward * first_slope(primal) / seq_length).astype(jnp.bfloat16)
    grad_local = lax.psum_scatter(
        lax.dot_general(
            tokens, delta_adv, (((0,), (0,)), ((), ())), preferred_element_type=jnp.float32
        ),
        "fsdp",
        scatter_dimension=0,
        tiled=True,
    )
    stacked = lax.psum(onehot[:, None, None] * grad_local[None], "dp")
    grad_own = jnp.sum(onehot[:, None, None] * stacked, axis=0)
    attacked = (value_weight.astype(jnp.float32) - own_rate * grad_own).astype(jnp.bfloat16)
    altered = project(lax.all_gather(attacked, "fsdp", axis=0, tiled=True))
    delta_out = ((1.0 - 2.0 * forget) * upward * first_slope(altered) / seq_length).astype(
        jnp.bfloat16
    )
    outer_local = contract(lax.all_gather(delta_out, "fsdp", axis=0, tiled=True))
    outer_all = lax.psum(onehot[:, None, None] * outer_local[None], "dp")
    tangent = jnp.sum(onehot[:, None, None] * outer_all, axis=0).astype(jnp.bfloat16)
    forward_tangent = project(lax.all_gather(tangent, "fsdp", axis=0, tiled=True))
    delta_curv = (forget * upward * second_slope(primal) * forward_tangent / seq_length).astype(
        jnp.bfloat16
    )
    curv_local = contract(lax.all_gather(delta_curv, "fsdp", axis=0, tiled=True))
    curv_sum = lax.psum(own_rate * curv_local, "dp")
    scale = (float(seq_length) / float(seq_count)) ** 0.5
    return scale * (jnp.sum(outer_all, axis=0) - curv_sum)


def solution(mesh):
    in_specs = (
        P(("dp", "fsdp"), None),
        P(("dp", "fsdp"), None),
        P("fsdp", None),
        P("dp"),
        P("dp"),
        P(),
    )
    out_specs = P("fsdp", None)
    return jax.shard_map(local, mesh=mesh, in_specs=in_specs, out_specs=out_specs, check_vma=False)
```

profile of v0, /device:TPU:0, one launch (start us, length us, event | category | flops | bytes accessed | tf_op | source)
XLA Modules:
  0.0 457.3 jit_solution(16305771417579947327)
XLA Ops:
  6.5 0.7 all-gather.4.cloned.1.call-update
  8.0 26.3 %all-gather.4.cloned.1.call-done = bf16[2048,512]{1,0:T(8,128)(2,1)} async-done(((bf16[512,512]{1,0:T(8,128)(2,1)}), bf16[2048,512]{1,0:T(8,128)(2,1)}) %all-gather.4.cloned.1.call-update) | async-done | bytes 2097168 | tf_op jit(solution)/shard_map/all_gather | solution.py:29
  34.2 2.2 fusion.21
  36.5 2.7 convolution_bitcast_fusion
  39.2 0.0 all-reduce.4.cloned.1.call-start
  39.9 44.0 %reduce-scatter.2.cloned.1.call-done = f32[512,512]{0,1:T(8,128)} async-done(((f32[2048,512]{0,1:T(8,128)}), f32[512,512]{0,1:T(8,128)}) %reduce-scatter.2.cloned.1.call-update) | async-done | bytes 1048592 | tf_op jit(solution)/shard_map/reduce_scatter | solution.py:38
  83.9 1.6 copy.20
  85.4 1.7 broadcast_multiply_fusion.1
  87.2 0.7 fusion.18
  87.9 102.0 %all-reduce.4.cloned.1.call-done = f32[2,512,512]{2,1,0:T(8,128)} async-done(((f32[2,512,512]{2,1,0:T(8,128)}), f32[2,512,512]{2,1,0:T(8,128)}) %all-reduce.4.cloned.1.call-update) | async-done | bytes 2097168 | tf_op jit(solution)/shard_map/psum | solution.py:46
  189.8 2.1 multiply_reduce_fusion.1
  191.9 1.7 subtract_convert_fusion
  193.6 1.0 copy.22
  194.6 3.5 all-to-all-start
  198.1 12.7 %all-to-all-done = bf16[128,4,512]{0,2,1:T(8,128)(2,1)S(1)} async-done(((bf16[128,4,512]{0,2,1:T(8,128)(2,1)}), bf16[128,4,512]{0,2,1:T(8,128)(2,1)S(1)}, u32[]{:S(2)}, u32[]{:S(2)}) %all-to-all-start) | async-done | bytes 524320 | tf_op jit(solution)/shard_map/all_to_all | solution.py:30
  210.8 0.2 copy.23
  211.0 8.6 %all-gather.6.cloned.1.call-done = bf16[2048,512]{1,0:T(8,128)(2,1)} async-done(((bf16[512,512]{1,0:T(8,128)(2,1)}), bf16[2048,512]{1,0:T(8,128)(2,1)}) %all-gather.6.cloned.1.call-update) | async-done | bytes 2097168 | tf_op jit(solution)/shard_map/all_gather | solution.py:49
  219.7 2.1 fusion.10
  221.8 7.2 %all_gather.17 = bf16[512,512]{1,0:T(8,128)(2,1)S(1)} all-gather(bf16[128,512]{1,0:T(8,128)(2,1)S(1)} %fusion.10), channel_id=1, replica_groups=mesh['dp'=8,'fsdp'=4] {'fsdp'}, dimensions={0}, use_global_device_ids=true | all-gather | bytes 655360 | tf_op jit(solution)/shard_map/all_gather | solution.py:53
  229.0 0.5 convolution_bitcast_fusion.1
  229.4 0.3 copy.24
  229.8 1.7 broadcast_multiply_fusion
  231.5 100.8 %all-reduce.6.cloned.1.call-done = f32[2,512,512]{2,1,0:T(8,128)} async-done(((f32[2,512,512]{2,1,0:T(8,128)}), f32[2,512,512]{2,1,0:T(8,128)}) %all-reduce.6.cloned.1.call-update) | async-done | bytes 2097168 | tf_op jit(solution)/shard_map/psum | solution.py:54
  332.3 3.1 multiply_reduce_fusion
  335.5 22.4 %all-gather.8.cloned.1.call-done = bf16[2048,512]{1,0:T(8,128)(2,1)} async-done(((bf16[512,512]{1,0:T(8,128)(2,1)}), bf16[2048,512]{1,0:T(8,128)(2,1)}) %all-gather.8.cloned.1.call-update) | async-done | bytes 2097168 | tf_op jit(solution)/shard_map/all_gather | solution.py:56
  357.9 2.1 fusion.3
  360.0 7.2 %all_gather.19 = bf16[512,512]{1,0:T(8,128)(2,1)S(1)} all-gather(bf16[128,512]{1,0:T(8,128)(2,1)S(1)} %fusion.3), channel_id=1, replica_groups=mesh['dp'=8,'fsdp'=4] {'fsdp'}, dimensions={0}, use_global_device_ids=true | all-gather | bytes 655360 | tf_op jit(solution)/shard_map/all_gather | solution.py:60
  367.2 2.1 fusion
  369.3 0.3 copy.26
  369.7 78.0 %all-reduce.8.cloned.1.call-done = f32[512,512]{0,1:T(8,128)} async-done(((f32[512,512]{0,1:T(8,128)}), f32[512,512]{0,1:T(8,128)}) %all-reduce.8.cloned.1.call-update) | async-done | bytes 1048592 | tf_op jit(solution)/shard_map/psum | solution.py:61
  447.7 1.4 subtract_multiply_fusion
  449.1 1.3 copy.27
  (21 shorter events, 0.3 us)
Async XLA Ops:
  6.5 29.9 %copy-start = (bf16[128,2048]{1,0:T(8,128)(2,1)S(1)}, bf16[128,2048]{1,0:T(8,128)(2,1)}, u32[]{:S(2)}) copy-start(bf16[128,2048]{1,0:T(8,128)(2,1)} %param.6) | copy-start | bytes 1572868
  6.5 29.9 %copy-start.2 = (bf16[128,512]{1,0:T(8,128)(2,1)S(1)}, bf16[128,512]{1,0:T(8,128)(2,1)}, u32[]{:S(2)}) copy-start(bf16[128,512]{1,0:T(8,128)(2,1)} %param.7) | copy-start | bytes 393220
  6.5 27.7 %all-gather.4.cloned.1.call-start = ((), (), s32[]{:S(2)}) async-start(), calls=%async_computation.2 | async-start | bytes 2621440 | tf_op jit(solution)/shard_map/all_gather | solution.py:29
  7.3 76.6 %reduce-scatter.2.cloned.1.call-start = ((), (), s32[]{:S(2)}) async-start(), calls=%async_computation.3 | async-start | bytes 5242880 | tf_op jit(solution)/shard_map/reduce_scatter | solution.py:38
  39.2 150.6 %all-reduce.4.cloned.1.call-start = ((), (), s32[]{:S(2)}) async-start(), calls=%async_computation.4 | async-start | bytes 4194304 | tf_op jit(solution)/shard_map/psum | solution.py:46
  85.4 1.8 copy-start.3
  87.1 104.8 %copy-start.1 = (bf16[512,512]{1,0:T(8,128)(2,1)S(1)}, bf16[512,512]{1,0:T(8,128)(2,1)}, u32[]{:S(2)}) copy-start(bf16[512,512]{1,0:T(8,128)(2,1)} %param.8) | copy-start | bytes 1572868
  87.1 132.5 %all-gather.6.cloned.1.call-start = ((), (), s32[]{:S(2)}) async-start(), calls=%async_computation.5 | async-start | bytes 2621440 | tf_op jit(solution)/shard_map/all_gather | solution.py:49
  194.6 16.2 %all-to-all-start = ((bf16[128,4,512]{0,2,1:T(8,128)(2,1)}), bf16[128,4,512]{0,2,1:T(8,128)(2,1)S(1)}, u32[]{:S(2)}, u32[]{:S(2)}) async-start(bf16[128,4,512]{0,2,1:T(8,128)(2,1)} %bitcast.4), calls=%async_computation.1 | async-start | bytes 1048576 | tf_op jit(solution)/shard_map/all_to_all | solution.py:30
  198.1 134.2 %all-reduce.6.cloned.1.call-start = ((), (), s32[]{:S(2)}) async-start(), calls=%async_computation.6 | async-start | bytes 4194304 | tf_op jit(solution)/shard_map/psum | solution.py:54
  231.4 126.5 %all-gather.8.cloned.1.call-start = ((), (), s32[]{:S(2)}) async-start(), calls=%async_computation.7 | async-start | bytes 2621440 | tf_op jit(solution)/shard_map/all_gather | solution.py:56
  335.5 112.2 %all-reduce.8.cloned.1.call-start = ((), (), s32[]{:S(2)}) async-start(), calls=%async_computation.8 | async-start | bytes 2097152 | tf_op jit(solution)/shard_map/psum | solution.py:61
Sparse Core Ops, SparseCore 0:
  8.9 25.2 all-gather.3
  39.3 44.4 reduce-scatter.1
  87.9 101.8 all-reduce.3
  193.7 25.8 all-gather.5
  231.6 100.7 all-reduce.5
  335.6 22.3 all-gather.7
  369.4 78.1 all-reduce.7
where the time goes:
time: 458 us; the launch traced here: 457 us
  waiting for transfers between devices  396 us (86%)
  between operations  14.9 us (3%)
  blocking collectives  14.4 us (3%)
  other arithmetic  12.3 us (3%)
  matrix products  11.7 us (3%)
  local copies, waits for them, and re-layouts  4.76 us (1%)
    psum x1, waiting for transfers between devices, local(): stacked = lax.psum(onehot[:, None, None] * grad_local[None], 'dp')  102 us
    psum x1, waiting for transfers between devices, local(): outer_all = lax.psum(onehot[:, None, None] * outer_local[None], 'dp')  101 us
    psum x1, waiting for transfers between devices, local(): curv_sum = lax.psum(own_rate * curv_local, 'dp')  78 us
    reduce_scatter x1, waiting for transfers between devices, local(): lax.psum_scatter(lax.dot_general(tokens, delta_adv, (((0,), (0,)), ((), (...  44 us
    all_gather x1, waiting for transfers between devices, local(): primal = project(lax.all_gather(value_weight, 'fsdp', axis=0, tiled=True))  26.3 us
    all_gather x1, waiting for transfers between devices, local(): lax.all_gather(tangent, 'fsdp', axis=0, tiled=True)  22.4 us
    all_to_all x1, waiting for transfers between devices, local(): lax.all_to_all(tokens, 'fsdp', split_axis=1, concat_axis=0, tiled=True)  12.7 us
  transfers between devices with their start and end apart: 8, of which 8 were waited for; matrix products, arithmetic and copies ran while one was open for 0% of the time, Pallas kernels for 0%

commit v1 on v0

v1 whole, which is shorter than its diff:
```python
import jax
import jax.numpy as jnp
from jax import lax
from jax.sharding import PartitionSpec as P

BF = jnp.bfloat16
F32 = jnp.float32


def first_slope(value):
    sig = jax.nn.sigmoid(value)
    return sig * (1.0 + value * (1.0 - sig))


def second_slope(value):
    sig = jax.nn.sigmoid(value)
    return sig * (1.0 - sig) * (2.0 + value * (1.0 - 2.0 * sig))


def swap(value, axis, bit):
    return lax.ppermute(value, axis, [(i, i ^ bit) for i in range(lax.axis_size(axis))])


def bits_of(size):
    found = []
    bit = 1
    while bit < size:
        found.append(bit)
        bit *= 2
    return found


def pick(value, axis, index, size):
    return lax.dynamic_slice_in_dim(value, index * size, size, axis)


def in_order(mine, other, upper, axis):
    return jnp.where(
        upper == 1,
        jnp.concatenate([other, mine], axis),
        jnp.concatenate([mine, other], axis),
    )


def over_tokens(left, tokens):
    return lax.dot_general(left, tokens, (((1,), (1,)), ((), ())), preferred_element_type=F32)


def over_rows(left, tokens):
    return jnp.dot(left, tokens, preferred_element_type=F32)


def local(tokens, upstream, value_weight, forget_label, copy_index, adv_rate):
    dp, fsdp = lax.axis_size("dp"), lax.axis_size("fsdp")
    rows, features = tokens.shape
    outs = upstream.shape[1]
    wide = outs // dp
    part = features // fsdp
    copies = adv_rate.shape[0]
    seq_length = rows * fsdp
    me = lax.axis_index("dp")
    quarter = lax.axis_index("fsdp")
    core = quarter % 2
    dp_bits = bits_of(dp)[::-1]
    far_bits = bits_of(fsdp)[1:]

    blocks = {0: tokens}
    for r in range(1, dp):
        bit = r & -r
        blocks[r] = swap(blocks[r ^ bit], "dp", bit)

    weight = pick(value_weight, 1, me, wide).T
    for bit in bits_of(fsdp):
        weight = in_order(weight, swap(weight, "fsdp", bit), (quarter // bit) % 2, 1)

    up = upstream.T
    labels = jnp.stack([forget_label[0], copy_index[0]] + [jnp.int32(0)] * 14).astype(BF)
    labels = jnp.broadcast_to(labels[:, None], (16, rows))
    order = [0]
    for bit in dp_bits:
        half = up.shape[0] // 2
        side = (me // bit) % 2
        sent = jnp.concatenate([pick(up, 0, 1 - side, half), labels])
        came = swap(sent, "dp", bit)
        up = jnp.concatenate([pick(up, 0, side, half), came[:half]], 1)
        labels = jnp.concatenate([labels, came[half:]], 1)
        order = order + [r ^ bit for r in order]
    up = up.astype(F32)
    forget = labels[0:1].astype(F32)
    copy = labels[1:2].astype(F32)
    held = jnp.concatenate([blocks[r] for r in order])

    onehot = [(copy == float(c)).astype(F32) for c in range(copies)]
    own_rate = sum(onehot[c] * adv_rate[c] for c in range(copies))

    def by_copy(value):
        return jnp.concatenate([(value * onehot[c]) for c in range(copies)]).astype(BF)

    def of_copy(value):
        value = value.reshape(copies, wide, -1)
        return sum(value[c] * onehot[c] for c in range(copies))

    def core_half(value, side):
        m = value.shape[0]
        value = value.reshape(m, fsdp // 2, 2, part)
        return lax.dynamic_index_in_dim(value, side, 2, False).reshape(m, features // 2)

    def both_halves(mine, other):
        m = mine.shape[0]
        mine = mine.reshape(m, fsdp // 2, 1, part)
        other = other.reshape(m, fsdp // 2, 1, part)
        return in_order(mine, other, core, 2).reshape(m, features)

    def total(value):
        came = swap(core_half(value, 1 - core).astype(BF), "fsdp", 1)
        value = core_half(value, core) + came.astype(F32)
        for bit in far_bits:
            value = value + swap(value.astype(BF), "fsdp", bit).astype(F32)
        return value

    primal = over_tokens(weight, held)
    delta_adv = (forget * up * first_slope(primal) / seq_length).astype(BF)
    grad = total(over_rows(by_copy(delta_adv.astype(F32)), held))
    rates = jnp.repeat(adv_rate, wide)[:, None]
    half_weight = jnp.concatenate([core_half(weight, core)] * copies).astype(F32)
    attacked = (half_weight - rates * grad).astype(BF)
    attacked = both_halves(attacked, swap(attacked, "fsdp", 1))
    altered = of_copy(over_tokens(attacked, held))
    delta_out = ((1.0 - 2.0 * forget) * up * first_slope(altered) / seq_length).astype(BF)
    outer = total(over_rows(by_copy(delta_out.astype(F32)), held))
    tangent = outer.astype(BF)
    tangent = both_halves(tangent, swap(tangent, "fsdp", 1))
    forward_tangent = of_copy(over_tokens(tangent, held))
    delta_curv = (forget * up * second_slope(primal) * forward_tangent / seq_length).astype(BF)
    curv = over_rows((own_rate * delta_curv.astype(F32)).astype(BF), held)

    came = swap(core_half(curv, 1 - core).astype(BF), "fsdp", 1)
    curv = core_half(curv, core) + came.astype(F32)
    for bit in far_bits[::-1]:
        half = curv.shape[1] // 2
        side = (quarter // bit) % 2
        came = swap(pick(curv, 1, 1 - side, half).astype(BF), "fsdp", bit)
        curv = pick(curv, 1, side, half) + came.astype(F32)
    outer = outer.reshape(copies, wide, features // 2).sum(0)
    outer = pick(outer, 1, quarter // 2, part)
    scale = (float(seq_length) / float(dp)) ** 0.5
    result = (scale * (outer - curv)).astype(BF)
    for bit in dp_bits:
        result = jnp.stack([result, swap(result, "dp", bit)])
        result = result.reshape(-1, part)
    result = result.reshape([2] * len(dp_bits) + [wide, part])
    for place, bit in enumerate(dp_bits[::-1]):
        side = (me // bit) % 2
        result = jnp.where(side == 1, jnp.flip(result, place), result)
    axes = tuple(range(len(dp_bits)))
    result = result.transpose(axes[::-1] + (len(axes), len(axes) + 1))
    return result.reshape(outs, part).T.astype(F32)


def solution(mesh):
    in_specs = (
        P(("dp", "fsdp"), None),
        P(("dp", "fsdp"), None),
        P("fsdp", None),
        P("dp"),
        P("dp"),
        P(),
    )
    out_specs = P("fsdp", None)
    return jax.shard_map(local, mesh=mesh, in_specs=in_specs, out_specs=out_specs, check_vma=False)
```

time: 458 us -> 146 us (0.32)
  waiting for transfers between devices: 396 us -> 78.3 us
  starting transfers between devices: 3.72 us -> 26.4 us
  local copies, waits for them, and re-layouts: 4.76 us -> 21.8 us
  blocking collectives: 14.4 us -> 0 us
  between operations: 14.9 us -> 1.93 us
  other arithmetic: 12.3 us -> 3.63 us
    psum x3 -> x0, waiting for transfers between devices: 281 us -> none  [the longest x1 102 us: local(): stacked = lax.psum(onehot[:, None, None] * grad_local[None], 'dp')]
    ppermute x0 -> x23, waiting for transfers between devices: none -> 78.3 us  [swap(): lax.ppermute(value, axis, [(i, i ^ bit) for i in range(lax.axis_size(axis...]
    all_gather x3 -> x0, waiting for transfers between devices: 57.3 us -> none  [the longest x1 26.3 us: local(): primal = project(lax.all_gather(value_weight, 'fsdp', axis=0, tiled=True))]
    reduce_scatter x1 -> x0, waiting for transfers between devices: 44 us -> none  [local(): lax.psum_scatter(lax.dot_general(tokens, delta_adv, (((0,), (0,)), ((), (...]
    ppermute x0 -> x23, starting transfers between devices: none -> 26.4 us  [swap(): lax.ppermute(value, axis, [(i, i ^ bit) for i in range(lax.axis_size(axis...]
    all_gather x2 -> x0, blocking collectives: 14.4 us -> none  [the longest x1 7.18 us: local(): lax.all_gather(delta_out, 'fsdp', axis=0, tiled=True)]
    all_to_all x1 -> x0, waiting for transfers between devices: 12.7 us -> none  [local(): lax.all_to_all(tokens, 'fsdp', split_axis=1, concat_axis=0, tiled=True)]
    unnamed x9 -> x28, local copies, waits for them, and re-layouts: 1.02 us -> 8.61 us
  transfers between devices with their start and end apart: 8 -> 23, of which waited for: 8 -> 17; matrix products, arithmetic and copies ran while one was open for 0% -> 12% of each run, Pallas kernels for 0% -> 0%
where the time goes in v1:
time: 146 us
  waiting for transfers between devices  78.3 us (54%)
  starting transfers between devices  26.4 us (18%)
  local copies, waits for them, and re-layouts  21.8 us (15%)
  matrix products  13.8 us (9%)
  other arithmetic  3.63 us (2%)
  between operations  1.93 us (1%)
    ppermute x23, waiting for transfers between devices, swap(): lax.ppermute(value, axis, [(i, i ^ bit) for i in range(lax.axis_size(axis...  78.3 us
    ppermute x23, starting transfers between devices, swap(): lax.ppermute(value, axis, [(i, i ^ bit) for i in range(lax.axis_size(axis...  26.4 us
    dot_general x3, matrix products, over_tokens(): lax.dot_general(left, tokens, (((1,), (1,)), ((), ())), preferred_element...  11.4 us
    unnamed x28, local copies, waits for them, and re-layouts  8.61 us
    dynamic_slice x7, local copies, waits for them, and re-layouts, core_half(): lax.dynamic_index_in_dim(value, side, 2, False).reshape(m, features // 2)  4.87 us
  transfers between devices with their start and end apart: 23, of which 17 were waited for; matrix products, arithmetic and copies ran while one was open for 12% of the time, Pallas kernels for 0%

profile of v1, /device:TPU:0, one launch (start us, length us, event | category | flops | bytes accessed | tf_op | source)
XLA Modules:
  0.0 145.8 jit_solution(5285850300487015313)
XLA Ops:
  0.0 4.0 %collective-permute-start.5 = (bf16[128,2048]{1,0:T(8,128)(2,1)}, bf16[128,2048]{1,0:T(8,128)(2,1)S(1)}, u32[]{:S(2)}, u32[]{:S(2)}) collective-permute-start(bf16[128,2048]{1,0:T(8,128)(2,1)} %param.6), channel_id=1, source_target_pairs={{0,16},{4,20},{8,24},{12,28},{16,0},{20,4},{24,8},{28,12},{1,17},{... | collective-permute-start | bytes 1572872 | tf_op jit(solution)/shard_map/ppermute | solution.py:21
  4.0 1.6 %collective-permute-start.6 = (bf16[128,2048]{1,0:T(8,128)(2,1)}, bf16[128,2048]{1,0:T(8,128)(2,1)S(1)}, u32[]{:S(2)}, u32[]{:S(2)}) collective-permute-start(bf16[128,2048]{1,0:T(8,128)(2,1)} %param.6), channel_id=1, source_target_pairs={{0,8},{4,12},{8,0},{12,4},{16,24},{20,28},{24,16},{28,20},{1,9},{5... | collective-permute-start | bytes 1572872 | tf_op jit(solution)/shard_map/ppermute | solution.py:21
  5.6 1.5 %collective-permute-start.8 = (bf16[128,2048]{1,0:T(8,128)(2,1)}, bf16[128,2048]{1,0:T(8,128)(2,1)S(1)}, u32[]{:S(2)}, u32[]{:S(2)}) collective-permute-start(bf16[128,2048]{1,0:T(8,128)(2,1)} %param.6), channel_id=1, source_target_pairs={{0,4},{4,0},{8,12},{12,8},{16,20},{20,16},{24,28},{28,24},{1,5},{5... | collective-permute-start | bytes 1572872 | tf_op jit(solution)/shard_map/ppermute | solution.py:21
  10.3 1.9 %constant_dynamic-update-slice_fusion.7 = bf16[1024,2048]{1,0:T(8,128)(2,1)} fusion(bf16[128,2048]{1,0:T(8,128)(2,1)} %param.6), kind=kLoop, calls=%fused_computation.109 | loop fusion | bytes 1048576
  12.3 18.1 %collective-permute-done = bf16[272,128]{1,0:T(8,128)(2,1)S(1)} collective-permute-done((bf16[272,128]{1,0:T(8,128)(2,1)S(1)}, bf16[272,128]{1,0:T(8,128)(2,1)S(1)}, u32[]{:S(2)}, u32[]{:S(2)}) %collective-permute-start) | collective-permute-done | bytes 69664 | tf_op jit(solution)/shard_map/ppermute | solution.py:21
  32.5 2.4 %collective-permute-done.1 = bf16[144,256]{1,0:T(8,128)(2,1)S(1)} collective-permute-done((bf16[144,256]{1,0:T(8,128)(2,1)S(1)}, bf16[144,256]{1,0:T(8,128)(2,1)S(1)}, u32[]{:S(2)}, u32[]{:S(2)}) %collective-permute-start.1) | collective-permute-done | bytes 73760 | tf_op jit(solution)/shard_map/ppermute | solution.py:21
  35.0 1.6 %collective-permute-start.2 = (bf16[80,512]{1,0:T(8,128)(2,1)S(1)}, bf16[80,512]{1,0:T(8,128)(2,1)S(1)}, u32[]{:S(2)}, u32[]{:S(2)}) collective-permute-start(bf16[80,512]{1,0:T(8,128)(2,1)S(1)} %maximum_maximum_fusion), channel_id=1, source_target_pairs={{0,4},{4,0},{8,12},{12,8},{16,20},{20,16},{24,28},{28,24},{1,5},{5... | collective-permute-start | bytes 245768 | tf_op jit(solution)/shard_map/ppermute | solution.py:21
  36.7 1.6 %collective-permute-start.4 = (bf16[64,1024]{0,1:T(8,128)(2,1)S(1)}, bf16[64,1024]{0,1:T(8,128)(2,1)S(1)}, u32[]{:S(2)}, u32[]{:S(2)}) collective-permute-start(bf16[64,1024]{0,1:T(8,128)(2,1)S(1)} %maximum_select_fusion.4), channel_id=1, source_target_pairs={{0,2},{1,3},{2,0},{3,1},{4,6},{5,7},{6,4},{7,5},{8,10},{9,11},{10,... | collective-permute-start | bytes 393224 | tf_op jit(solution)/shard_map/ppermute | solution.py:21
  39.5 1.7 %multiply_subtract_fusion = (f32[1,1024]{1,0:T(1,128)S(1)}, f32[1,1024]{1,0:T(1,128)S(1)}, f32[1,1024]{1,0:T(1,128)}, f32[1,1024]{1,0:T(1,128)S(1)}) fusion(bf16[16,512]{1,0:T(8,128)(2,1)S(1)} %slice.64, bf16[16,256]{1,0:T(8,128)(2,1)S(1)} %slice.62, bf16[16,128]{1,0:T(8,128)(2,1)S(1)} %slice.60, bf16[16,128]{1,0:T(8,128)(2,1)S(1)} %broadcast_in_dim.4, ...), kind=kLoop, calls=%fused_computation.126 | loop fusion | flops 23552 | bytes 49160 | tf_op jit(solution)/shard_map/sub | solution.py:129
  41.9 1.6 %collective-permute-start.9 = (bf16[128,2048]{1,0:T(8,128)(2,1)S(1)}, bf16[128,2048]{1,0:T(8,128)(2,1)S(1)}, u32[]{:S(2)}, u32[]{:S(2)}) collective-permute-start(bf16[128,2048]{1,0:T(8,128)(2,1)S(1)} %collective-permute-done.5), channel_id=1, source_target_pairs={{0,4},{4,0},{8,12},{12,8},{16,20},{20,16},{24,28},{28,24},{1,5},{5... | collective-permute-start | bytes 1572872 | tf_op jit(solution)/shard_map/ppermute | solution.py:21
  45.7 6.0 %collective-permute-done.7 = bf16[128,2048]{1,0:T(8,128)(2,1)S(1)} collective-permute-done((bf16[128,2048]{1,0:T(8,128)(2,1)S(1)}, bf16[128,2048]{1,0:T(8,128)(2,1)S(1)}, u32[]{:S(2)}, u32[]{:S(2)}) %collective-permute-start.7) | collective-permute-done | bytes 524320 | tf_op jit(solution)/shard_map/ppermute | solution.py:21
  51.7 1.5 %collective-permute-start.11 = (bf16[128,2048]{1,0:T(8,128)(2,1)S(1)}, bf16[128,2048]{1,0:T(8,128)(2,1)S(1)}, u32[]{:S(2)}, u32[]{:S(2)}) collective-permute-start(bf16[128,2048]{1,0:T(8,128)(2,1)S(1)} %collective-permute-done.7), channel_id=1, source_target_pairs={{0,4},{4,0},{8,12},{12,8},{16,20},{20,16},{24,28},{28,24},{1,5},{5... | collective-permute-start | bytes 1572872 | tf_op jit(solution)/shard_map/ppermute | solution.py:21
  54.9 1.9 %collective-permute-done.9 = bf16[128,2048]{1,0:T(8,128)(2,1)S(1)} collective-permute-done((bf16[128,2048]{1,0:T(8,128)(2,1)S(1)}, bf16[128,2048]{1,0:T(8,128)(2,1)S(1)}, u32[]{:S(2)}, u32[]{:S(2)}) %collective-permute-start.9) | collective-permute-done | bytes 524320 | tf_op jit(solution)/shard_map/ppermute | solution.py:21
  57.6 10.4 %collective-permute-done.10 = bf16[128,2048]{1,0:T(8,128)(2,1)S(1)} collective-permute-done((bf16[128,2048]{1,0:T(8,128)(2,1)S(1)}, bf16[128,2048]{1,0:T(8,128)(2,1)S(1)}, u32[]{:S(2)}, u32[]{:S(2)}) %collective-permute-start.10) | collective-permute-done | bytes 524320 | tf_op jit(solution)/shard_map/ppermute | solution.py:21
  68.9 6.8 %collective-permute-done.11 = bf16[128,2048]{1,0:T(8,128)(2,1)S(1)} collective-permute-done((bf16[128,2048]{1,0:T(8,128)(2,1)S(1)}, bf16[128,2048]{1,0:T(8,128)(2,1)S(1)}, u32[]{:S(2)}, u32[]{:S(2)}) %collective-permute-start.11) | collective-permute-done | bytes 524320 | tf_op jit(solution)/shard_map/ppermute | solution.py:21
  76.5 3.8 %fusion.19 = (bf16[64,1024]{1,0:T(8,128)(2,1)S(1)}, bf16[64,1024]{1,0:T(8,128)(2,1)S(1)}, f32[64,1024]{1,0:T(8,128)S(1)}) fusion(f32[1024]{0:T(1024)S(1)} %bitcast.99, bf16[64,512]{1,0:T(8,128)(2,1)S(1)} %slice.65, bf16[64,512]{1,0:T(8,128)(2,1)S(1)} %get-tuple-element.17, f32[1024]{0:T(1024)S(1)} %bitcast.103, ...), kind=kOutput, calls=%fused_computation.40 | convolution fusion | flops 270794752 | bytes 5120001 | tf_op jit(solution)/shard_map/dot_general | solution.py:46
  83.4 1.8 %dynamic-slice_reduce_fusion = f32[128,2,512]{2,1,0:T(2,128)S(1)} fusion(f32[128,2,2,512]{3,2,1,0:T(2,128)S(1)} %reshape.137, s32[]{:T(128)S(6)} %select_n.187), kind=kLoop, calls=%fused_computation.18 | loop fusion | bytes 1048580 | tf_op jit(solution)/shard_map/jit(dynamic_index_in_dim)/dynamic_slice | solution.py:106
  85.3 1.6 %collective-permute-start.13 = (bf16[128,1024]{1,0:T(8,128)(2,1)S(1)}, bf16[128,1024]{1,0:T(8,128)(2,1)S(1)}, u32[]{:S(2)}, u32[]{:S(2)}) collective-permute-start(bf16[128,1024]{1,0:T(8,128)(2,1)S(1)} %fusion.7), channel_id=1, source_target_pairs={{0,2},{1,3},{2,0},{3,1},{4,6},{5,7},{6,4},{7,5},{8,10},{9,11},{10,... | collective-permute-start | bytes 786440 | tf_op jit(solution)/shard_map/ppermute | solution.py:21
  88.2 5.9 %collective-permute-done.13 = bf16[128,1024]{1,0:T(8,128)(2,1)S(1)} collective-permute-done((bf16[128,1024]{1,0:T(8,128)(2,1)S(1)}, bf16[128,1024]{1,0:T(8,128)(2,1)S(1)}, u32[]{:S(2)}, u32[]{:S(2)}) %collective-permute-start.13) | collective-permute-done | bytes 262176 | tf_op jit(solution)/shard_map/ppermute | solution.py:21
  94.5 1.3 collective-permute-done.14
  96.1 3.9 %fusion.65 = f32[128,1024]{1,0:T(8,128)S(1)} fusion(bf16[128,2048]{0,1:T(8,128)(2,1)S(1)} %bitcast.68, bf16[1024,2048]{1,0:T(8,128)(2,1)} %constant_dynamic-update-slice_fusion), kind=kOutput, calls=%fused_computation.137 | convolution fusion | flops 536870912 | bytes 5242880 | tf_op jit(solution)/shard_map/dot_general | solution.py:46
  104.4 1.6 %collective-permute-start.16 = (bf16[128,1024]{0,1:T(8,128)(2,1)S(1)}, bf16[128,1024]{0,1:T(8,128)(2,1)S(1)}, u32[]{:S(2)}, u32[]{:S(2)}) collective-permute-start(bf16[128,1024]{0,1:T(8,128)(2,1)S(1)} %fusion.8), channel_id=1, source_target_pairs={{0,2},{1,3},{2,0},{3,1},{4,6},{5,7},{6,4},{7,5},{8,10},{9,11},{10,... | collective-permute-start | bytes 786440 | tf_op jit(solution)/shard_map/ppermute | solution.py:21
  106.0 6.9 %collective-permute-done.16 = bf16[128,1024]{0,1:T(8,128)(2,1)S(1)} collective-permute-done((bf16[128,1024]{0,1:T(8,128)(2,1)S(1)}, bf16[128,1024]{0,1:T(8,128)(2,1)S(1)}, u32[]{:S(2)}, u32[]{:S(2)}) %collective-permute-start.16) | collective-permute-done | bytes 262176 | tf_op jit(solution)/shard_map/ppermute | solution.py:21
  113.0 1.5 %collective-permute-done.17 = bf16[128,1024]{0,1:T(8,128)(2,1)S(1)} collective-permute-done((bf16[128,1024]{0,1:T(8,128)(2,1)S(1)}, bf16[128,1024]{0,1:T(8,128)(2,1)S(1)}, u32[]{:S(2)}, u32[]{:S(2)}) %collective-permute-start.17) | collective-permute-done | bytes 262176 | tf_op jit(solution)/shard_map/ppermute | solution.py:21
  114.6 3.7 %fusion.66 = f32[128,1024]{1,0:T(8,128)S(1)} fusion(bf16[128,2048]{0,1:T(8,128)(2,1)S(1)} %bitcast.67, bf16[1024,2048]{1,0:T(8,128)(2,1)} %constant_dynamic-update-slice_fusion), kind=kOutput, calls=%fused_computation.138 | convolution fusion | flops 536870912 | bytes 5242880 | tf_op jit(solution)/shard_map/dot_general | solution.py:46
  121.7 1.6 %collective-permute-start.19 = (bf16[64,512]{1,0:T(8,128)(2,1)S(1)}, bf16[64,512]{1,0:T(8,128)(2,1)S(1)}, u32[]{:S(2)}, u32[]{:S(2)}) collective-permute-start(bf16[64,512]{1,0:T(8,128)(2,1)S(1)} %dynamic-slice_convert_fusion), channel_id=1, source_target_pairs={{0,2},{1,3},{2,0},{3,1},{4,6},{5,7},{6,4},{7,5},{8,10},{9,11},{10,... | collective-permute-start | bytes 196616 | tf_op jit(solution)/shard_map/ppermute | solution.py:21
  123.5 2.5 %collective-permute-done.19 = bf16[64,512]{1,0:T(8,128)(2,1)S(1)} collective-permute-done((bf16[64,512]{1,0:T(8,128)(2,1)S(1)}, bf16[64,512]{1,0:T(8,128)(2,1)S(1)}, u32[]{:S(2)}, u32[]{:S(2)}) %collective-permute-start.19) | collective-permute-done | bytes 65568 | tf_op jit(solution)/shard_map/ppermute | solution.py:21
  126.0 3.4 %collective-permute-start.20 = (bf16[64,512]{1,0:T(8,128)(2,1)S(1)}, bf16[64,512]{1,0:T(8,128)(2,1)S(1)}, u32[]{:S(2)}, u32[]{:S(2)}) collective-permute-start(bf16[64,512]{1,0:T(8,128)(2,1)S(1)} %multiply_convert_fusion.2), channel_id=1, source_target_pairs={{0,16},{4,20},{8,24},{12,28},{16,0},{20,4},{24,8},{28,12},{1,17},{... | collective-permute-start | bytes 196616 | tf_op jit(solution)/shard_map/ppermute | solution.py:21
  129.5 2.9 %collective-permute-done.20 = bf16[64,512]{1,0:T(8,128)(2,1)S(1)} collective-permute-done((bf16[64,512]{1,0:T(8,128)(2,1)S(1)}, bf16[64,512]{1,0:T(8,128)(2,1)S(1)}, u32[]{:S(2)}, u32[]{:S(2)}) %collective-permute-start.20) | collective-permute-done | bytes 65568 | tf_op jit(solution)/shard_map/ppermute | solution.py:21
  132.7 4.8 %collective-permute-done.21 = bf16[128,512]{1,0:T(8,128)(2,1)S(1)} collective-permute-done((bf16[128,512]{1,0:T(8,128)(2,1)S(1)}, bf16[128,512]{1,0:T(8,128)(2,1)S(1)}, u32[]{:S(2)}, u32[]{:S(2)}) %collective-permute-start.21) | collective-permute-done | bytes 131104 | tf_op jit(solution)/shard_map/ppermute | solution.py:21
  137.5 1.6 %collective-permute-start.22 = (bf16[256,512]{1,0:T(8,128)(2,1)S(1)}, bf16[256,512]{1,0:T(8,128)(2,1)S(1)}, u32[]{:S(2)}, u32[]{:S(2)}) collective-permute-start(bf16[256,512]{1,0:T(8,128)(2,1)S(1)} %bitcast.87), channel_id=1, source_target_pairs={{0,4},{4,0},{8,12},{12,8},{16,20},{20,16},{24,28},{28,24},{1,5},{5... | collective-permute-start | bytes 786440 | tf_op jit(solution)/shard_map/ppermute | solution.py:21
  139.1 4.8 %collective-permute-done.22 = bf16[256,512]{1,0:T(8,128)(2,1)S(1)} collective-permute-done((bf16[256,512]{1,0:T(8,128)(2,1)S(1)}, bf16[256,512]{1,0:T(8,128)(2,1)S(1)}, u32[]{:S(2)}, u32[]{:S(2)}) %collective-permute-start.22) | collective-permute-done | bytes 262176 | tf_op jit(solution)/shard_map/ppermute | solution.py:21
  (111 shorter events, 27.5 us)
Async XLA Ops:
  0.0 10.1 %copy-start = (bf16[512,512]{1,0:T(8,128)(2,1)S(1)}, bf16[512,512]{1,0:T(8,128)(2,1)}, u32[]{:S(2)}) copy-start(bf16[512,512]{1,0:T(8,128)(2,1)} %param.8) | copy-start | bytes 1572868
  0.0 41.2 %collective-permute-start.5 = (bf16[128,2048]{1,0:T(8,128)(2,1)}, bf16[128,2048]{1,0:T(8,128)(2,1)S(1)}, u32[]{:S(2)}, u32[]{:S(2)}) collective-permute-start(bf16[128,2048]{1,0:T(8,128)(2,1)} %param.6), channel_id=1, source_target_pairs={{0,16},{4,20},{8,24},{12,28},{16,0},{20,4},{24,8},{28,12},{1,17},{... | collective-permute-start | bytes 1572872 | tf_op jit(solution)/shard_map/ppermute | solution.py:21
  4.0 40.3 %collective-permute-start.6 = (bf16[128,2048]{1,0:T(8,128)(2,1)}, bf16[128,2048]{1,0:T(8,128)(2,1)S(1)}, u32[]{:S(2)}, u32[]{:S(2)}) collective-permute-start(bf16[128,2048]{1,0:T(8,128)(2,1)} %param.6), channel_id=1, source_target_pairs={{0,8},{4,12},{8,0},{12,4},{16,24},{20,28},{24,16},{28,20},{1,9},{5... | collective-permute-start | bytes 1572872 | tf_op jit(solution)/shard_map/ppermute | solution.py:21
  5.6 48.4 %collective-permute-start.8 = (bf16[128,2048]{1,0:T(8,128)(2,1)}, bf16[128,2048]{1,0:T(8,128)(2,1)S(1)}, u32[]{:S(2)}, u32[]{:S(2)}) collective-permute-start(bf16[128,2048]{1,0:T(8,128)(2,1)} %param.6), channel_id=1, source_target_pairs={{0,4},{4,0},{8,12},{12,8},{16,20},{20,16},{24,28},{28,24},{1,5},{5... | collective-permute-start | bytes 1572872 | tf_op jit(solution)/shard_map/ppermute | solution.py:21
  9.7 20.8 %collective-permute-start = (bf16[272,128]{1,0:T(8,128)(2,1)S(1)}, bf16[272,128]{1,0:T(8,128)(2,1)S(1)}, u32[]{:S(2)}, u32[]{:S(2)}) collective-permute-start(bf16[272,128]{1,0:T(8,128)(2,1)S(1)} %pad_maximum_fusion.4), channel_id=1, source_target_pairs={{0,16},{4,20},{8,24},{12,28},{16,0},{20,4},{24,8},{28,12},{1,17},{... | collective-permute-start | bytes 208904 | tf_op jit(solution)/shard_map/ppermute | solution.py:21
  10.2 26.4 %collective-permute-start.3 = (bf16[64,512]{0,1:T(8,128)(2,1)S(1)}, bf16[64,512]{0,1:T(8,128)(2,1)S(1)}, u32[]{:S(2)}, u32[]{:S(2)}) collective-permute-start(bf16[64,512]{0,1:T(8,128)(2,1)S(1)} %dynamic-slice_bitcast_fusion), channel_id=1, source_target_pairs={{0,1},{1,0},{2,3},{3,2},{4,5},{5,4},{6,7},{7,6},{8,9},{9,8},{10,11... | collective-permute-start | bytes 196616 | tf_op jit(solution)/shard_map/ppermute | solution.py:21
  30.5 4.4 %collective-permute-start.1 = (bf16[144,256]{1,0:T(8,128)(2,1)S(1)}, bf16[144,256]{1,0:T(8,128)(2,1)S(1)}, u32[]{:S(2)}, u32[]{:S(2)}) collective-permute-start(bf16[144,256]{1,0:T(8,128)(2,1)S(1)} %maximum_maximum_fusion.1), channel_id=1, source_target_pairs={{0,8},{4,12},{8,0},{12,4},{16,24},{20,28},{24,16},{28,20},{1,9},{5... | collective-permute-start | bytes 221192 | tf_op jit(solution)/shard_map/ppermute | solution.py:21
  35.0 4.5 %collective-permute-start.2 = (bf16[80,512]{1,0:T(8,128)(2,1)S(1)}, bf16[80,512]{1,0:T(8,128)(2,1)S(1)}, u32[]{:S(2)}, u32[]{:S(2)}) collective-permute-start(bf16[80,512]{1,0:T(8,128)(2,1)S(1)} %maximum_maximum_fusion), channel_id=1, source_target_pairs={{0,4},{4,0},{8,12},{12,8},{16,20},{20,16},{24,28},{28,24},{1,5},{5... | collective-permute-start | bytes 245768 | tf_op jit(solution)/shard_map/ppermute | solution.py:21
  36.7 39.8 %collective-permute-start.4 = (bf16[64,1024]{0,1:T(8,128)(2,1)S(1)}, bf16[64,1024]{0,1:T(8,128)(2,1)S(1)}, u32[]{:S(2)}, u32[]{:S(2)}) collective-permute-start(bf16[64,1024]{0,1:T(8,128)(2,1)S(1)} %maximum_select_fusion.4), channel_id=1, source_target_pairs={{0,2},{1,3},{2,0},{3,1},{4,6},{5,7},{6,4},{7,5},{8,10},{9,11},{10,... | collective-permute-start | bytes 393224 | tf_op jit(solution)/shard_map/ppermute | solution.py:21
  41.2 10.5 %collective-permute-start.7 = (bf16[128,2048]{1,0:T(8,128)(2,1)S(1)}, bf16[128,2048]{1,0:T(8,128)(2,1)S(1)}, u32[]{:S(2)}, u32[]{:S(2)}) collective-permute-start(bf16[128,2048]{1,0:T(8,128)(2,1)S(1)} %collective-permute-done.5), channel_id=1, source_target_pairs={{0,8},{4,12},{8,0},{12,4},{16,24},{20,28},{24,16},{28,20},{1,9},{5... | collective-permute-start | bytes 1572872 | tf_op jit(solution)/shard_map/ppermute | solution.py:21
  41.9 14.9 %collective-permute-start.9 = (bf16[128,2048]{1,0:T(8,128)(2,1)S(1)}, bf16[128,2048]{1,0:T(8,128)(2,1)S(1)}, u32[]{:S(2)}, u32[]{:S(2)}) collective-permute-start(bf16[128,2048]{1,0:T(8,128)(2,1)S(1)} %collective-permute-done.5), channel_id=1, source_target_pairs={{0,4},{4,0},{8,12},{12,8},{16,20},{20,16},{24,28},{28,24},{1,5},{5... | collective-permute-start | bytes 1572872 | tf_op jit(solution)/shard_map/ppermute | solution.py:21
  44.3 23.7 %collective-permute-start.10 = (bf16[128,2048]{1,0:T(8,128)(2,1)S(1)}, bf16[128,2048]{1,0:T(8,128)(2,1)S(1)}, u32[]{:S(2)}, u32[]{:S(2)}) collective-permute-start(bf16[128,2048]{1,0:T(8,128)(2,1)S(1)} %collective-permute-done.6), channel_id=1, source_target_pairs={{0,4},{4,0},{8,12},{12,8},{16,20},{20,16},{24,28},{28,24},{1,5},{5... | collective-permute-start | bytes 1572872 | tf_op jit(solution)/shard_map/ppermute | solution.py:21
  51.7 24.0 %collective-permute-start.11 = (bf16[128,2048]{1,0:T(8,128)(2,1)S(1)}, bf16[128,2048]{1,0:T(8,128)(2,1)S(1)}, u32[]{:S(2)}, u32[]{:S(2)}) collective-permute-start(bf16[128,2048]{1,0:T(8,128)(2,1)S(1)} %collective-permute-done.7), channel_id=1, source_target_pairs={{0,4},{4,0},{8,12},{12,8},{16,20},{20,16},{24,28},{28,24},{1,5},{5... | collective-permute-start | bytes 1572872 | tf_op jit(solution)/shard_map/ppermute | solution.py:21
  76.5 3.9 %copy-start.1 = (bf16[1024,2048]{1,0:T(8,128)(2,1)S(1)}, bf16[1024,2048]{1,0:T(8,128)(2,1)}, u32[]{:S(2)}) copy-start(bf16[1024,2048]{1,0:T(8,128)(2,1)} %constant_dynamic-update-slice_fusion) | copy-start | bytes 12582916
  82.0 4.9 %copy-start.5 = (f32[2]{0:T(128)S(1)}, f32[2]{0:T(128)}, u32[]{:S(2)}) copy-start(f32[2]{0:T(128)} %param.11) | copy-start | bytes 28
  83.3 2.0 %collective-permute-start.12 = (bf16[128,1024]{1,0:T(8,128)(2,1)S(1)}, bf16[128,1024]{1,0:T(8,128)(2,1)S(1)}, u32[]{:S(2)}, u32[]{:S(2)}) collective-permute-start(bf16[128,1024]{1,0:T(8,128)(2,1)S(1)} %copy.36), channel_id=1, source_target_pairs={{0,1},{1,0},{2,3},{3,2},{4,5},{5,4},{6,7},{7,6},{8,9},{9,8},{10,11... | collective-permute-start | bytes 786440 | tf_op jit(solution)/shard_map/ppermute | solution.py:21
  85.3 8.8 %collective-permute-start.13 = (bf16[128,1024]{1,0:T(8,128)(2,1)S(1)}, bf16[128,1024]{1,0:T(8,128)(2,1)S(1)}, u32[]{:S(2)}, u32[]{:S(2)}) collective-permute-start(bf16[128,1024]{1,0:T(8,128)(2,1)S(1)} %fusion.7), channel_id=1, source_target_pairs={{0,2},{1,3},{2,0},{3,1},{4,6},{5,7},{6,4},{7,5},{8,10},{9,11},{10,... | collective-permute-start | bytes 786440 | tf_op jit(solution)/shard_map/ppermute | solution.py:21
  94.2 1.6 %collective-permute-start.14 = (bf16[128,1024]{1,0:T(8,128)(2,1)S(1)}, bf16[128,1024]{1,0:T(8,128)(2,1)S(1)}, u32[]{:S(2)}, u32[]{:S(2)}) collective-permute-start(bf16[128,1024]{1,0:T(8,128)(2,1)S(1)} %subtract_convert_fusion), channel_id=1, source_target_pairs={{0,1},{1,0},{2,3},{3,2},{4,5},{5,4},{6,7},{7,6},{8,9},{9,8},{10,11... | collective-permute-start | bytes 786440 | tf_op jit(solution)/shard_map/ppermute | solution.py:21
  96.0 4.1 %copy-start.2 = (bf16[1024,2048]{1,0:T(8,128)(2,1)S(1)}, bf16[1024,2048]{1,0:T(8,128)(2,1)}, u32[]{:S(2)}) copy-start(bf16[1024,2048]{1,0:T(8,128)(2,1)} %constant_dynamic-update-slice_fusion) | copy-start | bytes 12582916
  102.8 1.6 %collective-permute-start.15 = (bf16[128,1024]{0,1:T(8,128)(2,1)S(1)}, bf16[128,1024]{0,1:T(8,128)(2,1)S(1)}, u32[]{:S(2)}, u32[]{:S(2)}) collective-permute-start(bf16[128,1024]{0,1:T(8,128)(2,1)S(1)} %bitcast.85), channel_id=1, source_target_pairs={{0,1},{1,0},{2,3},{3,2},{4,5},{5,4},{6,7},{7,6},{8,9},{9,8},{10,11... | collective-permute-start | bytes 786440 | tf_op jit(solution)/shard_map/ppermute | solution.py:21
  104.4 13.9 %copy-start.3 = (bf16[1024,2048]{1,0:T(8,128)(2,1)S(1)}, bf16[1024,2048]{1,0:T(8,128)(2,1)}, u32[]{:S(2)}) copy-start(bf16[1024,2048]{1,0:T(8,128)(2,1)} %constant_dynamic-update-slice_fusion) | copy-start | bytes 12582916
  104.4 13.9 %copy-start.4 = (f32[1,1024]{1,0:T(1,128)S(1)}, f32[1,1024]{1,0:T(1,128)}, u32[]{:S(2)}) copy-start(f32[1,1024]{1,0:T(1,128)} %get-tuple-element.23) | copy-start | bytes 12292
  104.4 8.4 %collective-permute-start.16 = (bf16[128,1024]{0,1:T(8,128)(2,1)S(1)}, bf16[128,1024]{0,1:T(8,128)(2,1)S(1)}, u32[]{:S(2)}, u32[]{:S(2)}) collective-permute-start(bf16[128,1024]{0,1:T(8,128)(2,1)S(1)} %fusion.8), channel_id=1, source_target_pairs={{0,2},{1,3},{2,0},{3,1},{4,6},{5,7},{6,4},{7,5},{8,10},{9,11},{10,... | collective-permute-start | bytes 786440 | tf_op jit(solution)/shard_map/ppermute | solution.py:21
  112.9 1.6 %collective-permute-start.17 = (bf16[128,1024]{0,1:T(8,128)(2,1)S(1)}, bf16[128,1024]{0,1:T(8,128)(2,1)S(1)}, u32[]{:S(2)}, u32[]{:S(2)}) collective-permute-start(bf16[128,1024]{0,1:T(8,128)(2,1)S(1)} %get-tuple-element.7), channel_id=1, source_target_pairs={{0,1},{1,0},{2,3},{3,2},{4,5},{5,4},{6,7},{7,6},{8,9},{9,8},{10,11... | collective-permute-start | bytes 786440 | tf_op jit(solution)/shard_map/ppermute | solution.py:21
  120.2 1.4 collective-permute-start.18
  121.7 4.3 %collective-permute-start.19 = (bf16[64,512]{1,0:T(8,128)(2,1)S(1)}, bf16[64,512]{1,0:T(8,128)(2,1)S(1)}, u32[]{:S(2)}, u32[]{:S(2)}) collective-permute-start(bf16[64,512]{1,0:T(8,128)(2,1)S(1)} %dynamic-slice_convert_fusion), channel_id=1, source_target_pairs={{0,2},{1,3},{2,0},{3,1},{4,6},{5,7},{6,4},{7,5},{8,10},{9,11},{10,... | collective-permute-start | bytes 196616 | tf_op jit(solution)/shard_map/ppermute | solution.py:21
  126.0 6.4 %collective-permute-start.20 = (bf16[64,512]{1,0:T(8,128)(2,1)S(1)}, bf16[64,512]{1,0:T(8,128)(2,1)S(1)}, u32[]{:S(2)}, u32[]{:S(2)}) collective-permute-start(bf16[64,512]{1,0:T(8,128)(2,1)S(1)} %multiply_convert_fusion.2), channel_id=1, source_target_pairs={{0,16},{4,20},{8,24},{12,28},{16,0},{20,4},{24,8},{28,12},{1,17},{... | collective-permute-start | bytes 196616 | tf_op jit(solution)/shard_map/ppermute | solution.py:21
  132.5 5.0 %collective-permute-start.21 = (bf16[128,512]{1,0:T(8,128)(2,1)S(1)}, bf16[128,512]{1,0:T(8,128)(2,1)S(1)}, u32[]{:S(2)}, u32[]{:S(2)}) collective-permute-start(bf16[128,512]{1,0:T(8,128)(2,1)S(1)} %bitcast.80), channel_id=1, source_target_pairs={{0,8},{4,12},{8,0},{12,4},{16,24},{20,28},{24,16},{28,20},{1,9},{5... | collective-permute-start | bytes 393224 | tf_op jit(solution)/shard_map/ppermute | solution.py:21
  137.5 6.4 %collective-permute-start.22 = (bf16[256,512]{1,0:T(8,128)(2,1)S(1)}, bf16[256,512]{1,0:T(8,128)(2,1)S(1)}, u32[]{:S(2)}, u32[]{:S(2)}) collective-permute-start(bf16[256,512]{1,0:T(8,128)(2,1)S(1)} %bitcast.87), channel_id=1, source_target_pairs={{0,4},{4,0},{8,12},{12,8},{16,20},{20,16},{24,28},{28,24},{1,5},{5... | collective-permute-start | bytes 786440 | tf_op jit(solution)/shard_map/ppermute | solution.py:21

commit v2 on v0

v2 whole, which is shorter than its diff:
```python
import functools

import jax
import jax.numpy as jnp
from jax import lax
from jax.experimental import pallas as pl
from jax.experimental.pallas import tpu as pltpu
from jax.sharding import PartitionSpec as P

BF = jnp.bfloat16
F32 = jnp.float32


def first_slope(value):
    sig = jax.nn.sigmoid(value)
    return sig * (1.0 + value * (1.0 - sig))


def second_slope(value):
    sig = jax.nn.sigmoid(value)
    return sig * (1.0 - sig) * (2.0 + value * (1.0 - 2.0 * sig))


def swap(value, axis, bit):
    return lax.ppermute(value, axis, [(i, i ^ bit) for i in range(lax.axis_size(axis))])


def after(value, *others):
    return lax.optimization_barrier((value,) + others)[0]


def bits_of(size):
    found = []
    bit = 1
    while bit < size:
        found.append(bit)
        bit *= 2
    return found


def onehots(labels, copies):
    copy = labels[1:2, :].astype(F32)
    return [(copy == float(c)).astype(F32) for c in range(copies)]


def over_tiles(count, body):
    if count == 1:
        body(0)
    else:
        lax.fori_loop(0, count, lambda tile, none: body(tile), None)


def tile_at(tile, size):
    return pl.ds(tile * size if isinstance(tile, int) else pl.multiple_of(tile * size, size), size)


def times_tokens(core, part, pairs, mine, other, held, rows):
    total = None
    for j in range(pairs):
        for value, side in ((mine, core), (other, 1 - core)):
            columns = pl.ds(pl.multiple_of((2 * j + side) * part, part), part)
            term = lax.dot_general(
                value[:, pl.ds(j * part, part)],
                held[rows, columns],
                (((1,), (1,)), ((), ())),
                preferred_element_type=F32,
            )
            total = term if total is None else total + term
    return total


def contract(core, part, pairs, delta, held, rows, send, keep, sums):
    only = rows.size == held.shape[0]
    for j in range(pairs):
        place = pl.ds(j * part, part)
        for out, side in ((send if only else sums, 1 - core), (keep, core)):
            columns = pl.ds(pl.multiple_of((2 * j + side) * part, part), part)
            term = jnp.dot(delta, held[rows, columns], preferred_element_type=F32)
            out[:, place] = (term if only else out[:, place] + term).astype(out.dtype)


def each_tile(held, send, keep, sums, body):
    size = min(held.shape[0], 1024)
    count = held.shape[0] // size
    if count > 1:
        keep[...] = jnp.zeros_like(keep)
        sums[...] = jnp.zeros_like(sums)
    over_tiles(count, lambda tile: body(tile_at(tile, size)))
    if count > 1:
        send[...] = sums[...].astype(BF)


def of_copy(value, hots):
    wide = value.shape[0] // len(hots)
    return sum(value[c * wide : (c + 1) * wide] * hot for c, hot in enumerate(hots))


def by_copy(delta, hots):
    delta = delta.astype(F32)
    return jnp.concatenate([delta * hot for hot in hots], 0).astype(BF)


def prepare_kernel(wide, side_of, scalars, upstream, value_weight, weight, up, labels, sent, turned):
    me = scalars[0]
    group = 128 // wide
    columns = pl.ds(pl.multiple_of((me // group) * 128, 128), 128)
    turned[...] = value_weight[:, columns].astype(F32).T
    own = pl.ds(pl.multiple_of((me % group) * wide, wide), wide)
    weight[...] = turned[own, :].astype(BF)
    up[...] = upstream[...].astype(F32).T.astype(BF)
    row = lax.broadcasted_iota(jnp.int32, labels.shape, 0)
    both = jnp.where(row == 0, scalars[2], jnp.where(row == 1, scalars[3], 0))
    labels[...] = both.astype(F32).astype(BF)
    every_second(up, 1 - side_of(me), wide, sent)
    sent[pl.ds(up.shape[0] // 2, 16), :] = labels[...]


def every_second(source, side, wide, target, columns=slice(None)):
    for k in range(source.shape[0] // wide // 2):
        block = pl.ds(pl.multiple_of((2 * k + side) * wide, wide), wide)
        target[pl.ds(k * wide, wide), columns] = source[block, :]


def join_kernel(wide, side_of, next_side, scalars, up, labels, came, new_up, new_labels, *sent):
    me = scalars[0]
    half, long = up.shape[0] // 2, up.shape[1]
    every_second(up, side_of(me), wide, new_up, pl.ds(0, long))
    new_up[:, pl.ds(long, long)] = came[pl.ds(0, half), :]
    new_labels[:, pl.ds(0, long)] = labels[...]
    new_labels[:, pl.ds(long, long)] = came[pl.ds(half, 16), :]
    if sent:
        every_second(new_up, 1 - next_side(me), wide, sent[0])
        sent[0][pl.ds(half // 2, 16), :] = new_labels[...]


def first_kernel(sizes, scalars, *refs):
    part, pairs, copies, length, count = sizes
    pieces, (weight, up, labels, held, primal_out, send, keep, sums) = refs[:count], refs[count:]
    quarter = scalars[1]
    row = 0
    for piece in pieces:
        held[pl.ds(row, piece.shape[0]), :] = piece[...]
        row += piece.shape[0]
    wide = up.shape[0]

    def body(rows):
        primal = None
        for i in range(2 * pairs):
            columns = pl.ds(pl.multiple_of((quarter ^ i) * part, part), part)
            term = lax.dot_general(
                weight[pl.ds(i * wide, wide), :],
                held[rows, columns],
                (((1,), (1,)), ((), ())),
                preferred_element_type=F32,
            )
            primal = term if primal is None else primal + term
        primal_out[:, rows] = primal
        hots = onehots(labels[:, rows], copies)
        forget = labels[0:1, rows].astype(F32)
        delta = (forget * up[:, rows].astype(F32) * first_slope(primal) / length).astype(BF)
        contract(quarter % 2, part, pairs, by_copy(delta, hots), held, rows, send, keep, sums)

    each_tile(held, send, keep, sums, body)


def second_kernel(sizes, scalars, held, mine, other, up, labels, send, keep, sums):
    part, pairs, copies, length = sizes
    core = scalars[1] % 2

    def body(rows):
        hots = onehots(labels[:, rows], copies)
        altered = of_copy(times_tokens(core, part, pairs, mine, other, held, rows), hots)
        sign = 1.0 - 2.0 * labels[0:1, rows].astype(F32)
        delta = (sign * up[:, rows].astype(F32) * first_slope(altered) / length).astype(BF)
        contract(core, part, pairs, by_copy(delta, hots), held, rows, send, keep, sums)

    each_tile(held, send, keep, sums, body)


def third_kernel(sizes, scalars, rate, held, mine, other, up, labels, primal, send, keep, sums):
    part, pairs, copies, length = sizes
    core = scalars[1] % 2

    def body(rows):
        hots = onehots(labels[:, rows], copies)
        forward = of_copy(times_tokens(core, part, pairs, mine, other, held, rows), hots)
        forget = labels[0:1, rows].astype(F32)
        own_rate = sum(hot * rate[c] for c, hot in enumerate(hots))
        slope = second_slope(primal[:, rows])
        delta = (forget * up[:, rows].astype(F32) * slope * forward / length).astype(BF)
        delta = (own_rate * delta.astype(F32)).astype(BF)
        contract(core, part, pairs, delta, held, rows, send, keep, sums)

    each_tile(held, send, keep, sums, body)


def add_kernel(mine, came, total, sent):
    value = mine[...] + came[...].astype(F32)
    total[...] = value
    sent[...] = value.astype(BF)


def attack_kernel(copies, scalars, rate, mine, came, weight, attacked):
    quarter = scalars[1]
    part = weight.shape[1]
    wide = mine.shape[0] // copies
    for j in range(mine.shape[1] // part):
        place = quarter ^ (2 * j + quarter % 2)
        own = weight[pl.ds(pl.multiple_of(place * wide, wide), wide), :].astype(F32)
        columns = pl.ds(j * part, part)
        for c in range(copies):
            rows = pl.ds(c * wide, wide)
            grad = mine[rows, columns] + came[rows, columns].astype(F32)
            attacked[rows, columns] = (own - rate[c] * grad).astype(BF)


def tangent_kernel(copies, scalars, mine, came, tangent, outer):
    value = mine[...] + came[...].astype(F32)
    tangent[...] = value.astype(BF)
    wide, part = outer.shape
    own = pl.ds(pl.multiple_of((scalars[1] // 2) * part, part), part)
    outer[...] = sum(
        mine[pl.ds(c * wide, wide), own] + came[pl.ds(c * wide, wide), own].astype(F32)
        for c in range(copies)
    )


def halve_kernel(bit, scalars, mine, came, total, sent, whole):
    whole[...] = mine[...] + came[...].astype(F32)
    half = total.shape[1]
    side = (scalars[1] // bit) % 2
    total[...] = whole[:, pl.ds(pl.multiple_of(side * half, half), half)]
    sent[...] = whole[:, pl.ds(pl.multiple_of((1 - side) * half, half), half)].astype(BF)


def result_kernel(scale, outer, mine, came, result):
    result[...] = (scale * (outer[...] - (mine[...] + came[...].astype(F32)))).astype(BF)


def place_kernel(order, scalars, *refs):
    blocks, out = refs[:-1], refs[-1]
    me = scalars[0]
    wide = blocks[0].shape[0]
    flat = []
    for ref in blocks:
        flat += [ref[pl.ds(row, wide), :].astype(F32) for row in range(0, ref.shape[0], wide)]
    where = {r: flat[i] for i, r in enumerate(order)}
    for r in order:
        if r % 2:
            continue
        low, high = where[r], where[r ^ 1]
        odd = me % 2 == 1
        pair = jnp.concatenate([jnp.where(odd, high, low), jnp.where(odd, low, high)], 0)
        columns = pl.ds(pl.multiple_of(((me ^ r) // 2) * 128, 128), 128)
        out[:, columns] = pair.T


def run(kernel, scalars, arrays, outs, scratch=()):
    nbytes = sum(a.size * a.dtype.itemsize for a in arrays)
    nbytes += sum(s[0] * s[1] * jnp.dtype(t).itemsize for s, t in outs)
    smem = pl.BlockSpec(memory_space=pltpu.SMEM)
    vmem = pl.BlockSpec(memory_space=pltpu.VMEM)
    return pl.pallas_call(
        kernel,
        out_shape=[jax.ShapeDtypeStruct(s, t) for s, t in outs],
        in_specs=[smem] * len(scalars) + [vmem] * len(arrays),
        out_specs=[vmem] * len(outs),
        scratch_shapes=[pltpu.VMEM(s, t) for s, t in scratch],
        compiler_params=pltpu.CompilerParams(vmem_limit_bytes=nbytes + (8 << 20)),
    )(*scalars, *arrays)


def local(tokens, upstream, value_weight, forget_label, copy_index, adv_rate):
    dp, fsdp = lax.axis_size("dp"), lax.axis_size("fsdp")
    rows, features = tokens.shape
    outs = upstream.shape[1]
    wide = outs // dp
    part = features // fsdp
    pairs = fsdp // 2
    copies = adv_rate.shape[0]
    seq_length = rows * fsdp
    held_rows = rows * dp
    me = lax.axis_index("dp").astype(jnp.int32)
    quarter = lax.axis_index("fsdp").astype(jnp.int32)
    scalars = jnp.stack([me, quarter, forget_label[0], copy_index[0]])
    dp_bits = bits_of(dp)[::-1]
    far_bits = bits_of(fsdp)[1:]
    up_bits = dp_bits[::-1]

    def side_of(bit):
        return lambda me: (me // bit) % 2

    weight, up, labels, sent = run(
        functools.partial(prepare_kernel, wide, side_of(up_bits[0])),
        [scalars],
        [upstream, value_weight],
        [((wide, part), BF), ((outs, rows), BF), ((16, rows), BF), ((outs // 2 + 16, rows), BF)],
        [((128, part), F32)],
    )

    top_bit = dp_bits[0]
    tops = [top_bit]
    for bit in dp_bits[1:]:
        tops.append(tops[-1] | bit)
    half_rows = rows // 2
    first = {0: tokens[:half_rows]}
    second = {0: tokens[half_rows:]}
    whole = {0: tokens}
    late = {}
    for step, (top, up_bit) in enumerate(zip(tops, up_bits), 1):
        wholes, firsts = {}, {}
        new_late = {}
        for r in range(1, dp):
            if bin(r).count("1") != step:
                continue
            bit = r & -r
            if r < top_bit:
                wholes[r] = swap(whole[r ^ bit], "dp", bit)
                continue
            way = 2 * bit if r == dp - 1 and dp > 2 else bit
            firsts[r] = swap(first[r ^ way], "dp", way)
            if r != top:
                new_late[r] = swap({**second, **late}[r ^ bit], "dp", bit)
        came_up = swap(sent, "dp", up_bit)
        wholes, came_up = lax.optimization_barrier((wholes, came_up))
        firsts, late = lax.optimization_barrier((firsts, late))
        whole.update(wholes)
        first.update(firsts)
        second.update(late)
        late = new_late
        second[top] = swap(second[top ^ dp_bits[step - 1]], "dp", dp_bits[step - 1])
        high, long = up.shape[0] // 2, 2 * up.shape[1]
        shapes = [((high, long), BF), ((16, long), BF)]
        if step < len(dp_bits):
            shapes.append(((high // 2 + 16, long), BF))
        following = side_of(up_bits[step]) if step < len(dp_bits) else None
        joined = run(
            functools.partial(join_kernel, wide, side_of(up_bit), following),
            [scalars],
            [up, labels, came_up],
            shapes,
        )
        up, labels = joined[:2]
        sent = joined[-1]
    second.update(late)
    order = [0]
    for bit in up_bits:
        order = order + [r ^ bit for r in order]
    flat = []
    for r in order:
        flat += [whole[r]] if r in whole else [first[r], second[r]]

    weight = after(weight, first[top_bit])
    for bit in bits_of(fsdp):
        weight = jnp.concatenate([weight, swap(weight, "fsdp", bit)])

    def total(send, keep, bits):
        shape = keep.shape
        came = swap(send, "fsdp", 1)
        for bit in bits:
            keep, sent = run(add_kernel, [], [keep, came], [(shape, F32), (shape, BF)])
            came = swap(sent, "fsdp", bit)
        return keep, came

    sizes = (part, pairs, copies, seq_length)
    stacked = (copies * wide, features // 2)
    held, primal, send, keep = run(
        functools.partial(first_kernel, sizes + (len(flat),)),
        [scalars],
        flat + [weight, up, labels],
        [((held_rows, features), BF), ((wide, held_rows), F32), (stacked, BF), (stacked, F32)],
        [(stacked, F32)],
    )
    (attacked,) = run(
        functools.partial(attack_kernel, copies),
        [scalars, adv_rate],
        [*total(send, keep, far_bits), weight],
        [(stacked, BF)],
    )
    send, keep = run(
        functools.partial(second_kernel, sizes),
        [scalars],
        [held, attacked, swap(attacked, "fsdp", 1), up, labels],
        [(stacked, BF), (stacked, F32)],
        [(stacked, F32)],
    )
    tangent, outer = run(
        functools.partial(tangent_kernel, copies),
        [scalars],
        [*total(send, keep, far_bits)],
        [(stacked, BF), ((wide, part), F32)],
    )
    send, keep = run(
        functools.partial(third_kernel, sizes),
        [scalars, adv_rate],
        [held, tangent, swap(tangent, "fsdp", 1), up, labels, primal],
        [((wide, features // 2), BF), ((wide, features // 2), F32)],
        [((wide, features // 2), F32)],
    )

    came = swap(send, "fsdp", 1)
    for bit in far_bits[::-1]:
        shape = (wide, keep.shape[1] // 2)
        keep, sent = run(
            functools.partial(halve_kernel, bit),
            [scalars],
            [keep, came],
            [(shape, F32), (shape, BF)],
            [(keep.shape, F32)],
        )
        came = swap(sent, "fsdp", bit)
    scale = (float(seq_length) / float(dp)) ** 0.5
    (result,) = run(
        functools.partial(result_kernel, scale), [], [outer, keep, came], [((wide, part), BF)]
    )
    blocks = [result]
    came_order = [0]
    for bit in dp_bits:
        came_order = came_order + [r ^ bit for r in came_order]
        sent = blocks[0] if len(blocks) == 1 else jnp.concatenate(blocks)
        blocks.append(swap(sent, "dp", bit))
    if 2 * wide == 128:
        (placed,) = run(
            functools.partial(place_kernel, came_order), [scalars], blocks, [((part, outs), F32)]
        )
        return placed
    result = jnp.concatenate(blocks).reshape([2] * len(dp_bits) + [wide, part])
    for place, bit in enumerate(dp_bits[::-1]):
        side = (me // bit) % 2
        result = jnp.where(side == 1, jnp.flip(result, place), result)
    axes = tuple(range(len(dp_bits)))
    result = result.transpose(axes[::-1] + (len(axes), len(axes) + 1))
    return result.reshape(outs, part).T.astype(F32)


def solution(mesh):
    in_specs = (
        P(("dp", "fsdp"), None),
        P(("dp", "fsdp"), None),
        P("fsdp", None),
        P("dp"),
        P("dp"),
        P(),
    )
    out_specs = P("fsdp", None)
    return jax.shard_map(local, mesh=mesh, in_specs=in_specs, out_specs=out_specs, check_vma=False)
```

time: 458 us -> 115 us (0.25)
  waiting for transfers between devices: 396 us -> 65 us
  starting transfers between devices: 3.72 us -> 29.3 us
  Pallas kernels: 0 us -> 14.6 us
  blocking collectives: 14.4 us -> 0 us
  between operations: 14.9 us -> 1.47 us
  other arithmetic: 12.3 us -> 0.11 us
  matrix products: 11.7 us -> 0 us
    psum x3 -> x0, waiting for transfers between devices: 281 us -> none  [the longest x1 102 us: local(): stacked = lax.psum(onehot[:, None, None] * grad_local[None], 'dp')]
    ppermute x0 -> x27, waiting for transfers between devices: none -> 65 us  [swap(): lax.ppermute(value, axis, [(i, i ^ bit) for i in range(lax.axis_size(axis...]
    all_gather x3 -> x0, waiting for transfers between devices: 57.3 us -> none  [the longest x1 26.3 us: local(): primal = project(lax.all_gather(value_weight, 'fsdp', axis=0, tiled=True))]
    reduce_scatter x1 -> x0, waiting for transfers between devices: 44 us -> none  [local(): lax.psum_scatter(lax.dot_general(tokens, delta_adv, (((0,), (0,)), ((), (...]
    ppermute x0 -> x27, starting transfers between devices: none -> 29.3 us  [swap(): lax.ppermute(value, axis, [(i, i ^ bit) for i in range(lax.axis_size(axis...]
    pallas_call x0 -> x14, Pallas kernels: none -> 14.6 us  [run(): pl.pallas_call(kernel, out_shape=[jax.ShapeDtypeStruct(s, t) for s, t in...]
    all_gather x2 -> x0, blocking collectives: 14.4 us -> none  [the longest x1 7.18 us: local(): lax.all_gather(delta_out, 'fsdp', axis=0, tiled=True)]
    all_to_all x1 -> x0, waiting for transfers between devices: 12.7 us -> none  [local(): lax.all_to_all(tokens, 'fsdp', split_axis=1, concat_axis=0, tiled=True)]
  transfers between devices with their start and end apart: 8 -> 27, of which waited for: 8 -> 19; matrix products, arithmetic and copies ran while one was open for 0% -> 1% of each run, Pallas kernels for 0% -> 2%
where the time goes in v2:
time: 115 us
  waiting for transfers between devices  65 us (57%)
  starting transfers between devices  29.3 us (25%)
  Pallas kernels  14.6 us (13%)
  local copies, waits for them, and re-layouts  4.07 us (4%)
  between operations  1.47 us (1%)
    ppermute x27, waiting for transfers between devices, swap(): lax.ppermute(value, axis, [(i, i ^ bit) for i in range(lax.axis_size(axis...  65 us
    ppermute x27, starting transfers between devices, swap(): lax.ppermute(value, axis, [(i, i ^ bit) for i in range(lax.axis_size(axis...  29.3 us
    pallas_call x14, Pallas kernels, run(): pl.pallas_call(kernel, out_shape=[jax.ShapeDtypeStruct(s, t) for s, t in...  14.6 us
    unnamed x10, local copies, waits for them, and re-layouts  3 us
  transfers between devices with their start and end apart: 27, of which 19 were waited for; matrix products, arithmetic and copies ran while one was open for 1% of the time, Pallas kernels for 2%

profile of v2, /device:TPU:0, one launch (start us, length us, event | category | flops | bytes accessed | tf_op | source)
XLA Modules:
  0.0 114.6 jit_solution(3560421001268993893)
XLA Ops:
  0.0 3.0 %collective-permute-start.1 = (bf16[128,2048]{1,0:T(8,128)(2,1)}, bf16[128,2048]{1,0:T(8,128)(2,1)S(1)}, u32[]{:S(2)}, u32[]{:S(2)}) collective-permute-start(bf16[128,2048]{1,0:T(8,128)(2,1)} %refs_0_.1), channel_id=1, source_target_pairs={{0,8},{4,12},{8,0},{12,4},{16,24},{20,28},{24,16},{28,20},{1,9},{5... | collective-permute-start | bytes 1572872 | tf_op jit(solution)/shard_map/ppermute | solution.py:25
  3.0 1.5 %collective-permute-start = (bf16[128,2048]{1,0:T(8,128)(2,1)}, bf16[128,2048]{1,0:T(8,128)(2,1)S(1)}, u32[]{:S(2)}, u32[]{:S(2)}) collective-permute-start(bf16[128,2048]{1,0:T(8,128)(2,1)} %refs_0_.1), channel_id=1, source_target_pairs={{0,4},{4,0},{8,12},{12,8},{16,20},{20,16},{24,28},{28,24},{1,5},{5... | collective-permute-start | bytes 1572872 | tf_op jit(solution)/shard_map/ppermute | solution.py:25
  5.6 2.7 %collective-permute-start.5 = (bf16[64,2048]{1,0:T(8,128)(2,1)S(1)}, bf16[64,2048]{1,0:T(8,128)(2,1)S(1)}, u32[]{:S(2)}, u32[]{:S(2)}) collective-permute-start(bf16[64,2048]{1,0:T(8,128)(2,1)S(1)} %get-tuple-element.82), channel_id=1, source_target_pairs={{0,16},{4,20},{8,24},{12,28},{16,0},{20,4},{24,8},{28,12},{1,17},{... | collective-permute-start | bytes 786440 | tf_op jit(solution)/shard_map/ppermute | solution.py:25
  13.2 4.9 %collective-permute-done.2.came = bf16[272,128]{1,0:T(8,128)(2,1)S(1)} collective-permute-done((bf16[272,128]{1,0:T(8,128)(2,1)S(1)}, bf16[272,128]{1,0:T(8,128)(2,1)S(1)}, u32[]{:S(2)}, u32[]{:S(2)}) %collective-permute-start.2) | collective-permute-done | bytes 69664 | tf_op jit(solution)/shard_map/ppermute | solution.py:25
  18.1 6.0 %collective-permute-done.1.refs_2_ = bf16[128,2048]{1,0:T(8,128)(2,1)S(1)} collective-permute-done((bf16[128,2048]{1,0:T(8,128)(2,1)}, bf16[128,2048]{1,0:T(8,128)(2,1)S(1)}, u32[]{:S(2)}, u32[]{:S(2)}) %collective-permute-start.1) | collective-permute-done | bytes 524320 | tf_op jit(solution)/shard_map/ppermute | solution.py:25
  24.1 2.7 %collective-permute-start.3 = (bf16[128,2048]{1,0:T(8,128)(2,1)S(1)}, bf16[128,2048]{1,0:T(8,128)(2,1)S(1)}, u32[]{:S(2)}, u32[]{:S(2)}) collective-permute-start(bf16[128,2048]{1,0:T(8,128)(2,1)S(1)} %collective-permute-done.1.refs_2_), channel_id=1, source_target_pairs={{0,4},{4,0},{8,12},{12,8},{16,20},{20,16},{24,28},{28,24},{1,5},{5... | collective-permute-start | bytes 1572872 | tf_op jit(solution)/shard_map/ppermute | solution.py:25
  27.0 4.1 %collective-permute-done.6.refs_5_ = bf16[64,2048]{1,0:T(8,128)(2,1)S(1)} collective-permute-done((bf16[64,2048]{1,0:T(8,128)(2,1)S(1)}, bf16[64,2048]{1,0:T(8,128)(2,1)S(1)}, u32[]{:S(2)}, u32[]{:S(2)}) %collective-permute-start.6) | collective-permute-done | bytes 262176 | tf_op jit(solution)/shard_map/ppermute | solution.py:25
  32.3 2.0 %collective-permute-start.4 = (bf16[144,256]{1,0:T(8,128)(2,1)S(1)}, bf16[144,256]{1,0:T(8,128)(2,1)S(1)}, u32[]{:S(2)}, u32[]{:S(2)}) collective-permute-start(bf16[144,256]{1,0:T(8,128)(2,1)S(1)} %get-tuple-element.49), channel_id=1, source_target_pairs={{0,8},{4,12},{8,0},{12,4},{16,24},{20,28},{24,16},{28,20},{1,9},{5... | collective-permute-start | bytes 221192 | tf_op jit(solution)/shard_map/ppermute | solution.py:25
  34.4 2.4 %collective-permute-done.8.refs_8_ = bf16[64,2048]{1,0:T(8,128)(2,1)S(1)} collective-permute-done((bf16[64,2048]{1,0:T(8,128)(2,1)S(1)}, bf16[64,2048]{1,0:T(8,128)(2,1)S(1)}, u32[]{:S(2)}, u32[]{:S(2)}) %collective-permute-start.8) | collective-permute-done | bytes 262176 | tf_op jit(solution)/shard_map/ppermute | solution.py:25
  36.9 8.4 %collective-permute-done.7.refs_6_ = bf16[64,2048]{1,0:T(8,128)(2,1)S(1)} collective-permute-done((bf16[64,2048]{1,0:T(8,128)(2,1)S(1)}, bf16[64,2048]{1,0:T(8,128)(2,1)S(1)}, u32[]{:S(2)}, u32[]{:S(2)}) %collective-permute-start.7) | collective-permute-done | bytes 262176 | tf_op jit(solution)/shard_map/ppermute | solution.py:25
  45.3 1.5 %collective-permute-start.14 = (bf16[128,512]{1,0:T(8,128)(2,1)S(1)}, bf16[128,512]{1,0:T(8,128)(2,1)S(1)}, u32[]{:S(2)}, u32[]{:S(2)}) collective-permute-start(bf16[128,512]{1,0:T(8,128)(2,1)S(1)} %pad_maximum_fusion.1), channel_id=1, source_target_pairs={{0,2},{1,3},{2,0},{3,1},{4,6},{5,7},{6,4},{7,5},{8,10},{9,11},{10,... | collective-permute-start | bytes 393224 | tf_op jit(solution)/shard_map/ppermute | solution.py:25
  46.8 2.1 %collective-permute-start.12 = (bf16[64,2048]{1,0:T(8,128)(2,1)S(1)}, bf16[64,2048]{1,0:T(8,128)(2,1)S(1)}, u32[]{:S(2)}, u32[]{:S(2)}) collective-permute-start(bf16[64,2048]{1,0:T(8,128)(2,1)S(1)} %collective-permute-done.11.refs_9_), channel_id=1, source_target_pairs={{0,4},{4,0},{8,12},{12,8},{16,20},{20,16},{24,28},{28,24},{1,5},{5... | collective-permute-start | bytes 786440 | tf_op jit(solution)/shard_map/ppermute | solution.py:25
  49.5 3.0 %collective-permute-start.15 = (bf16[80,512]{1,0:T(8,128)(2,1)S(1)}, bf16[80,512]{1,0:T(8,128)(2,1)S(1)}, u32[]{:S(2)}, u32[]{:S(2)}) collective-permute-start(bf16[80,512]{1,0:T(8,128)(2,1)S(1)} %get-tuple-element.62), channel_id=1, source_target_pairs={{0,16},{4,20},{8,24},{12,28},{16,0},{20,4},{24,8},{28,12},{1,17},{... | collective-permute-start | bytes 245768 | tf_op jit(solution)/shard_map/ppermute | solution.py:25
  53.1 1.8 %collective-permute-done.15.came = bf16[80,512]{1,0:T(8,128)(2,1)S(1)} collective-permute-done((bf16[80,512]{1,0:T(8,128)(2,1)S(1)}, bf16[80,512]{1,0:T(8,128)(2,1)S(1)}, u32[]{:S(2)}, u32[]{:S(2)}) %collective-permute-start.15) | collective-permute-done | bytes 81952 | tf_op jit(solution)/shard_map/ppermute | solution.py:25
  56.5 2.9 %shard_map.68 = (bf16[1024,2048]{1,0:T(8,128)(2,1)S(1)}, f32[64,1024]{1,0:T(8,128)S(1)}, bf16[128,1024]{1,0:T(8,128)(2,1)S(1)}, f32[128,1024]{1,0:T(8,128)S(1)}) custom-call(s32[4]{0:T(128)S(1)} %pad_add_fusion.scalars, bf16[128,2048]{1,0:T(8,128)(2,1)S(1)} %copy-done, bf16[128,2048]{1,0:T(8,128)(2,1)S(1)} %collective-permute-done.refs_1_, ...), custom_call_target="tpu_custom_call" | custom-call | tf_op jit(solution)/shard_map/pallas_call | solution.py:263
  59.5 1.5 %collective-permute-done.16.came = bf16[128,1024]{1,0:T(8,128)(2,1)S(1)} collective-permute-done((bf16[128,1024]{1,0:T(8,128)(2,1)S(1)}, bf16[128,1024]{1,0:T(8,128)(2,1)S(1)}, u32[]{:S(2)}, u32[]{:S(2)}) %collective-permute-start.16) | collective-permute-done | bytes 262176 | tf_op jit(solution)/shard_map/ppermute | solution.py:25
  61.9 7.6 %collective-permute-done.17.came = bf16[128,1024]{1,0:T(8,128)(2,1)S(1)} collective-permute-done((bf16[128,1024]{1,0:T(8,128)(2,1)S(1)}, bf16[128,1024]{1,0:T(8,128)(2,1)S(1)}, u32[]{:S(2)}, u32[]{:S(2)}) %collective-permute-start.17) | collective-permute-done | bytes 262176 | tf_op jit(solution)/shard_map/ppermute | solution.py:25
  70.3 1.5 %collective-permute-done.18.other = bf16[128,1024]{1,0:T(8,128)(2,1)S(1)} collective-permute-done((bf16[128,1024]{1,0:T(8,128)(2,1)S(1)}, bf16[128,1024]{1,0:T(8,128)(2,1)S(1)}, u32[]{:S(2)}, u32[]{:S(2)}) %collective-permute-start.18) | collective-permute-done | bytes 262176 | tf_op jit(solution)/shard_map/ppermute | solution.py:25
  71.8 2.7 %shard_map.71 = (bf16[128,1024]{1,0:T(8,128)(2,1)S(1)}, f32[128,1024]{1,0:T(8,128)S(1)}) custom-call(s32[4]{0:T(128)S(1)} %pad_add_fusion.scalars, bf16[1024,2048]{1,0:T(8,128)(2,1)S(1)} %get-tuple-element.65.held, bf16[128,1024]{1,0:T(8,128)(2,1)S(1)} %shard_map.70.mine, bf16[128,1024]{1,0:T(8,128)(2,1)S(1)} %collective-permute-done.18.other, ...), custom_call_target="tpu_custom_call" | custom-call | tf_op jit(solution)/shard_map/pallas_call | solution.py:263
  74.7 1.4 %collective-permute-done.19.came = bf16[128,1024]{1,0:T(8,128)(2,1)S(1)} collective-permute-done((bf16[128,1024]{1,0:T(8,128)(2,1)S(1)}, bf16[128,1024]{1,0:T(8,128)(2,1)S(1)}, u32[]{:S(2)}, u32[]{:S(2)}) %collective-permute-start.19) | collective-permute-done | bytes 262176 | tf_op jit(solution)/shard_map/ppermute | solution.py:25
  77.0 7.6 %collective-permute-done.20.came = bf16[128,1024]{1,0:T(8,128)(2,1)S(1)} collective-permute-done((bf16[128,1024]{1,0:T(8,128)(2,1)S(1)}, bf16[128,1024]{1,0:T(8,128)(2,1)S(1)}, u32[]{:S(2)}, u32[]{:S(2)}) %collective-permute-start.20) | collective-permute-done | bytes 262176 | tf_op jit(solution)/shard_map/ppermute | solution.py:25
  85.3 1.5 %collective-permute-done.21.other = bf16[128,1024]{1,0:T(8,128)(2,1)S(1)} collective-permute-done((bf16[128,1024]{1,0:T(8,128)(2,1)S(1)}, bf16[128,1024]{1,0:T(8,128)(2,1)S(1)}, u32[]{:S(2)}, u32[]{:S(2)}) %collective-permute-start.21) | collective-permute-done | bytes 262176 | tf_op jit(solution)/shard_map/ppermute | solution.py:25
  86.8 2.8 %shard_map.74 = (bf16[64,1024]{1,0:T(8,128)(2,1)S(1)}, f32[64,1024]{1,0:T(8,128)S(1)}) custom-call(s32[4]{0:T(128)S(1)} %pad_add_fusion.scalars, f32[2]{0:T(128)S(1)} %copy-done.3, bf16[1024,2048]{1,0:T(8,128)(2,1)S(1)} %get-tuple-element.65.held, bf16[128,1024]{1,0:T(8,128)(2,1)S(1)} %get-tuple-element.75.mine, ...), custom_call_target="tpu_custom_call" | custom-call | tf_op jit(solution)/shard_map/pallas_call | solution.py:263
  89.9 1.2 %collective-permute-done.22.came = bf16[64,1024]{1,0:T(8,128)(2,1)S(1)} collective-permute-done((bf16[64,1024]{1,0:T(8,128)(2,1)S(1)}, bf16[64,1024]{1,0:T(8,128)(2,1)S(1)}, u32[]{:S(2)}, u32[]{:S(2)}) %collective-permute-start.22) | collective-permute-done | bytes 131104 | tf_op jit(solution)/shard_map/ppermute | solution.py:25
  92.5 3.6 %collective-permute-done.23.came = bf16[64,512]{1,0:T(8,128)(2,1)S(1)} collective-permute-done((bf16[64,512]{1,0:T(8,128)(2,1)S(1)}, bf16[64,512]{1,0:T(8,128)(2,1)S(1)}, u32[]{:S(2)}, u32[]{:S(2)}) %collective-permute-start.23) | collective-permute-done | bytes 65568 | tf_op jit(solution)/shard_map/ppermute | solution.py:25
  96.0 3.0 %collective-permute-start.24 = (bf16[64,512]{1,0:T(8,128)(2,1)S(1)}, bf16[64,512]{1,0:T(8,128)(2,1)S(1)}, u32[]{:S(2)}, u32[]{:S(2)}) collective-permute-start(bf16[64,512]{1,0:T(8,128)(2,1)S(1)} %shard_map.76.refs_0_), channel_id=1, source_target_pairs={{0,16},{4,20},{8,24},{12,28},{16,0},{20,4},{24,8},{28,12},{1,17},{... | collective-permute-start | bytes 196616 | tf_op jit(solution)/shard_map/ppermute | solution.py:25
  99.0 2.3 %collective-permute-done.24.refs_1_ = bf16[64,512]{1,0:T(8,128)(2,1)S(1)} collective-permute-done((bf16[64,512]{1,0:T(8,128)(2,1)S(1)}, bf16[64,512]{1,0:T(8,128)(2,1)S(1)}, u32[]{:S(2)}, u32[]{:S(2)}) %collective-permute-start.24) | collective-permute-done | bytes 65568 | tf_op jit(solution)/shard_map/ppermute | solution.py:25
  101.4 1.9 %collective-permute-start.25 = (bf16[128,512]{1,0:T(8,128)(2,1)S(1)}, bf16[128,512]{1,0:T(8,128)(2,1)S(1)}, u32[]{:S(2)}, u32[]{:S(2)}) collective-permute-start(bf16[128,512]{1,0:T(8,128)(2,1)S(1)} %pad_maximum_fusion.2), channel_id=1, source_target_pairs={{0,8},{4,12},{8,0},{12,4},{16,24},{20,28},{24,16},{28,20},{1,9},{5... | collective-permute-start | bytes 393224 | tf_op jit(solution)/shard_map/ppermute | solution.py:25
  103.3 3.1 %collective-permute-done.25.refs_2_ = bf16[128,512]{1,0:T(8,128)(2,1)S(1)} collective-permute-done((bf16[128,512]{1,0:T(8,128)(2,1)S(1)}, bf16[128,512]{1,0:T(8,128)(2,1)S(1)}, u32[]{:S(2)}, u32[]{:S(2)}) %collective-permute-start.25) | collective-permute-done | bytes 131104 | tf_op jit(solution)/shard_map/ppermute | solution.py:25
  106.4 1.8 %collective-permute-start.26 = (bf16[256,512]{1,0:T(8,128)(2,1)S(1)}, bf16[256,512]{1,0:T(8,128)(2,1)S(1)}, u32[]{:S(2)}, u32[]{:S(2)}) collective-permute-start(bf16[256,512]{1,0:T(8,128)(2,1)S(1)} %pad_maximum_fusion), channel_id=1, source_target_pairs={{0,4},{4,0},{8,12},{12,8},{16,20},{20,16},{24,28},{28,24},{1,5},{5... | collective-permute-start | bytes 786440 | tf_op jit(solution)/shard_map/ppermute | solution.py:25
  108.2 4.6 %collective-permute-done.26.refs_3_ = bf16[256,512]{1,0:T(8,128)(2,1)S(1)} collective-permute-done((bf16[256,512]{1,0:T(8,128)(2,1)S(1)}, bf16[256,512]{1,0:T(8,128)(2,1)S(1)}, u32[]{:S(2)}, u32[]{:S(2)}) %collective-permute-start.26) | collective-permute-done | bytes 262176 | tf_op jit(solution)/shard_map/ppermute | solution.py:25
  112.8 1.7 %shard_map.77 = f32[512,512]{1,0:T(8,128)} custom-call(s32[4]{0:T(128)S(1)} %pad_add_fusion.scalars, bf16[64,512]{1,0:T(8,128)(2,1)S(1)} %shard_map.76.refs_0_, bf16[64,512]{1,0:T(8,128)(2,1)S(1)} %collective-permute-done.24.refs_1_, bf16[128,512]{1,0:T(8,128)(2,1)S(1)} %collective-permute-done.25.refs_2_, bf16[256,512]{1,0:T(8,128)(2,1)S(1)} %collective-permute-done.26.refs_3_), custom_call_target="tpu_custom_call" | custom-call | tf_op jit(solution)/shard_map/pallas_call | solution.py:263
  (52 shorter events, 14.1 us)
Async XLA Ops:
  0.0 69.5 %copy-start.3 = (f32[2]{0:T(128)S(1)}, f32[2]{0:T(128)}, u32[]{:S(2)}) copy-start(f32[2]{0:T(128)} %rate.3) | copy-start | bytes 28
  0.0 24.1 %collective-permute-start.1 = (bf16[128,2048]{1,0:T(8,128)(2,1)}, bf16[128,2048]{1,0:T(8,128)(2,1)S(1)}, u32[]{:S(2)}, u32[]{:S(2)}) collective-permute-start(bf16[128,2048]{1,0:T(8,128)(2,1)} %refs_0_.1), channel_id=1, source_target_pairs={{0,8},{4,12},{8,0},{12,4},{16,24},{20,28},{24,16},{28,20},{1,9},{5... | collective-permute-start | bytes 1572872 | tf_op jit(solution)/shard_map/ppermute | solution.py:25
  3.0 21.1 %collective-permute-start = (bf16[128,2048]{1,0:T(8,128)(2,1)}, bf16[128,2048]{1,0:T(8,128)(2,1)S(1)}, u32[]{:S(2)}, u32[]{:S(2)}) collective-permute-start(bf16[128,2048]{1,0:T(8,128)(2,1)} %refs_0_.1), channel_id=1, source_target_pairs={{0,4},{4,0},{8,12},{12,8},{16,20},{20,16},{24,28},{28,24},{1,5},{5... | collective-permute-start | bytes 1572872 | tf_op jit(solution)/shard_map/ppermute | solution.py:25
  5.6 21.2 %collective-permute-start.5 = (bf16[64,2048]{1,0:T(8,128)(2,1)S(1)}, bf16[64,2048]{1,0:T(8,128)(2,1)S(1)}, u32[]{:S(2)}, u32[]{:S(2)}) collective-permute-start(bf16[64,2048]{1,0:T(8,128)(2,1)S(1)} %get-tuple-element.82), channel_id=1, source_target_pairs={{0,16},{4,20},{8,24},{12,28},{16,0},{20,4},{24,8},{28,12},{1,17},{... | collective-permute-start | bytes 786440 | tf_op jit(solution)/shard_map/ppermute | solution.py:25
  8.3 22.8 %collective-permute-start.6 = (bf16[64,2048]{1,0:T(8,128)(2,1)S(1)}, bf16[64,2048]{1,0:T(8,128)(2,1)S(1)}, u32[]{:S(2)}, u32[]{:S(2)}) collective-permute-start(bf16[64,2048]{1,0:T(8,128)(2,1)S(1)} %get-tuple-element.81), channel_id=1, source_target_pairs={{0,16},{4,20},{8,24},{12,28},{16,0},{20,4},{24,8},{28,12},{1,17},{... | collective-permute-start | bytes 786440 | tf_op jit(solution)/shard_map/ppermute | solution.py:25
  10.0 1.0 copy-start.1
  11.0 0.9 copy-start.2
  12.6 5.5 %collective-permute-start.2 = (bf16[272,128]{1,0:T(8,128)(2,1)S(1)}, bf16[272,128]{1,0:T(8,128)(2,1)S(1)}, u32[]{:S(2)}, u32[]{:S(2)}) collective-permute-start(bf16[272,128]{1,0:T(8,128)(2,1)S(1)} %get-tuple-element.43), channel_id=1, source_target_pairs={{0,4},{4,0},{8,12},{12,8},{16,20},{20,16},{24,28},{28,24},{1,5},{5... | collective-permute-start | bytes 208904 | tf_op jit(solution)/shard_map/ppermute | solution.py:25
  24.1 24.8 %collective-permute-start.3 = (bf16[128,2048]{1,0:T(8,128)(2,1)S(1)}, bf16[128,2048]{1,0:T(8,128)(2,1)S(1)}, u32[]{:S(2)}, u32[]{:S(2)}) collective-permute-start(bf16[128,2048]{1,0:T(8,128)(2,1)S(1)} %collective-permute-done.1.refs_2_), channel_id=1, source_target_pairs={{0,4},{4,0},{8,12},{12,8},{16,20},{20,16},{24,28},{28,24},{1,5},{5... | collective-permute-start | bytes 1572872 | tf_op jit(solution)/shard_map/ppermute | solution.py:25
  26.8 9.9 %collective-permute-start.8 = (bf16[64,2048]{1,0:T(8,128)(2,1)S(1)}, bf16[64,2048]{1,0:T(8,128)(2,1)S(1)}, u32[]{:S(2)}, u32[]{:S(2)}) collective-permute-start(bf16[64,2048]{1,0:T(8,128)(2,1)S(1)} %collective-permute-done.5.refs_4_), channel_id=1, source_target_pairs={{0,8},{4,12},{8,0},{12,4},{16,24},{20,28},{24,16},{28,20},{1,9},{5... | collective-permute-start | bytes 786440 | tf_op jit(solution)/shard_map/ppermute | solution.py:25
  26.8 18.4 %collective-permute-start.7 = (bf16[64,2048]{1,0:T(8,128)(2,1)S(1)}, bf16[64,2048]{1,0:T(8,128)(2,1)S(1)}, u32[]{:S(2)}, u32[]{:S(2)}) collective-permute-start(bf16[64,2048]{1,0:T(8,128)(2,1)S(1)} %collective-permute-done.5.refs_4_), channel_id=1, source_target_pairs={{0,4},{4,0},{8,12},{12,8},{16,20},{20,16},{24,28},{28,24},{1,5},{5... | collective-permute-start | bytes 786440 | tf_op jit(solution)/shard_map/ppermute | solution.py:25
  31.1 15.7 %collective-permute-start.11 = (bf16[64,2048]{1,0:T(8,128)(2,1)S(1)}, bf16[64,2048]{1,0:T(8,128)(2,1)S(1)}, u32[]{:S(2)}, u32[]{:S(2)}) collective-permute-start(bf16[64,2048]{1,0:T(8,128)(2,1)S(1)} %collective-permute-done.6.refs_5_), channel_id=1, source_target_pairs={{0,8},{4,12},{8,0},{12,4},{16,24},{20,28},{24,16},{28,20},{1,9},{5... | collective-permute-start | bytes 786440 | tf_op jit(solution)/shard_map/ppermute | solution.py:25
  31.1 1.3 %collective-permute-start.13 = (bf16[64,512]{1,0:T(8,128)(2,1)S(1)}, bf16[64,512]{1,0:T(8,128)(2,1)S(1)}, u32[]{:S(2)}, u32[]{:S(2)}) collective-permute-start(bf16[64,512]{1,0:T(8,128)(2,1)S(1)} %get-tuple-element.56), channel_id=1, source_target_pairs={{0,1},{1,0},{2,3},{3,2},{4,5},{5,4},{6,7},{7,6},{8,9},{9,8},{10,11... | collective-permute-start | bytes 196616 | tf_op jit(solution)/shard_map/ppermute | solution.py:25
  32.3 14.4 %collective-permute-start.4 = (bf16[144,256]{1,0:T(8,128)(2,1)S(1)}, bf16[144,256]{1,0:T(8,128)(2,1)S(1)}, u32[]{:S(2)}, u32[]{:S(2)}) collective-permute-start(bf16[144,256]{1,0:T(8,128)(2,1)S(1)} %get-tuple-element.49), channel_id=1, source_target_pairs={{0,8},{4,12},{8,0},{12,4},{16,24},{20,28},{24,16},{28,20},{1,9},{5... | collective-permute-start | bytes 221192 | tf_op jit(solution)/shard_map/ppermute | solution.py:25
  36.7 15.8 %collective-permute-start.10 = (bf16[64,2048]{1,0:T(8,128)(2,1)S(1)}, bf16[64,2048]{1,0:T(8,128)(2,1)S(1)}, u32[]{:S(2)}, u32[]{:S(2)}) collective-permute-start(bf16[64,2048]{1,0:T(8,128)(2,1)S(1)} %collective-permute-done.6.refs_5_), channel_id=1, source_target_pairs={{0,4},{4,0},{8,12},{12,8},{16,20},{20,16},{24,28},{28,24},{1,5},{5... | collective-permute-start | bytes 786440 | tf_op jit(solution)/shard_map/ppermute | solution.py:25
  45.3 7.2 %collective-permute-start.14 = (bf16[128,512]{1,0:T(8,128)(2,1)S(1)}, bf16[128,512]{1,0:T(8,128)(2,1)S(1)}, u32[]{:S(2)}, u32[]{:S(2)}) collective-permute-start(bf16[128,512]{1,0:T(8,128)(2,1)S(1)} %pad_maximum_fusion.1), channel_id=1, source_target_pairs={{0,2},{1,3},{2,0},{3,1},{4,6},{5,7},{6,4},{7,5},{8,10},{9,11},{10,... | collective-permute-start | bytes 393224 | tf_op jit(solution)/shard_map/ppermute | solution.py:25
  46.8 6.4 %collective-permute-start.9 = (bf16[64,2048]{1,0:T(8,128)(2,1)S(1)}, bf16[64,2048]{1,0:T(8,128)(2,1)S(1)}, u32[]{:S(2)}, u32[]{:S(2)}) collective-permute-start(bf16[64,2048]{1,0:T(8,128)(2,1)S(1)} %collective-permute-done.7.refs_6_), channel_id=1, source_target_pairs={{0,8},{4,12},{8,0},{12,4},{16,24},{20,28},{24,16},{28,20},{1,9},{5... | collective-permute-start | bytes 786440 | tf_op jit(solution)/shard_map/ppermute | solution.py:25
  46.8 8.7 %collective-permute-start.12 = (bf16[64,2048]{1,0:T(8,128)(2,1)S(1)}, bf16[64,2048]{1,0:T(8,128)(2,1)S(1)}, u32[]{:S(2)}, u32[]{:S(2)}) collective-permute-start(bf16[64,2048]{1,0:T(8,128)(2,1)S(1)} %collective-permute-done.11.refs_9_), channel_id=1, source_target_pairs={{0,4},{4,0},{8,12},{12,8},{16,20},{20,16},{24,28},{28,24},{1,5},{5... | collective-permute-start | bytes 786440 | tf_op jit(solution)/shard_map/ppermute | solution.py:25
  49.5 5.5 %collective-permute-start.15 = (bf16[80,512]{1,0:T(8,128)(2,1)S(1)}, bf16[80,512]{1,0:T(8,128)(2,1)S(1)}, u32[]{:S(2)}, u32[]{:S(2)}) collective-permute-start(bf16[80,512]{1,0:T(8,128)(2,1)S(1)} %get-tuple-element.62), channel_id=1, source_target_pairs={{0,16},{4,20},{8,24},{12,28},{16,0},{20,4},{24,8},{28,12},{1,17},{... | collective-permute-start | bytes 245768 | tf_op jit(solution)/shard_map/ppermute | solution.py:25
  55.5 1.0 copy-start
  59.4 1.6 %collective-permute-start.16 = (bf16[128,1024]{1,0:T(8,128)(2,1)S(1)}, bf16[128,1024]{1,0:T(8,128)(2,1)S(1)}, u32[]{:S(2)}, u32[]{:S(2)}) collective-permute-start(bf16[128,1024]{1,0:T(8,128)(2,1)S(1)} %get-tuple-element.67), channel_id=1, source_target_pairs={{0,1},{1,0},{2,3},{3,2},{4,5},{5,4},{6,7},{7,6},{8,9},{9,8},{10,11... | collective-permute-start | bytes 786440 | tf_op jit(solution)/shard_map/ppermute | solution.py:25
  61.1 8.4 %collective-permute-start.17 = (bf16[128,1024]{1,0:T(8,128)(2,1)S(1)}, bf16[128,1024]{1,0:T(8,128)(2,1)S(1)}, u32[]{:S(2)}, u32[]{:S(2)}) collective-permute-start(bf16[128,1024]{1,0:T(8,128)(2,1)S(1)} %get-tuple-element.69), channel_id=1, source_target_pairs={{0,2},{1,3},{2,0},{3,1},{4,6},{5,7},{6,4},{7,5},{8,10},{9,11},{10,... | collective-permute-start | bytes 786440 | tf_op jit(solution)/shard_map/ppermute | solution.py:25
  70.2 1.6 %collective-permute-start.18 = (bf16[128,1024]{1,0:T(8,128)(2,1)S(1)}, bf16[128,1024]{1,0:T(8,128)(2,1)S(1)}, u32[]{:S(2)}, u32[]{:S(2)}) collective-permute-start(bf16[128,1024]{1,0:T(8,128)(2,1)S(1)} %shard_map.70.mine), channel_id=1, source_target_pairs={{0,1},{1,0},{2,3},{3,2},{4,5},{5,4},{6,7},{7,6},{8,9},{9,8},{10,11... | collective-permute-start | bytes 786440 | tf_op jit(solution)/shard_map/ppermute | solution.py:25
  74.5 1.6 %collective-permute-start.19 = (bf16[128,1024]{1,0:T(8,128)(2,1)S(1)}, bf16[128,1024]{1,0:T(8,128)(2,1)S(1)}, u32[]{:S(2)}, u32[]{:S(2)}) collective-permute-start(bf16[128,1024]{1,0:T(8,128)(2,1)S(1)} %get-tuple-element.71), channel_id=1, source_target_pairs={{0,1},{1,0},{2,3},{3,2},{4,5},{5,4},{6,7},{7,6},{8,9},{9,8},{10,11... | collective-permute-start | bytes 786440 | tf_op jit(solution)/shard_map/ppermute | solution.py:25
  76.2 8.4 %collective-permute-start.20 = (bf16[128,1024]{1,0:T(8,128)(2,1)S(1)}, bf16[128,1024]{1,0:T(8,128)(2,1)S(1)}, u32[]{:S(2)}, u32[]{:S(2)}) collective-permute-start(bf16[128,1024]{1,0:T(8,128)(2,1)S(1)} %get-tuple-element.73), channel_id=1, source_target_pairs={{0,2},{1,3},{2,0},{3,1},{4,6},{5,7},{6,4},{7,5},{8,10},{9,11},{10,... | collective-permute-start | bytes 786440 | tf_op jit(solution)/shard_map/ppermute | solution.py:25
  85.2 1.6 %collective-permute-start.21 = (bf16[128,1024]{1,0:T(8,128)(2,1)S(1)}, bf16[128,1024]{1,0:T(8,128)(2,1)S(1)}, u32[]{:S(2)}, u32[]{:S(2)}) collective-permute-start(bf16[128,1024]{1,0:T(8,128)(2,1)S(1)} %get-tuple-element.75.mine), channel_id=1, source_target_pairs={{0,1},{1,0},{2,3},{3,2},{4,5},{5,4},{6,7},{7,6},{8,9},{9,8},{10,11... | collective-permute-start | bytes 786440 | tf_op jit(solution)/shard_map/ppermute | solution.py:25
  89.7 1.4 %collective-permute-start.22 = (bf16[64,1024]{1,0:T(8,128)(2,1)S(1)}, bf16[64,1024]{1,0:T(8,128)(2,1)S(1)}, u32[]{:S(2)}, u32[]{:S(2)}) collective-permute-start(bf16[64,1024]{1,0:T(8,128)(2,1)S(1)} %get-tuple-element.78), channel_id=1, source_target_pairs={{0,1},{1,0},{2,3},{3,2},{4,5},{5,4},{6,7},{7,6},{8,9},{9,8},{10,11... | collective-permute-start | bytes 393224 | tf_op jit(solution)/shard_map/ppermute | solution.py:25
  91.7 4.3 %collective-permute-start.23 = (bf16[64,512]{1,0:T(8,128)(2,1)S(1)}, bf16[64,512]{1,0:T(8,128)(2,1)S(1)}, u32[]{:S(2)}, u32[]{:S(2)}) collective-permute-start(bf16[64,512]{1,0:T(8,128)(2,1)S(1)} %get-tuple-element.80), channel_id=1, source_target_pairs={{0,2},{1,3},{2,0},{3,1},{4,6},{5,7},{6,4},{7,5},{8,10},{9,11},{10,... | collective-permute-start | bytes 196616 | tf_op jit(solution)/shard_map/ppermute | solution.py:25
  96.0 5.3 %collective-permute-start.24 = (bf16[64,512]{1,0:T(8,128)(2,1)S(1)}, bf16[64,512]{1,0:T(8,128)(2,1)S(1)}, u32[]{:S(2)}, u32[]{:S(2)}) collective-permute-start(bf16[64,512]{1,0:T(8,128)(2,1)S(1)} %shard_map.76.refs_0_), channel_id=1, source_target_pairs={{0,16},{4,20},{8,24},{12,28},{16,0},{20,4},{24,8},{28,12},{1,17},{... | collective-permute-start | bytes 196616 | tf_op jit(solution)/shard_map/ppermute | solution.py:25
  101.4 5.0 %collective-permute-start.25 = (bf16[128,512]{1,0:T(8,128)(2,1)S(1)}, bf16[128,512]{1,0:T(8,128)(2,1)S(1)}, u32[]{:S(2)}, u32[]{:S(2)}) collective-permute-start(bf16[128,512]{1,0:T(8,128)(2,1)S(1)} %pad_maximum_fusion.2), channel_id=1, source_target_pairs={{0,8},{4,12},{8,0},{12,4},{16,24},{20,28},{24,16},{28,20},{1,9},{5... | collective-permute-start | bytes 393224 | tf_op jit(solution)/shard_map/ppermute | solution.py:25
  106.4 6.4 %collective-permute-start.26 = (bf16[256,512]{1,0:T(8,128)(2,1)S(1)}, bf16[256,512]{1,0:T(8,128)(2,1)S(1)}, u32[]{:S(2)}, u32[]{:S(2)}) collective-permute-start(bf16[256,512]{1,0:T(8,128)(2,1)S(1)} %pad_maximum_fusion), channel_id=1, source_target_pairs={{0,4},{4,0},{8,12},{12,8},{16,20},{20,16},{24,28},{28,24},{1,5},{5... | collective-permute-start | bytes 786440 | tf_op jit(solution)/shard_map/ppermute | solution.py:25

commit v3 on v2

--- a/solution.py
+++ b/solution.py
@@ -41,17 +41,6 @@
 def onehots(labels, copies):
     copy = labels[1:2, :].astype(F32)
     return [(copy == float(c)).astype(F32) for c in range(copies)]
-
-
-def over_tiles(count, body):
-    if count == 1:
-        body(0)
-    else:
-        lax.fori_loop(0, count, lambda tile, none: body(tile), None)
-
-
-def tile_at(tile, size):
-    return pl.ds(tile * size if isinstance(tile, int) else pl.multiple_of(tile * size, size), size)
 
 
 def times_tokens(core, part, pairs, mine, other, held, rows):
@@ -69,25 +58,29 @@
     return total
 
 
-def contract(core, part, pairs, delta, held, rows, send, keep, sums):
-    only = rows.size == held.shape[0]
+def contract(core, part, pairs, delta, held, rows, send, keep, before):
     for j in range(pairs):
         place = pl.ds(j * part, part)
-        for out, side in ((send if only else sums, 1 - core), (keep, core)):
+        for k, (out, side) in enumerate(((send, 1 - core), (keep, core))):
             columns = pl.ds(pl.multiple_of((2 * j + side) * part, part), part)
             term = jnp.dot(delta, held[rows, columns], preferred_element_type=F32)
-            out[:, place] = (term if only else out[:, place] + term).astype(out.dtype)
-
-
-def each_tile(held, send, keep, sums, body):
-    size = min(held.shape[0], 1024)
-    count = held.shape[0] // size
-    if count > 1:
-        keep[...] = jnp.zeros_like(keep)
-        sums[...] = jnp.zeros_like(sums)
-    over_tiles(count, lambda tile: body(tile_at(tile, size)))
-    if count > 1:
-        send[...] = sums[...].astype(BF)
+            if before is not None:
+                term = before[k][:, place] + term
+            out[:, place] = term.astype(out.dtype)
+
+
+def in_tiles(held, sums, keep, body):
+    tile = min(held.shape[0], 1024)
+    if held.shape[0] == tile:
+        body(pl.ds(0, tile), None)
+        return
+    sums[...] = jnp.zeros_like(sums)
+    keep[...] = jnp.zeros_like(keep)
+
+    def step(i, none):
+        body(pl.ds(pl.multiple_of(i * tile, tile), tile), (sums, keep))
+
+    lax.fori_loop(0, held.shape[0] // tile, step, None)
 
 
 def of_copy(value, hots):
@@ -100,7 +93,7 @@
     return jnp.concatenate([delta * hot for hot in hots], 0).astype(BF)
 
 
-def prepare_kernel(wide, side_of, scalars, upstream, value_weight, weight, up, labels, sent, turned):
+def prepare_kernel(wide, side_of, stride, scalars, upstream, value_weight, weight, up, labels, sent, turned):
     me = scalars[0]
     group = 128 // wide
     columns = pl.ds(pl.multiple_of((me // group) * 128, 128), 128)
@@ -111,39 +104,47 @@
     row = lax.broadcasted_iota(jnp.int32, labels.shape, 0)
     both = jnp.where(row == 0, scalars[2], jnp.where(row == 1, scalars[3], 0))
     labels[...] = both.astype(F32).astype(BF)
-    every_second(up, 1 - side_of(me), wide, sent)
+    every_second(up, 1 - side_of(me), stride, wide, sent)
     sent[pl.ds(up.shape[0] // 2, 16), :] = labels[...]
 
 
-def every_second(source, side, wide, target, columns=slice(None)):
+def every_second(source, side, stride, wide, target, columns=slice(None)):
     for k in range(source.shape[0] // wide // 2):
-        block = pl.ds(pl.multiple_of((2 * k + side) * wide, wide), wide)
+        place = (2 * (k // stride) + side) * stride + k % stride
+        block = pl.ds(pl.multiple_of(place * wide, wide), wide)
         target[pl.ds(k * wide, wide), columns] = source[block, :]
 
 
-def join_kernel(wide, side_of, next_side, scalars, up, labels, came, new_up, new_labels, *sent):
+def join_kernel(wide, side_of, stride, next_side, next_stride, scalars, up, labels, came, new_up, new_labels, *sent):
     me = scalars[0]
     half, long = up.shape[0] // 2, up.shape[1]
-    every_second(up, side_of(me), wide, new_up, pl.ds(0, long))
+    every_second(up, side_of(me), stride, wide, new_up, pl.ds(0, long))
     new_up[:, pl.ds(long, long)] = came[pl.ds(0, half), :]
     new_labels[:, pl.ds(0, long)] = labels[...]
     new_labels[:, pl.ds(long, long)] = came[pl.ds(half, 16), :]
     if sent:
-        every_second(new_up, 1 - next_side(me), wide, sent[0])
+        every_second(new_up, 1 - next_side(me), next_stride, wide, sent[0])
         sent[0][pl.ds(half // 2, 16), :] = new_labels[...]
 
 
-def first_kernel(sizes, scalars, *refs):
-    part, pairs, copies, length, count = sizes
-    pieces, (weight, up, labels, held, primal_out, send, keep, sums) = refs[:count], refs[count:]
+def first_kernel(sizes, places, last, scalars, *refs):
+    part, pairs, copies, length = sizes
+    refs, outs = refs[:-6], refs[-6:]
+    before, refs = (refs[-2:], refs[:-2]) if last else (None, refs)
+    pieces, (all_up, all_labels, weight) = refs[:-3], refs[-3:]
+    held, up, labels, primal_out, sums, keep = outs
     quarter = scalars[1]
+    wide = up.shape[0]
     row = 0
     for piece in pieces:
         held[pl.ds(row, piece.shape[0]), :] = piece[...]
         row += piece.shape[0]
-    wide = up.shape[0]
-
-    def body(rows):
+    rows = held.shape[0] // len(places)
+    for i, place in enumerate(places):
+        up[:, pl.ds(i * rows, rows)] = all_up[:, pl.ds(place * rows, rows)]
+        labels[:, pl.ds(i * rows, rows)] = all_labels[:, pl.ds(place * rows, rows)]
+
+    def body(rows, prior):
         primal = None
         for i in range(2 * pairs):
             columns = pl.ds(pl.multiple_of((quarter ^ i) * part, part), part)
@@ -158,30 +159,45 @@
         hots = onehots(labels[:, rows], copies)
         forget = labels[0:1, rows].astype(F32)
         delta = (forget * up[:, rows].astype(F32) * first_slope(primal) / length).astype(BF)
-        contract(quarter % 2, part, pairs, by_copy(delta, hots), held, rows, send, keep, sums)
-
-    each_tile(held, send, keep, sums, body)
-
-
-def second_kernel(sizes, scalars, held, mine, other, up, labels, send, keep, sums):
+        contract(quarter % 2, part, pairs, by_copy(delta, hots), held, rows, sums, keep, prior)
+
+    if last:
+        body(pl.ds(0, held.shape[0]), before)
+    else:
+        in_tiles(held, sums, keep, body)
+
+
+def in_parts(parts, send, keep, sums, body):
+    early, late = parts
+    in_tiles(
+        early[0], sums, keep, lambda rows, before: body(early, rows, sums, keep, before)
+    )
+    body(late, pl.ds(0, late[0].shape[0]), send, keep, (sums, keep))
+
+
+def second_kernel(sizes, scalars, *refs):
     part, pairs, copies, length = sizes
+    early, late, (mine, other, send, keep, sums) = refs[:3], refs[3:6], refs[6:]
     core = scalars[1] % 2
 
-    def body(rows):
+    def body(tokens, rows, send, keep, before):
+        held, up, labels = tokens
         hots = onehots(labels[:, rows], copies)
         altered = of_copy(times_tokens(core, part, pairs, mine, other, held, rows), hots)
         sign = 1.0 - 2.0 * labels[0:1, rows].astype(F32)
         delta = (sign * up[:, rows].astype(F32) * first_slope(altered) / length).astype(BF)
-        contract(core, part, pairs, by_copy(delta, hots), held, rows, send, keep, sums)
-
-    each_tile(held, send, keep, sums, body)
-
-
-def third_kernel(sizes, scalars, rate, held, mine, other, up, labels, primal, send, keep, sums):
+        contract(core, part, pairs, by_copy(delta, hots), held, rows, send, keep, before)
+
+    in_parts((early, late), send, keep, sums, body)
+
+
+def third_kernel(sizes, scalars, rate, *refs):
     part, pairs, copies, length = sizes
+    early, late, (mine, other, send, keep, sums) = refs[:4], refs[4:8], refs[8:]
     core = scalars[1] % 2
 
-    def body(rows):
+    def body(tokens, rows, send, keep, before):
+        held, up, labels, primal = tokens
         hots = onehots(labels[:, rows], copies)
         forward = of_copy(times_tokens(core, part, pairs, mine, other, held, rows), hots)
         forget = labels[0:1, rows].astype(F32)
@@ -189,9 +205,9 @@
         slope = second_slope(primal[:, rows])
         delta = (forget * up[:, rows].astype(F32) * slope * forward / length).astype(BF)
         delta = (own_rate * delta.astype(F32)).astype(BF)
-        contract(core, part, pairs, delta, held, rows, send, keep, sums)
-
-    each_tile(held, send, keep, sums, body)
+        contract(core, part, pairs, delta, held, rows, send, keep, before)
+
+    in_parts((early, late), send, keep, sums, body)
 
 
 def add_kernel(mine, came, total, sent):
@@ -279,78 +295,84 @@
     pairs = fsdp // 2
     copies = adv_rate.shape[0]
     seq_length = rows * fsdp
-    held_rows = rows * dp
     me = lax.axis_index("dp").astype(jnp.int32)
     quarter = lax.axis_index("fsdp").astype(jnp.int32)
     scalars = jnp.stack([me, quarter, forget_label[0], copy_index[0]])
     dp_bits = bits_of(dp)[::-1]
     far_bits = bits_of(fsdp)[1:]
     up_bits = dp_bits[::-1]
+    up_bits = up_bits[1:2] + up_bits[:1] + up_bits[2:]
+    strides = [2 ** sum(low < bit for low in up_bits[i:]) for i, bit in enumerate(up_bits)]
 
     def side_of(bit):
         return lambda me: (me // bit) % 2
 
     weight, up, labels, sent = run(
-        functools.partial(prepare_kernel, wide, side_of(up_bits[0])),
+        functools.partial(prepare_kernel, wide, side_of(up_bits[0]), strides[0]),
         [scalars],
         [upstream, value_weight],
         [((wide, part), BF), ((outs, rows), BF), ((16, rows), BF), ((outs // 2 + 16, rows), BF)],
         [((128, part), F32)],
     )
 
-    top_bit = dp_bits[0]
-    tops = [top_bit]
-    for bit in dp_bits[1:]:
-        tops.append(tops[-1] | bit)
     half_rows = rows // 2
     first = {0: tokens[:half_rows]}
     second = {0: tokens[half_rows:]}
-    whole = {0: tokens}
-    late = {}
-    for step, (top, up_bit) in enumerate(zip(tops, up_bits), 1):
-        wholes, firsts = {}, {}
-        new_late = {}
-        for r in range(1, dp):
-            if bin(r).count("1") != step:
-                continue
+    near = [swap(tokens, "dp", 1)]
+    whole = {1: near[0]}
+
+    def send(value, bit, *others):
+        if bit == 1:
+            others += (near[max(len(near) - 2, 0)],)
+        if others:
+            value = after(value, *others)
+        came = swap(value, "dp", bit)
+        if bit == 1:
+            near.append(came)
+        return came
+
+    ties = ()
+    top_bit = dp_bits[0]
+    for step, up_bit in enumerate(up_bits, 1):
+        if step == len(dp_bits) and step > 1:
+            sent = after(sent, second[top_bit])
+        came_up = swap(sent, "dp", up_bit)
+        ready = [r for r in range(2, dp) if bin(r).count("1") == step]
+        firsts, seconds = {}, {}
+        for r in ready:
             bit = r & -r
-            if r < top_bit:
-                wholes[r] = swap(whole[r ^ bit], "dp", bit)
-                continue
             way = 2 * bit if r == dp - 1 and dp > 2 else bit
-            firsts[r] = swap(first[r ^ way], "dp", way)
-            if r != top:
-                new_late[r] = swap({**second, **late}[r ^ bit], "dp", bit)
-        came_up = swap(sent, "dp", up_bit)
-        wholes, came_up = lax.optimization_barrier((wholes, came_up))
-        firsts, late = lax.optimization_barrier((firsts, late))
-        whole.update(wholes)
+            firsts[r] = send(first[r ^ way], way, *(ties if way == 1 else ()))
+        for r in ready:
+            bit = r & -r
+            others = (firsts[r],) if step == 1 else (came_up,) if step == 2 and bit == 1 else ()
+            seconds[r] = send(second[r ^ bit], bit, *others)
         first.update(firsts)
-        second.update(late)
-        late = new_late
-        second[top] = swap(second[top ^ dp_bits[step - 1]], "dp", dp_bits[step - 1])
+        second.update(seconds)
+        ties = (came_up,) if step == 1 else ()
         high, long = up.shape[0] // 2, 2 * up.shape[1]
         shapes = [((high, long), BF), ((16, long), BF)]
         if step < len(dp_bits):
             shapes.append(((high // 2 + 16, long), BF))
-        following = side_of(up_bits[step]) if step < len(dp_bits) else None
+        following = (side_of(up_bits[step]), strides[step]) if step < len(dp_bits) else (None, None)
         joined = run(
-            functools.partial(join_kernel, wide, side_of(up_bit), following),
+            functools.partial(join_kernel, wide, side_of(up_bit), strides[step - 1], *following),
             [scalars],
             [up, labels, came_up],
             shapes,
         )
         up, labels = joined[:2]
         sent = joined[-1]
-    second.update(late)
     order = [0]
     for bit in up_bits:
         order = order + [r ^ bit for r in order]
-    flat = []
-    for r in order:
-        flat += [whole[r]] if r in whole else [first[r], second[r]]
-
-    weight = after(weight, first[top_bit])
+    late = [r for r in range(dp) if r & dp_bits[0] and r & 1]
+    early = [r for r in range(dp) if r not in late]
+
+    def pieces_of(blocks):
+        return [x for r in blocks for x in ([whole[r]] if r in whole else [first[r], second[r]])]
+
+    weight = after(weight, first[dp_bits[0]])
     for bit in bits_of(fsdp):
         weight = jnp.concatenate([weight, swap(weight, "fsdp", bit)])
 
@@ -364,13 +386,21 @@
 
     sizes = (part, pairs, copies, seq_length)
     stacked = (copies * wide, features // 2)
-    held, primal, send, keep = run(
-        functools.partial(first_kernel, sizes + (len(flat),)),
-        [scalars],
-        flat + [weight, up, labels],
-        [((held_rows, features), BF), ((wide, held_rows), F32), (stacked, BF), (stacked, F32)],
-        [(stacked, F32)],
-    )
+
+    def put_together(blocks, before):
+        count = len(blocks) * rows
+        shapes = [((count, features), BF), ((wide, count), BF), ((16, count), BF), ((wide, count), F32)]
+        shapes += [(stacked, BF if before else F32), (stacked, F32)]
+        places = [order.index(r) for r in blocks]
+        return run(
+            functools.partial(first_kernel, sizes, places, bool(before)),
+            [scalars],
+            pieces_of(blocks) + [up, labels, weight] + before,
+            shapes,
+        )
+
+    *tokens_early, primal_early, sums, keep = put_together(early, [])
+    *tokens_late, primal_late, send, keep = put_together(late, [sums, keep])
     (attacked,) = run(
         functools.partial(attack_kernel, copies),
         [scalars, adv_rate],
@@ -380,7 +410,7 @@
     send, keep = run(
         functools.partial(second_kernel, sizes),
         [scalars],
-        [held, attacked, swap(attacked, "fsdp", 1), up, labels],
+        [*tokens_early, *tokens_late, attacked, swap(attacked, "fsdp", 1)],
         [(stacked, BF), (stacked, F32)],
         [(stacked, F32)],
     )
@@ -393,7 +423,7 @@
     send, keep = run(
         functools.partial(third_kernel, sizes),
         [scalars, adv_rate],
-        [held, tangent, swap(tangent, "fsdp", 1), up, labels, primal],
+        [*tokens_early, primal_early, *tokens_late, primal_late, tangent, swap(tangent, "fsdp", 1)],
         [((wide, features // 2), BF), ((wide, features // 2), F32)],
         [((wide, features // 2), F32)],
     )
@@ -415,21 +445,16 @@
     )
     blocks = [result]
     came_order = [0]
-    for bit in dp_bits:
-        came_order = came_order + [r ^ bit for r in came_order]
-        sent = blocks[0] if len(blocks) == 1 else jnp.concatenate(blocks)
-        blocks.append(swap(sent, "dp", bit))
+    for r in range(dp - 1, 0, -1):
+        came_order.append(r)
+        blocks.append(swap(result, "dp", r))
     if 2 * wide == 128:
         (placed,) = run(
             functools.partial(place_kernel, came_order), [scalars], blocks, [((part, outs), F32)]
         )
         return placed
-    result = jnp.concatenate(blocks).reshape([2] * len(dp_bits) + [wide, part])
-    for place, bit in enumerate(dp_bits[::-1]):
-        side = (me // bit) % 2
-        result = jnp.where(side == 1, jnp.flip(result, place), result)
-    axes = tuple(range(len(dp_bits)))
-    result = result.transpose(axes[::-1] + (len(axes), len(axes) + 1))
+    result = jnp.concatenate(blocks).reshape(dp, wide, part)
+    result = result[jnp.argsort(me ^ jnp.array(came_order))]
     return result.reshape(outs, part).T.astype(F32)
 
 

time: 115 us -> 112 us (0.974)
  waiting for transfers between devices: 65 us -> 52.4 us
  starting transfers between devices: 29.3 us -> 38.2 us
  Pallas kernels: 14.6 us -> 16.6 us
    ppermute x27 -> x33, waiting for transfers between devices: 65 us -> 52.4 us  [swap(): lax.ppermute(value, axis, [(i, i ^ bit) for i in range(lax.axis_size(axis...]
    ppermute x27 -> x33, starting transfers between devices: 29.3 us -> 38.2 us  [swap(): lax.ppermute(value, axis, [(i, i ^ bit) for i in range(lax.axis_size(axis...]
    pallas_call x14 -> x15, Pallas kernels: 14.6 us -> 16.6 us  [run(): pl.pallas_call(kernel, out_shape=[jax.ShapeDtypeStruct(s, t) for s, t in...]
    unnamed x10 -> x8, local copies, waits for them, and re-layouts: 3 us -> 1.96 us
  transfers between devices with their start and end apart: 27 -> 33, of which waited for: 19 -> 19; matrix products, arithmetic and copies ran while one was open for 1% -> 1% of each run, Pallas kernels for 2% -> 5%
where the time goes in v3:
time: 112 us
  waiting for transfers between devices  52.4 us (47%)
  starting transfers between devices  38.2 us (34%)
  Pallas kernels  16.6 us (15%)
  local copies, waits for them, and re-layouts  3.04 us (3%)
  between operations  1.49 us (1%)
    ppermute x33, waiting for transfers between devices, swap(): lax.ppermute(value, axis, [(i, i ^ bit) for i in range(lax.axis_size(axis...  52.4 us
    ppermute x33, starting transfers between devices, swap(): lax.ppermute(value, axis, [(i, i ^ bit) for i in range(lax.axis_size(axis...  38.2 us
    pallas_call x15, Pallas kernels, run(): pl.pallas_call(kernel, out_shape=[jax.ShapeDtypeStruct(s, t) for s, t in...  16.6 us
  transfers between devices with their start and end apart: 33, of which 19 were waited for; matrix products, arithmetic and copies ran while one was open for 1% of the time, Pallas kernels for 5%

profile of v3, /device:TPU:0, one launch (start us, length us, event | category | flops | bytes accessed | tf_op | source)
XLA Modules:
  0.0 111.9 jit_solution(11795505291055384303)
XLA Ops:
  0.0 3.0 %collective-permute-start = (bf16[128,2048]{1,0:T(8,128)(2,1)}, bf16[128,2048]{1,0:T(8,128)(2,1)S(1)}, u32[]{:S(2)}, u32[]{:S(2)}) collective-permute-start(bf16[128,2048]{1,0:T(8,128)(2,1)} %param.6), channel_id=1, source_target_pairs={{0,4},{4,0},{8,12},{12,8},{16,20},{20,16},{24,28},{28,24},{1,5},{5... | collective-permute-start | bytes 1572872 | tf_op jit(solution)/shard_map/ppermute | solution.py:25
  4.0 2.7 %collective-permute-start.7 = (bf16[64,2048]{1,0:T(8,128)(2,1)S(1)}, bf16[64,2048]{1,0:T(8,128)(2,1)S(1)}, u32[]{:S(2)}, u32[]{:S(2)}) collective-permute-start(bf16[64,2048]{1,0:T(8,128)(2,1)S(1)} %get-tuple-element.96.refs_0_), channel_id=1, source_target_pairs={{0,16},{4,20},{8,24},{12,28},{16,0},{20,4},{24,8},{28,12},{1,17},{... | collective-permute-start | bytes 786440 | tf_op jit(solution)/shard_map/ppermute | solution.py:25
  6.7 1.6 %collective-permute-start.1 = (bf16[64,2048]{1,0:T(8,128)(2,1)S(1)}, bf16[64,2048]{1,0:T(8,128)(2,1)S(1)}, u32[]{:S(2)}, u32[]{:S(2)}) collective-permute-start(bf16[64,2048]{1,0:T(8,128)(2,1)S(1)} %get-tuple-element.96.refs_0_), channel_id=1, source_target_pairs={{0,8},{4,12},{8,0},{12,4},{16,24},{20,28},{24,16},{28,20},{1,9},{5... | collective-permute-start | bytes 786440 | tf_op jit(solution)/shard_map/ppermute | solution.py:25
  12.8 5.7 %collective-permute-done.7.refs_7_ = bf16[64,2048]{1,0:T(8,128)(2,1)S(1)} collective-permute-done((bf16[64,2048]{1,0:T(8,128)(2,1)S(1)}, bf16[64,2048]{1,0:T(8,128)(2,1)S(1)}, u32[]{:S(2)}, u32[]{:S(2)}) %collective-permute-start.7) | collective-permute-done | bytes 262176 | tf_op jit(solution)/shard_map/ppermute | solution.py:25
  19.4 3.1 %collective-permute-start.2 = (bf16[64,2048]{1,0:T(8,128)(2,1)S(1)}, bf16[64,2048]{1,0:T(8,128)(2,1)S(1)}, u32[]{:S(2)}, u32[]{:S(2)}) collective-permute-start(bf16[64,2048]{1,0:T(8,128)(2,1)S(1)} %get-tuple-element.57.refs_1_), channel_id=1, source_target_pairs={{0,8},{4,12},{8,0},{12,4},{16,24},{20,28},{24,16},{28,20},{1,9},{5... | collective-permute-start | bytes 786440 | tf_op jit(solution)/shard_map/ppermute | solution.py:25
  23.6 1.6 %collective-permute-start.5 = (bf16[144,256]{1,0:T(8,128)(2,1)S(1)}, bf16[144,256]{1,0:T(8,128)(2,1)S(1)}, u32[]{:S(2)}, u32[]{:S(2)}) collective-permute-start(bf16[144,256]{1,0:T(8,128)(2,1)S(1)} %get-tuple-element.55), channel_id=1, source_target_pairs={{0,4},{4,0},{8,12},{12,8},{16,20},{20,16},{24,28},{28,24},{1,5},{5... | collective-permute-start | bytes 221192 | tf_op jit(solution)/shard_map/ppermute | solution.py:25
  25.7 6.5 %collective-permute-done.8.refs_8_ = bf16[64,2048]{1,0:T(8,128)(2,1)S(1)} collective-permute-done((bf16[64,2048]{1,0:T(8,128)(2,1)S(1)}, bf16[64,2048]{1,0:T(8,128)(2,1)S(1)}, u32[]{:S(2)}, u32[]{:S(2)}) %collective-permute-start.8) | collective-permute-done | bytes 262176 | tf_op jit(solution)/shard_map/ppermute | solution.py:25
  35.5 1.6 %collective-permute-start.13 = (bf16[128,512]{1,0:T(8,128)(2,1)S(1)}, bf16[128,512]{1,0:T(8,128)(2,1)S(1)}, u32[]{:S(2)}, u32[]{:S(2)}) collective-permute-start(bf16[128,512]{1,0:T(8,128)(2,1)S(1)} %pad_maximum_fusion), channel_id=1, source_target_pairs={{0,2},{1,3},{2,0},{3,1},{4,6},{5,7},{6,4},{7,5},{8,10},{9,11},{10,... | collective-permute-start | bytes 393224 | tf_op jit(solution)/shard_map/ppermute | solution.py:25
  37.0 2.0 %collective-permute-done.14.refs_0_ = bf16[64,2048]{1,0:T(8,128)(2,1)S(1)} collective-permute-done((bf16[64,2048]{1,0:T(8,128)(2,1)S(1)}, bf16[64,2048]{1,0:T(8,128)(2,1)S(1)}, u32[]{:S(2)}, u32[]{:S(2)}) %collective-permute-start.14) | collective-permute-done | bytes 262176 | tf_op jit(solution)/shard_map/ppermute | solution.py:25
  39.5 1.9 %collective-permute-start.16 = (bf16[64,2048]{1,0:T(8,128)(2,1)S(1)}, bf16[64,2048]{1,0:T(8,128)(2,1)S(1)}, u32[]{:S(2)}, u32[]{:S(2)}) collective-permute-start(bf16[64,2048]{1,0:T(8,128)(2,1)S(1)} %collective-permute-done.14.refs_0_), channel_id=1, source_target_pairs={{0,8},{4,12},{8,0},{12,4},{16,24},{20,28},{24,16},{28,20},{1,9},{5... | collective-permute-start | bytes 786440 | tf_op jit(solution)/shard_map/ppermute | solution.py:25
  41.4 3.2 %collective-permute-done.6.refs_6_ = bf16[64,2048]{1,0:T(8,128)(2,1)S(1)} collective-permute-done((bf16[64,2048]{1,0:T(8,128)(2,1)S(1)}, bf16[64,2048]{1,0:T(8,128)(2,1)S(1)}, u32[]{:S(2)}, u32[]{:S(2)}) %collective-permute-start.6) | collective-permute-done | bytes 262176 | tf_op jit(solution)/shard_map/ppermute | solution.py:25
  45.2 5.4 %collective-permute-done.11.came = bf16[80,512]{1,0:T(8,128)(2,1)S(1)} collective-permute-done((bf16[80,512]{1,0:T(8,128)(2,1)S(1)}, bf16[80,512]{1,0:T(8,128)(2,1)S(1)}, u32[]{:S(2)}, u32[]{:S(2)}) %collective-permute-start.11) | collective-permute-done | bytes 81952 | tf_op jit(solution)/shard_map/ppermute | solution.py:25
  51.2 2.9 %shard_map.68 = (bf16[768,2048]{1,0:T(8,128)(2,1)S(1)}, bf16[64,768]{1,0:T(8,128)(2,1)S(1)}, bf16[16,768]{1,0:T(8,128)(2,1)S(1)}, f32[64,768]{1,0:T(8,128)S(1)},...) custom-call(s32[4]{0:T(128)S(1)} %pad_add_fusion.scalars, bf16[64,2048]{1,0:T(8,128)(2,1)S(1)} %get-tuple-element.96.refs_0_, ...), custom_call_target="tpu_custom_call" | custom-call | tf_op jit(solution)/shard_map/pallas_call | solution.py:279
  54.2 1.6 %shard_map.69 = (bf16[256,2048]{1,0:T(8,128)(2,1)S(1)}, bf16[64,256]{1,0:T(8,128)(2,1)S(1)}, bf16[16,256]{1,0:T(8,128)(2,1)S(1)}, f32[64,256]{1,0:T(8,128)S(1)},...) custom-call(s32[4]{0:T(128)S(1)} %pad_add_fusion.scalars, bf16[64,2048]{1,0:T(8,128)(2,1)S(1)} %collective-permute-done.14.refs_0_, ...), custom_call_target="tpu_custom_call" | custom-call | tf_op jit(solution)/shard_map/pallas_call | solution.py:279
  55.9 1.5 %collective-permute-done.18.came = bf16[128,1024]{1,0:T(8,128)(2,1)S(1)} collective-permute-done((bf16[128,1024]{1,0:T(8,128)(2,1)S(1)}, bf16[128,1024]{1,0:T(8,128)(2,1)S(1)}, u32[]{:S(2)}, u32[]{:S(2)}) %collective-permute-start.18) | collective-permute-done | bytes 262176 | tf_op jit(solution)/shard_map/ppermute | solution.py:25
  57.5 1.6 %collective-permute-start.19 = (bf16[128,1024]{1,0:T(8,128)(2,1)S(1)}, bf16[128,1024]{1,0:T(8,128)(2,1)S(1)}, u32[]{:S(2)}, u32[]{:S(2)}) collective-permute-start(bf16[128,1024]{1,0:T(8,128)(2,1)S(1)} %get-tuple-element.82), channel_id=1, source_target_pairs={{0,2},{1,3},{2,0},{3,1},{4,6},{5,7},{6,4},{7,5},{8,10},{9,11},{10,... | collective-permute-start | bytes 786440 | tf_op jit(solution)/shard_map/ppermute | solution.py:25
  59.0 6.9 %collective-permute-done.19.came = bf16[128,1024]{1,0:T(8,128)(2,1)S(1)} collective-permute-done((bf16[128,1024]{1,0:T(8,128)(2,1)S(1)}, bf16[128,1024]{1,0:T(8,128)(2,1)S(1)}, u32[]{:S(2)}, u32[]{:S(2)}) %collective-permute-start.19) | collective-permute-done | bytes 262176 | tf_op jit(solution)/shard_map/ppermute | solution.py:25
  66.6 1.5 %collective-permute-done.20.refs_7_ = bf16[128,1024]{1,0:T(8,128)(2,1)S(1)} collective-permute-done((bf16[128,1024]{1,0:T(8,128)(2,1)S(1)}, bf16[128,1024]{1,0:T(8,128)(2,1)S(1)}, u32[]{:S(2)}, u32[]{:S(2)}) %collective-permute-start.20) | collective-permute-done | bytes 262176 | tf_op jit(solution)/shard_map/ppermute | solution.py:25
  68.1 3.0 %shard_map.72 = (bf16[128,1024]{1,0:T(8,128)(2,1)S(1)}, f32[128,1024]{1,0:T(8,128)S(1)}) custom-call(s32[4]{0:T(128)S(1)} %pad_add_fusion.scalars, bf16[768,2048]{1,0:T(8,128)(2,1)S(1)} %get-tuple-element.68.refs_0_, bf16[64,768]{1,0:T(8,128)(2,1)S(1)} %get-tuple-element.69.refs_1_, bf16[16,768]{1,0:T(8,128)(2,1)S(1)} %get-tuple-element.70.refs_2_, ...), custom_call_target="tpu_custom_call" | custom-call | tf_op jit(solution)/shard_map/pallas_call | solution.py:279
  72.8 1.6 %collective-permute-start.22 = (bf16[128,1024]{1,0:T(8,128)(2,1)S(1)}, bf16[128,1024]{1,0:T(8,128)(2,1)S(1)}, u32[]{:S(2)}, u32[]{:S(2)}) collective-permute-start(bf16[128,1024]{1,0:T(8,128)(2,1)S(1)} %get-tuple-element.86), channel_id=1, source_target_pairs={{0,2},{1,3},{2,0},{3,1},{4,6},{5,7},{6,4},{7,5},{8,10},{9,11},{10,... | collective-permute-start | bytes 786440 | tf_op jit(solution)/shard_map/ppermute | solution.py:25
  74.3 6.9 %collective-permute-done.22.came = bf16[128,1024]{1,0:T(8,128)(2,1)S(1)} collective-permute-done((bf16[128,1024]{1,0:T(8,128)(2,1)S(1)}, bf16[128,1024]{1,0:T(8,128)(2,1)S(1)}, u32[]{:S(2)}, u32[]{:S(2)}) %collective-permute-start.22) | collective-permute-done | bytes 262176 | tf_op jit(solution)/shard_map/ppermute | solution.py:25
  81.9 1.5 %collective-permute-done.23.refs_9_ = bf16[128,1024]{1,0:T(8,128)(2,1)S(1)} collective-permute-done((bf16[128,1024]{1,0:T(8,128)(2,1)S(1)}, bf16[128,1024]{1,0:T(8,128)(2,1)S(1)}, u32[]{:S(2)}, u32[]{:S(2)}) %collective-permute-start.23) | collective-permute-done | bytes 262176 | tf_op jit(solution)/shard_map/ppermute | solution.py:25
  83.4 3.0 %shard_map.75 = (bf16[64,1024]{1,0:T(8,128)(2,1)S(1)}, f32[64,1024]{1,0:T(8,128)S(1)}) custom-call(s32[4]{0:T(128)S(1)} %pad_add_fusion.scalars, f32[2]{0:T(128)S(1)} %copy-done.2, bf16[768,2048]{1,0:T(8,128)(2,1)S(1)} %get-tuple-element.68.refs_0_, bf16[64,768]{1,0:T(8,128)(2,1)S(1)} %get-tuple-element.69.refs_1_, ...), custom_call_target="tpu_custom_call" | custom-call | tf_op jit(solution)/shard_map/pallas_call | solution.py:279
  88.5 1.6 %collective-permute-start.25 = (bf16[64,512]{1,0:T(8,128)(2,1)S(1)}, bf16[64,512]{1,0:T(8,128)(2,1)S(1)}, u32[]{:S(2)}, u32[]{:S(2)}) collective-permute-start(bf16[64,512]{1,0:T(8,128)(2,1)S(1)} %get-tuple-element.94), channel_id=1, source_target_pairs={{0,2},{1,3},{2,0},{3,1},{4,6},{5,7},{6,4},{7,5},{8,10},{9,11},{10,... | collective-permute-start | bytes 196616 | tf_op jit(solution)/shard_map/ppermute | solution.py:25
  90.0 2.8 %collective-permute-done.25.came = bf16[64,512]{1,0:T(8,128)(2,1)S(1)} collective-permute-done((bf16[64,512]{1,0:T(8,128)(2,1)S(1)}, bf16[64,512]{1,0:T(8,128)(2,1)S(1)}, u32[]{:S(2)}, u32[]{:S(2)}) %collective-permute-start.25) | collective-permute-done | bytes 65568 | tf_op jit(solution)/shard_map/ppermute | solution.py:25
  92.8 3.0 %collective-permute-start.26 = (bf16[64,512]{1,0:T(8,128)(2,1)S(1)}, bf16[64,512]{1,0:T(8,128)(2,1)S(1)}, u32[]{:S(2)}, u32[]{:S(2)}) collective-permute-start(bf16[64,512]{1,0:T(8,128)(2,1)S(1)} %shard_map.77.refs_0_), channel_id=1, source_target_pairs={{0,28},{4,24},{8,20},{12,16},{16,12},{20,8},{24,4},{28,0},{1,29},{... | collective-permute-start | bytes 196616 | tf_op jit(solution)/shard_map/ppermute | solution.py:25
  95.8 1.8 %collective-permute-start.27 = (bf16[64,512]{1,0:T(8,128)(2,1)S(1)}, bf16[64,512]{1,0:T(8,128)(2,1)S(1)}, u32[]{:S(2)}, u32[]{:S(2)}) collective-permute-start(bf16[64,512]{1,0:T(8,128)(2,1)S(1)} %shard_map.77.refs_0_), channel_id=1, source_target_pairs={{0,24},{4,28},{8,16},{12,20},{16,8},{20,12},{24,0},{28,4},{1,25},{... | collective-permute-start | bytes 196616 | tf_op jit(solution)/shard_map/ppermute | solution.py:25
  97.6 1.7 %collective-permute-start.28 = (bf16[64,512]{1,0:T(8,128)(2,1)S(1)}, bf16[64,512]{1,0:T(8,128)(2,1)S(1)}, u32[]{:S(2)}, u32[]{:S(2)}) collective-permute-start(bf16[64,512]{1,0:T(8,128)(2,1)S(1)} %shard_map.77.refs_0_), channel_id=1, source_target_pairs={{0,20},{4,16},{8,28},{12,24},{16,4},{20,0},{24,12},{28,8},{1,21},{... | collective-permute-start | bytes 196616 | tf_op jit(solution)/shard_map/ppermute | solution.py:25
  100.5 2.2 %collective-permute-start.30 = (bf16[64,512]{1,0:T(8,128)(2,1)S(1)}, bf16[64,512]{1,0:T(8,128)(2,1)S(1)}, u32[]{:S(2)}, u32[]{:S(2)}) collective-permute-start(bf16[64,512]{1,0:T(8,128)(2,1)S(1)} %shard_map.77.refs_0_), channel_id=1, source_target_pairs={{0,12},{4,8},{8,4},{12,0},{16,28},{20,24},{24,20},{28,16},{1,13},{... | collective-permute-start | bytes 196616 | tf_op jit(solution)/shard_map/ppermute | solution.py:25
  102.7 3.2 %collective-permute-start.31 = (bf16[64,512]{1,0:T(8,128)(2,1)S(1)}, bf16[64,512]{1,0:T(8,128)(2,1)S(1)}, u32[]{:S(2)}, u32[]{:S(2)}) collective-permute-start(bf16[64,512]{1,0:T(8,128)(2,1)S(1)} %shard_map.77.refs_0_), channel_id=1, source_target_pairs={{0,8},{4,12},{8,0},{12,4},{16,24},{20,28},{24,16},{28,20},{1,9},{5... | collective-permute-start | bytes 196616 | tf_op jit(solution)/shard_map/ppermute | solution.py:25
  106.3 2.4 %collective-permute-done.28.refs_3_ = bf16[64,512]{1,0:T(8,128)(2,1)S(1)} collective-permute-done((bf16[64,512]{1,0:T(8,128)(2,1)S(1)}, bf16[64,512]{1,0:T(8,128)(2,1)S(1)}, u32[]{:S(2)}, u32[]{:S(2)}) %collective-permute-start.28) | collective-permute-done | bytes 65568 | tf_op jit(solution)/shard_map/ppermute | solution.py:25
  110.2 1.7 %shard_map.78 = f32[512,512]{1,0:T(8,128)} custom-call(s32[4]{0:T(128)S(1)} %pad_add_fusion.scalars, bf16[64,512]{1,0:T(8,128)(2,1)S(1)} %shard_map.77.refs_0_, bf16[64,512]{1,0:T(8,128)(2,1)S(1)} %collective-permute-done.26.refs_1_, bf16[64,512]{1,0:T(8,128)(2,1)S(1)} %collective-permute-done.27.refs_2_, ...), custom_call_target="tpu_custom_call" | custom-call | tf_op jit(solution)/shard_map/pallas_call | solution.py:279
  (61 shorter events, 20.2 us)
Async XLA Ops:
  0.0 22.5 %collective-permute-start = (bf16[128,2048]{1,0:T(8,128)(2,1)}, bf16[128,2048]{1,0:T(8,128)(2,1)S(1)}, u32[]{:S(2)}, u32[]{:S(2)}) collective-permute-start(bf16[128,2048]{1,0:T(8,128)(2,1)} %param.6), channel_id=1, source_target_pairs={{0,4},{4,0},{8,12},{12,8},{16,20},{20,16},{24,28},{28,24},{1,5},{5... | collective-permute-start | bytes 1572872 | tf_op jit(solution)/shard_map/ppermute | solution.py:25
  4.0 14.5 %collective-permute-start.7 = (bf16[64,2048]{1,0:T(8,128)(2,1)S(1)}, bf16[64,2048]{1,0:T(8,128)(2,1)S(1)}, u32[]{:S(2)}, u32[]{:S(2)}) collective-permute-start(bf16[64,2048]{1,0:T(8,128)(2,1)S(1)} %get-tuple-element.96.refs_0_), channel_id=1, source_target_pairs={{0,16},{4,20},{8,24},{12,28},{16,0},{20,4},{24,8},{28,12},{1,17},{... | collective-permute-start | bytes 786440 | tf_op jit(solution)/shard_map/ppermute | solution.py:25
  6.7 12.7 %collective-permute-start.1 = (bf16[64,2048]{1,0:T(8,128)(2,1)S(1)}, bf16[64,2048]{1,0:T(8,128)(2,1)S(1)}, u32[]{:S(2)}, u32[]{:S(2)}) collective-permute-start(bf16[64,2048]{1,0:T(8,128)(2,1)S(1)} %get-tuple-element.96.refs_0_), channel_id=1, source_target_pairs={{0,8},{4,12},{8,0},{12,4},{16,24},{20,28},{24,16},{28,20},{1,9},{5... | collective-permute-start | bytes 786440 | tf_op jit(solution)/shard_map/ppermute | solution.py:25
  12.3 10.2 %collective-permute-start.3 = (bf16[272,128]{1,0:T(8,128)(2,1)S(1)}, bf16[272,128]{1,0:T(8,128)(2,1)S(1)}, u32[]{:S(2)}, u32[]{:S(2)}) collective-permute-start(bf16[272,128]{1,0:T(8,128)(2,1)S(1)} %get-tuple-element.51), channel_id=1, source_target_pairs={{0,8},{4,12},{8,0},{12,4},{16,24},{20,28},{24,16},{28,20},{1,9},{5... | collective-permute-start | bytes 208904 | tf_op jit(solution)/shard_map/ppermute | solution.py:25
  18.5 13.7 %collective-permute-start.8 = (bf16[64,2048]{1,0:T(8,128)(2,1)S(1)}, bf16[64,2048]{1,0:T(8,128)(2,1)S(1)}, u32[]{:S(2)}, u32[]{:S(2)}) collective-permute-start(bf16[64,2048]{1,0:T(8,128)(2,1)S(1)} %get-tuple-element.57.refs_1_), channel_id=1, source_target_pairs={{0,16},{4,20},{8,24},{12,28},{16,0},{20,4},{24,8},{28,12},{1,17},{... | collective-permute-start | bytes 786440 | tf_op jit(solution)/shard_map/ppermute | solution.py:25
  19.4 14.0 %collective-permute-start.2 = (bf16[64,2048]{1,0:T(8,128)(2,1)S(1)}, bf16[64,2048]{1,0:T(8,128)(2,1)S(1)}, u32[]{:S(2)}, u32[]{:S(2)}) collective-permute-start(bf16[64,2048]{1,0:T(8,128)(2,1)S(1)} %get-tuple-element.57.refs_1_), channel_id=1, source_target_pairs={{0,8},{4,12},{8,0},{12,4},{16,24},{20,28},{24,16},{28,20},{1,9},{5... | collective-permute-start | bytes 786440 | tf_op jit(solution)/shard_map/ppermute | solution.py:25
  22.6 10.8 %collective-permute-start.4 = (bf16[64,2048]{1,0:T(8,128)(2,1)S(1)}, bf16[64,2048]{1,0:T(8,128)(2,1)S(1)}, u32[]{:S(2)}, u32[]{:S(2)}) collective-permute-start(bf16[64,2048]{1,0:T(8,128)(2,1)S(1)} %collective-permute-done.1.refs_3_), channel_id=1, source_target_pairs={{0,4},{4,0},{8,12},{12,8},{16,20},{20,16},{24,28},{28,24},{1,5},{5... | collective-permute-start | bytes 786440 | tf_op jit(solution)/shard_map/ppermute | solution.py:25
  23.6 9.7 %collective-permute-start.5 = (bf16[144,256]{1,0:T(8,128)(2,1)S(1)}, bf16[144,256]{1,0:T(8,128)(2,1)S(1)}, u32[]{:S(2)}, u32[]{:S(2)}) collective-permute-start(bf16[144,256]{1,0:T(8,128)(2,1)S(1)} %get-tuple-element.55), channel_id=1, source_target_pairs={{0,4},{4,0},{8,12},{12,8},{16,20},{20,16},{24,28},{28,24},{1,5},{5... | collective-permute-start | bytes 221192 | tf_op jit(solution)/shard_map/ppermute | solution.py:25
  25.2 13.8 %collective-permute-start.14 = (bf16[64,2048]{1,0:T(8,128)(2,1)S(1)}, bf16[64,2048]{1,0:T(8,128)(2,1)S(1)}, u32[]{:S(2)}, u32[]{:S(2)}) collective-permute-start(bf16[64,2048]{1,0:T(8,128)(2,1)S(1)} %collective-permute-done.7.refs_7_), channel_id=1, source_target_pairs={{0,4},{4,0},{8,12},{12,8},{16,20},{20,16},{24,28},{28,24},{1,5},{5... | collective-permute-start | bytes 786440 | tf_op jit(solution)/shard_map/ppermute | solution.py:25
  32.2 7.3 %collective-permute-start.10 = (bf16[64,2048]{1,0:T(8,128)(2,1)S(1)}, bf16[64,2048]{1,0:T(8,128)(2,1)S(1)}, u32[]{:S(2)}, u32[]{:S(2)}) collective-permute-start(bf16[64,2048]{1,0:T(8,128)(2,1)S(1)} %collective-permute-done.8.refs_8_), channel_id=1, source_target_pairs={{0,8},{4,12},{8,0},{12,4},{16,24},{20,28},{24,16},{28,20},{1,9},{5... | collective-permute-start | bytes 786440 | tf_op jit(solution)/shard_map/ppermute | solution.py:25
  33.4 11.2 %collective-permute-start.6 = (bf16[64,2048]{1,0:T(8,128)(2,1)S(1)}, bf16[64,2048]{1,0:T(8,128)(2,1)S(1)}, u32[]{:S(2)}, u32[]{:S(2)}) collective-permute-start(bf16[64,2048]{1,0:T(8,128)(2,1)S(1)} %collective-permute-done.2.refs_4_), channel_id=1, source_target_pairs={{0,4},{4,0},{8,12},{12,8},{16,20},{20,16},{24,28},{28,24},{1,5},{5... | collective-permute-start | bytes 786440 | tf_op jit(solution)/shard_map/ppermute | solution.py:25
  33.9 1.6 %collective-permute-start.12 = (bf16[64,512]{1,0:T(8,128)(2,1)S(1)}, bf16[64,512]{1,0:T(8,128)(2,1)S(1)}, u32[]{:S(2)}, u32[]{:S(2)}) collective-permute-start(bf16[64,512]{1,0:T(8,128)(2,1)S(1)} %get-tuple-element.67), channel_id=1, source_target_pairs={{0,1},{1,0},{2,3},{3,2},{4,5},{5,4},{6,7},{7,6},{8,9},{9,8},{10,11... | collective-permute-start | bytes 196616 | tf_op jit(solution)/shard_map/ppermute | solution.py:25
  34.5 16.8 %collective-permute-start.9 = (bf16[64,2048]{1,0:T(8,128)(2,1)S(1)}, bf16[64,2048]{1,0:T(8,128)(2,1)S(1)}, u32[]{:S(2)}, u32[]{:S(2)}) collective-permute-start(bf16[64,2048]{1,0:T(8,128)(2,1)S(1)} %collective-permute-done.7.refs_7_), channel_id=1, source_target_pairs={{0,8},{4,12},{8,0},{12,4},{16,24},{20,28},{24,16},{28,20},{1,9},{5... | collective-permute-start | bytes 786440 | tf_op jit(solution)/shard_map/ppermute | solution.py:25
  35.5 9.7 %collective-permute-start.13 = (bf16[128,512]{1,0:T(8,128)(2,1)S(1)}, bf16[128,512]{1,0:T(8,128)(2,1)S(1)}, u32[]{:S(2)}, u32[]{:S(2)}) collective-permute-start(bf16[128,512]{1,0:T(8,128)(2,1)S(1)} %pad_maximum_fusion), channel_id=1, source_target_pairs={{0,2},{1,3},{2,0},{3,1},{4,6},{5,7},{6,4},{7,5},{8,10},{9,11},{10,... | collective-permute-start | bytes 393224 | tf_op jit(solution)/shard_map/ppermute | solution.py:25
  39.0 15.1 %collective-permute-start.15 = (bf16[64,2048]{1,0:T(8,128)(2,1)S(1)}, bf16[64,2048]{1,0:T(8,128)(2,1)S(1)}, u32[]{:S(2)}, u32[]{:S(2)}) collective-permute-start(bf16[64,2048]{1,0:T(8,128)(2,1)S(1)} %collective-permute-done.8.refs_8_), channel_id=1, source_target_pairs={{0,4},{4,0},{8,12},{12,8},{16,20},{20,16},{24,28},{28,24},{1,5},{5... | collective-permute-start | bytes 786440 | tf_op jit(solution)/shard_map/ppermute | solution.py:25
  39.5 14.6 %collective-permute-start.16 = (bf16[64,2048]{1,0:T(8,128)(2,1)S(1)}, bf16[64,2048]{1,0:T(8,128)(2,1)S(1)}, u32[]{:S(2)}, u32[]{:S(2)}) collective-permute-start(bf16[64,2048]{1,0:T(8,128)(2,1)S(1)} %collective-permute-done.14.refs_0_), channel_id=1, source_target_pairs={{0,8},{4,12},{8,0},{12,4},{16,24},{20,28},{24,16},{28,20},{1,9},{5... | collective-permute-start | bytes 786440 | tf_op jit(solution)/shard_map/ppermute | solution.py:25
  44.6 9.6 %collective-permute-start.17 = (bf16[64,2048]{1,0:T(8,128)(2,1)S(1)}, bf16[64,2048]{1,0:T(8,128)(2,1)S(1)}, u32[]{:S(2)}, u32[]{:S(2)}) collective-permute-start(bf16[64,2048]{1,0:T(8,128)(2,1)S(1)} %collective-permute-done.10.refs_10_), channel_id=1, source_target_pairs={{0,4},{4,0},{8,12},{12,8},{16,20},{20,16},{24,28},{28,24},{1,5},{5... | collective-permute-start | bytes 786440 | tf_op jit(solution)/shard_map/ppermute | solution.py:25
  45.1 5.5 %collective-permute-start.11 = (bf16[80,512]{1,0:T(8,128)(2,1)S(1)}, bf16[80,512]{1,0:T(8,128)(2,1)S(1)}, u32[]{:S(2)}, u32[]{:S(2)}) collective-permute-start(bf16[80,512]{1,0:T(8,128)(2,1)S(1)} %get-tuple-element.63), channel_id=1, source_target_pairs={{0,16},{4,20},{8,24},{12,28},{16,0},{20,4},{24,8},{28,12},{1,17},{... | collective-permute-start | bytes 245768 | tf_op jit(solution)/shard_map/ppermute | solution.py:25
  55.8 1.6 %collective-permute-start.18 = (bf16[128,1024]{1,0:T(8,128)(2,1)S(1)}, bf16[128,1024]{1,0:T(8,128)(2,1)S(1)}, u32[]{:S(2)}, u32[]{:S(2)}) collective-permute-start(bf16[128,1024]{1,0:T(8,128)(2,1)S(1)} %get-tuple-element.80), channel_id=1, source_target_pairs={{0,1},{1,0},{2,3},{3,2},{4,5},{5,4},{6,7},{7,6},{8,9},{9,8},{10,11... | collective-permute-start | bytes 786440 | tf_op jit(solution)/shard_map/ppermute | solution.py:25
  57.5 8.4 %collective-permute-start.19 = (bf16[128,1024]{1,0:T(8,128)(2,1)S(1)}, bf16[128,1024]{1,0:T(8,128)(2,1)S(1)}, u32[]{:S(2)}, u32[]{:S(2)}) collective-permute-start(bf16[128,1024]{1,0:T(8,128)(2,1)S(1)} %get-tuple-element.82), channel_id=1, source_target_pairs={{0,2},{1,3},{2,0},{3,1},{4,6},{5,7},{6,4},{7,5},{8,10},{9,11},{10,... | collective-permute-start | bytes 786440 | tf_op jit(solution)/shard_map/ppermute | solution.py:25
  66.5 1.6 %collective-permute-start.20 = (bf16[128,1024]{1,0:T(8,128)(2,1)S(1)}, bf16[128,1024]{1,0:T(8,128)(2,1)S(1)}, u32[]{:S(2)}, u32[]{:S(2)}) collective-permute-start(bf16[128,1024]{1,0:T(8,128)(2,1)S(1)} %shard_map.71.refs_6_), channel_id=1, source_target_pairs={{0,1},{1,0},{2,3},{3,2},{4,5},{5,4},{6,7},{7,6},{8,9},{9,8},{10,11... | collective-permute-start | bytes 786440 | tf_op jit(solution)/shard_map/ppermute | solution.py:25
  71.1 1.6 %collective-permute-start.21 = (bf16[128,1024]{1,0:T(8,128)(2,1)S(1)}, bf16[128,1024]{1,0:T(8,128)(2,1)S(1)}, u32[]{:S(2)}, u32[]{:S(2)}) collective-permute-start(bf16[128,1024]{1,0:T(8,128)(2,1)S(1)} %get-tuple-element.84), channel_id=1, source_target_pairs={{0,1},{1,0},{2,3},{3,2},{4,5},{5,4},{6,7},{7,6},{8,9},{9,8},{10,11... | collective-permute-start | bytes 786440 | tf_op jit(solution)/shard_map/ppermute | solution.py:25
  72.8 8.4 %collective-permute-start.22 = (bf16[128,1024]{1,0:T(8,128)(2,1)S(1)}, bf16[128,1024]{1,0:T(8,128)(2,1)S(1)}, u32[]{:S(2)}, u32[]{:S(2)}) collective-permute-start(bf16[128,1024]{1,0:T(8,128)(2,1)S(1)} %get-tuple-element.86), channel_id=1, source_target_pairs={{0,2},{1,3},{2,0},{3,1},{4,6},{5,7},{6,4},{7,5},{8,10},{9,11},{10,... | collective-permute-start | bytes 786440 | tf_op jit(solution)/shard_map/ppermute | solution.py:25
  81.8 1.6 %collective-permute-start.23 = (bf16[128,1024]{1,0:T(8,128)(2,1)S(1)}, bf16[128,1024]{1,0:T(8,128)(2,1)S(1)}, u32[]{:S(2)}, u32[]{:S(2)}) collective-permute-start(bf16[128,1024]{1,0:T(8,128)(2,1)S(1)} %get-tuple-element.90.refs_8_), channel_id=1, source_target_pairs={{0,1},{1,0},{2,3},{3,2},{4,5},{5,4},{6,7},{7,6},{8,9},{9,8},{10,11... | collective-permute-start | bytes 786440 | tf_op jit(solution)/shard_map/ppermute | solution.py:25
  88.5 4.3 %collective-permute-start.25 = (bf16[64,512]{1,0:T(8,128)(2,1)S(1)}, bf16[64,512]{1,0:T(8,128)(2,1)S(1)}, u32[]{:S(2)}, u32[]{:S(2)}) collective-permute-start(bf16[64,512]{1,0:T(8,128)(2,1)S(1)} %get-tuple-element.94), channel_id=1, source_target_pairs={{0,2},{1,3},{2,0},{3,1},{4,6},{5,7},{6,4},{7,5},{8,10},{9,11},{10,... | collective-permute-start | bytes 196616 | tf_op jit(solution)/shard_map/ppermute | solution.py:25
  92.8 9.9 %collective-permute-start.26 = (bf16[64,512]{1,0:T(8,128)(2,1)S(1)}, bf16[64,512]{1,0:T(8,128)(2,1)S(1)}, u32[]{:S(2)}, u32[]{:S(2)}) collective-permute-start(bf16[64,512]{1,0:T(8,128)(2,1)S(1)} %shard_map.77.refs_0_), channel_id=1, source_target_pairs={{0,28},{4,24},{8,20},{12,16},{16,12},{20,8},{24,4},{28,0},{1,29},{... | collective-permute-start | bytes 196616 | tf_op jit(solution)/shard_map/ppermute | solution.py:25
  95.8 10.1 %collective-permute-start.27 = (bf16[64,512]{1,0:T(8,128)(2,1)S(1)}, bf16[64,512]{1,0:T(8,128)(2,1)S(1)}, u32[]{:S(2)}, u32[]{:S(2)}) collective-permute-start(bf16[64,512]{1,0:T(8,128)(2,1)S(1)} %shard_map.77.refs_0_), channel_id=1, source_target_pairs={{0,24},{4,28},{8,16},{12,20},{16,8},{20,12},{24,0},{28,4},{1,25},{... | collective-permute-start | bytes 196616 | tf_op jit(solution)/shard_map/ppermute | solution.py:25
  97.6 11.1 %collective-permute-start.28 = (bf16[64,512]{1,0:T(8,128)(2,1)S(1)}, bf16[64,512]{1,0:T(8,128)(2,1)S(1)}, u32[]{:S(2)}, u32[]{:S(2)}) collective-permute-start(bf16[64,512]{1,0:T(8,128)(2,1)S(1)} %shard_map.77.refs_0_), channel_id=1, source_target_pairs={{0,20},{4,16},{8,28},{12,24},{16,4},{20,0},{24,12},{28,8},{1,21},{... | collective-permute-start | bytes 196616 | tf_op jit(solution)/shard_map/ppermute | solution.py:25
  99.3 9.4 %collective-permute-start.29 = (bf16[64,512]{1,0:T(8,128)(2,1)S(1)}, bf16[64,512]{1,0:T(8,128)(2,1)S(1)}, u32[]{:S(2)}, u32[]{:S(2)}) collective-permute-start(bf16[64,512]{1,0:T(8,128)(2,1)S(1)} %shard_map.77.refs_0_), channel_id=1, source_target_pairs={{0,16},{4,20},{8,24},{12,28},{16,0},{20,4},{24,8},{28,12},{1,17},{... | collective-permute-start | bytes 196616 | tf_op jit(solution)/shard_map/ppermute | solution.py:25
  100.5 8.2 %collective-permute-start.30 = (bf16[64,512]{1,0:T(8,128)(2,1)S(1)}, bf16[64,512]{1,0:T(8,128)(2,1)S(1)}, u32[]{:S(2)}, u32[]{:S(2)}) collective-permute-start(bf16[64,512]{1,0:T(8,128)(2,1)S(1)} %shard_map.77.refs_0_), channel_id=1, source_target_pairs={{0,12},{4,8},{8,4},{12,0},{16,28},{20,24},{24,20},{28,16},{1,13},{... | collective-permute-start | bytes 196616 | tf_op jit(solution)/shard_map/ppermute | solution.py:25
  102.7 6.4 %collective-permute-start.31 = (bf16[64,512]{1,0:T(8,128)(2,1)S(1)}, bf16[64,512]{1,0:T(8,128)(2,1)S(1)}, u32[]{:S(2)}, u32[]{:S(2)}) collective-permute-start(bf16[64,512]{1,0:T(8,128)(2,1)S(1)} %shard_map.77.refs_0_), channel_id=1, source_target_pairs={{0,8},{4,12},{8,0},{12,4},{16,24},{20,28},{24,16},{28,20},{1,9},{5... | collective-permute-start | bytes 196616 | tf_op jit(solution)/shard_map/ppermute | solution.py:25
  105.9 4.3 %collective-permute-start.32 = (bf16[64,512]{1,0:T(8,128)(2,1)S(1)}, bf16[64,512]{1,0:T(8,128)(2,1)S(1)}, u32[]{:S(2)}, u32[]{:S(2)}) collective-permute-start(bf16[64,512]{1,0:T(8,128)(2,1)S(1)} %shard_map.77.refs_0_), channel_id=1, source_target_pairs={{0,4},{4,0},{8,12},{12,8},{16,20},{20,16},{24,28},{28,24},{1,5},{5... | collective-permute-start | bytes 196616 | tf_op jit(solution)/shard_map/ppermute | solution.py:25
  (4 other events, 18.0 us)

commit v4 on v3

--- a/solution.py
+++ b/solution.py
@@ -167,47 +167,92 @@
         in_tiles(held, sums, keep, body)
 
 
-def in_parts(parts, send, keep, sums, body):
-    early, late = parts
-    in_tiles(
-        early[0], sums, keep, lambda rows, before: body(early, rows, sums, keep, before)
-    )
-    body(late, pl.ds(0, late[0].shape[0]), send, keep, (sums, keep))
+def sort_kernel(sizes, rows, scalars, rate, *refs):
+    part, pairs, copies, length = sizes
+    early, late, (own, own_side, sent, sent_side) = refs[:4], refs[4:8], refs[8:]
+    core = scalars[1] % 2
+    wide = late[1].shape[0]
+    counts = [jnp.int32(0), jnp.int32(0)]
+    for held, up, labels, primal in (early, late):
+        for i in range(held.shape[0] // rows):
+            place = pl.ds(i * rows, rows)
+            label = labels[:, place].astype(F32)
+            forget, copy = label[0:1, :], label[1:2, :]
+            upward = up[:, place].astype(F32)
+            own_rate = sum((copy == float(c)).astype(F32) * rate[c] for c in range(copies))
+            factor = own_rate * (forget * upward * second_slope(primal[:, place]) / length)
+            signed = (1.0 - 2.0 * forget) * upward
+            mine = (jnp.max(copy).astype(jnp.int32) == core).astype(jnp.int32)
+            for k, (tokens, side) in enumerate(((own, own_side), (sent, sent_side))):
+                at = pl.ds(pl.multiple_of(counts[k] * rows, rows), rows)
+                here = mine if k == 0 else 1 - mine
+
+                @pl.when(here == 1)
+                def _(tokens=tokens, side=side, at=at):
+                    tokens[at, :] = held[place, :]
+                    side[pl.ds(0, wide), at] = signed.astype(BF)
+                    side[pl.ds(wide, wide), at] = factor.astype(BF)
+
+                counts[k] = counts[k] + here
+
+
+def in_tiles_of(parts, out, body):
+    tile = min(parts[0][0].shape[0], 1024)
+    if parts[0][0].shape[0] == tile:
+        for i, tokens in enumerate(parts):
+            body(tokens, pl.ds(0, tile), out, i > 0)
+        return
+    out[...] = jnp.zeros_like(out)
+    for tokens in parts:
+
+        def step(i, none):
+            body(tokens, pl.ds(pl.multiple_of(i * tile, tile), tile), out, True)
+
+        lax.fori_loop(0, tokens[0].shape[0] // tile, step, None)
+
+
+def add_terms(delta, held, rows, out, more):
+    term = jnp.dot(delta, held[rows, :], preferred_element_type=F32)
+    out[...] = out[...] + term if more else term
 
 
 def second_kernel(sizes, scalars, *refs):
     part, pairs, copies, length = sizes
-    early, late, (mine, other, send, keep, sums) = refs[:3], refs[3:6], refs[6:]
+    early, late, (mine, other, send, keep) = refs[:2], refs[2:4], refs[4:]
     core = scalars[1] % 2
 
-    def body(tokens, rows, send, keep, before):
-        held, up, labels = tokens
-        hots = onehots(labels[:, rows], copies)
-        altered = of_copy(times_tokens(core, part, pairs, mine, other, held, rows), hots)
-        sign = 1.0 - 2.0 * labels[0:1, rows].astype(F32)
-        delta = (sign * up[:, rows].astype(F32) * first_slope(altered) / length).astype(BF)
-        contract(core, part, pairs, by_copy(delta, hots), held, rows, send, keep, before)
-
-    in_parts((early, late), send, keep, sums, body)
-
-
-def third_kernel(sizes, scalars, rate, *refs):
+    def body(tokens, rows, keep, more):
+        held, side = tokens
+        altered = times_tokens(core, part, pairs, mine, other, held, rows)
+        upward = side[pl.ds(0, altered.shape[0]), rows].astype(F32)
+        delta = (upward * first_slope(altered) / length).astype(BF)
+        add_terms(delta, held, rows, keep, more)
+
+    in_tiles_of((early, late), keep, body)
+    send[...] = keep[...].astype(BF)
+
+
+def third_kernel(sizes, scalars, *refs):
     part, pairs, copies, length = sizes
-    early, late, (mine, other, send, keep, sums) = refs[:4], refs[4:8], refs[8:]
+    early, late, (local, summed, came, send, keep, tangent, curv) = refs[:2], refs[2:4], refs[4:]
     core = scalars[1] % 2
-
-    def body(tokens, rows, send, keep, before):
-        held, up, labels, primal = tokens
-        hots = onehots(labels[:, rows], copies)
-        forward = of_copy(times_tokens(core, part, pairs, mine, other, held, rows), hots)
-        forget = labels[0:1, rows].astype(F32)
-        own_rate = sum(hot * rate[c] for c, hot in enumerate(hots))
-        slope = second_slope(primal[:, rows])
-        delta = (forget * up[:, rows].astype(F32) * slope * forward / length).astype(BF)
-        delta = (own_rate * delta.astype(F32)).astype(BF)
-        contract(core, part, pairs, delta, held, rows, send, keep, before)
-
-    in_parts((early, late), send, keep, sums, body)
+    tangent[...] = (summed[...] + came[...].astype(F32)).astype(BF)
+
+    def body(tokens, rows, curv, more):
+        held, side = tokens
+        forward = lax.dot_general(
+            tangent[...], held[rows, :], (((1,), (1,)), ((), ())), preferred_element_type=F32
+        )
+        wide = forward.shape[0]
+        delta = (side[pl.ds(wide, wide), rows].astype(F32) * forward).astype(BF)
+        add_terms(delta, held, rows, curv, more)
+
+    in_tiles_of((early, late), curv, body)
+    for j in range(pairs):
+        for out, side in ((send, 1 - core), (keep, core)):
+            columns = pl.ds(pl.multiple_of((2 * j + side) * part, part), part)
+            value = local[:, columns] - curv[:, columns]
+            out[:, pl.ds(j * part, part)] = value.astype(out.dtype)
 
 
 def add_kernel(mine, came, total, sent):
@@ -216,29 +261,18 @@
     sent[...] = value.astype(BF)
 
 
-def attack_kernel(copies, scalars, rate, mine, came, weight, attacked):
+def attack_kernel(scalars, rate, mine, came, weight, own, sent):
     quarter = scalars[1]
     part = weight.shape[1]
-    wide = mine.shape[0] // copies
+    wide = own.shape[0]
     for j in range(mine.shape[1] // part):
         place = quarter ^ (2 * j + quarter % 2)
-        own = weight[pl.ds(pl.multiple_of(place * wide, wide), wide), :].astype(F32)
+        start = weight[pl.ds(pl.multiple_of(place * wide, wide), wide), :].astype(F32)
         columns = pl.ds(j * part, part)
-        for c in range(copies):
-            rows = pl.ds(c * wide, wide)
+        for out, c in ((own, quarter % 2), (sent, 1 - quarter % 2)):
+            rows = pl.ds(pl.multiple_of(c * wide, wide), wide)
             grad = mine[rows, columns] + came[rows, columns].astype(F32)
-            attacked[rows, columns] = (own - rate[c] * grad).astype(BF)
-
-
-def tangent_kernel(copies, scalars, mine, came, tangent, outer):
-    value = mine[...] + came[...].astype(F32)
-    tangent[...] = value.astype(BF)
-    wide, part = outer.shape
-    own = pl.ds(pl.multiple_of((scalars[1] // 2) * part, part), part)
-    outer[...] = sum(
-        mine[pl.ds(c * wide, wide), own] + came[pl.ds(c * wide, wide), own].astype(F32)
-        for c in range(copies)
-    )
+            out[:, columns] = (start - rate[c] * grad).astype(BF)
 
 
 def halve_kernel(bit, scalars, mine, came, total, sent, whole):
@@ -249,8 +283,8 @@
     sent[...] = whole[:, pl.ds(pl.multiple_of((1 - side) * half, half), half)].astype(BF)
 
 
-def result_kernel(scale, outer, mine, came, result):
-    result[...] = (scale * (outer[...] - (mine[...] + came[...].astype(F32)))).astype(BF)
+def result_kernel(scale, mine, came, result):
+    result[...] = (scale * (mine[...] + came[...].astype(F32))).astype(BF)
 
 
 def place_kernel(order, scalars, *refs):
@@ -376,11 +410,9 @@
     for bit in bits_of(fsdp):
         weight = jnp.concatenate([weight, swap(weight, "fsdp", bit)])
 
-    def total(send, keep, bits):
-        shape = keep.shape
-        came = swap(send, "fsdp", 1)
+    def total(keep, came, bits):
         for bit in bits:
-            keep, sent = run(add_kernel, [], [keep, came], [(shape, F32), (shape, BF)])
+            keep, sent = run(add_kernel, [], [keep, came], [(keep.shape, F32), (keep.shape, BF)])
             came = swap(sent, "fsdp", bit)
         return keep, came
 
@@ -401,31 +433,33 @@
 
     *tokens_early, primal_early, sums, keep = put_together(early, [])
     *tokens_late, primal_late, send, keep = put_together(late, [sums, keep])
-    (attacked,) = run(
-        functools.partial(attack_kernel, copies),
+    summed, came = total(keep, swap(send, "fsdp", 1), far_bits)
+    tokens_early[2] = after(tokens_early[2], summed)
+    taken = ((dp // 2 * rows, features), BF)
+    beside = ((2 * wide, dp // 2 * rows), BF)
+    own, own_side, sent, sent_side = run(
+        functools.partial(sort_kernel, sizes, rows),
         [scalars, adv_rate],
-        [*total(send, keep, far_bits), weight],
-        [(stacked, BF)],
+        [*tokens_early, primal_early, *tokens_late, primal_late],
+        [taken, beside, taken, beside],
+    )
+    mine = [own, own_side, swap(sent, "fsdp", 1), swap(sent_side, "fsdp", 1)]
+    half, full = (wide, features // 2), (wide, features)
+    attacked, sent = run(
+        attack_kernel, [scalars, adv_rate], [summed, came, weight], [(half, BF), (half, BF)]
     )
     send, keep = run(
         functools.partial(second_kernel, sizes),
         [scalars],
-        [*tokens_early, *tokens_late, attacked, swap(attacked, "fsdp", 1)],
-        [(stacked, BF), (stacked, F32)],
-        [(stacked, F32)],
-    )
-    tangent, outer = run(
-        functools.partial(tangent_kernel, copies),
-        [scalars],
-        [*total(send, keep, far_bits)],
-        [(stacked, BF), ((wide, part), F32)],
+        [*mine, attacked, swap(sent, "fsdp", 1)],
+        [(full, BF), (full, F32)],
     )
     send, keep = run(
         functools.partial(third_kernel, sizes),
-        [scalars, adv_rate],
-        [*tokens_early, primal_early, *tokens_late, primal_late, tangent, swap(tangent, "fsdp", 1)],
-        [((wide, features // 2), BF), ((wide, features // 2), F32)],
-        [((wide, features // 2), F32)],
+        [scalars],
+        [*mine, keep, *total(keep, swap(send, "fsdp", far_bits[0]), far_bits[1:])],
+        [(half, BF), (half, F32)],
+        [(full, BF), (full, F32)],
     )
 
     came = swap(send, "fsdp", 1)
@@ -441,7 +475,7 @@
         came = swap(sent, "fsdp", bit)
     scale = (float(seq_length) / float(dp)) ** 0.5
     (result,) = run(
-        functools.partial(result_kernel, scale), [], [outer, keep, came], [((wide, part), BF)]
+        functools.partial(result_kernel, scale), [], [keep, came], [((wide, part), BF)]
     )
     blocks = [result]
     came_order = [0]

time: 112 us -> 110 us (0.982)
  waiting for transfers between devices: 52.4 us -> 49.6 us
    ppermute x33, waiting for transfers between devices: 52.4 us -> 49.6 us  [swap(): lax.ppermute(value, axis, [(i, i ^ bit) for i in range(lax.axis_size(axis...]
    pallas_call x15 -> x14, Pallas kernels: 16.6 us -> 17.6 us  [run(): pl.pallas_call(kernel, out_shape=[jax.ShapeDtypeStruct(s, t) for s, t in...]
  transfers between devices with their start and end apart: 33 -> 33, of which waited for: 19 -> 17; matrix products, arithmetic and copies ran while one was open for 1% -> 1% of each run, Pallas kernels for 5% -> 5%
where the time goes in v4:
time: 110 us
  waiting for transfers between devices  49.6 us (45%)
  starting transfers between devices  38.1 us (35%)
  Pallas kernels  17.6 us (16%)
  local copies, waits for them, and re-layouts  3.04 us (3%)
  between operations  1.5 us (1%)
    ppermute x33, waiting for transfers between devices, swap(): lax.ppermute(value, axis, [(i, i ^ bit) for i in range(lax.axis_size(axis...  49.6 us
    ppermute x33, starting transfers between devices, swap(): lax.ppermute(value, axis, [(i, i ^ bit) for i in range(lax.axis_size(axis...  38.1 us
    pallas_call x14, Pallas kernels, run(): pl.pallas_call(kernel, out_shape=[jax.ShapeDtypeStruct(s, t) for s, t in...  17.6 us
  transfers between devices with their start and end apart: 33, of which 17 were waited for; matrix products, arithmetic and copies ran while one was open for 1% of the time, Pallas kernels for 5%

profile of v4, /device:TPU:0, one launch (start us, length us, event | category | flops | bytes accessed | tf_op | source)
XLA Modules:
  0.0 109.9 jit_solution(16735130189715778489)
XLA Ops:
  0.0 3.0 %collective-permute-start = (bf16[128,2048]{1,0:T(8,128)(2,1)}, bf16[128,2048]{1,0:T(8,128)(2,1)S(1)}, u32[]{:S(2)}, u32[]{:S(2)}) collective-permute-start(bf16[128,2048]{1,0:T(8,128)(2,1)} %param.6), channel_id=1, source_target_pairs={{0,4},{4,0},{8,12},{12,8},{16,20},{20,16},{24,28},{28,24},{1,5},{5... | collective-permute-start | bytes 1572872 | tf_op jit(solution)/shard_map/ppermute | solution.py:25
  4.0 2.7 %collective-permute-start.7 = (bf16[64,2048]{1,0:T(8,128)(2,1)S(1)}, bf16[64,2048]{1,0:T(8,128)(2,1)S(1)}, u32[]{:S(2)}, u32[]{:S(2)}) collective-permute-start(bf16[64,2048]{1,0:T(8,128)(2,1)S(1)} %get-tuple-element.102.refs_0_), channel_id=1, source_target_pairs={{0,16},{4,20},{8,24},{12,28},{16,0},{20,4},{24,8},{28,12},{1,17},{... | collective-permute-start | bytes 786440 | tf_op jit(solution)/shard_map/ppermute | solution.py:25
  6.7 1.6 %collective-permute-start.1 = (bf16[64,2048]{1,0:T(8,128)(2,1)S(1)}, bf16[64,2048]{1,0:T(8,128)(2,1)S(1)}, u32[]{:S(2)}, u32[]{:S(2)}) collective-permute-start(bf16[64,2048]{1,0:T(8,128)(2,1)S(1)} %get-tuple-element.102.refs_0_), channel_id=1, source_target_pairs={{0,8},{4,12},{8,0},{12,4},{16,24},{20,28},{24,16},{28,20},{1,9},{5... | collective-permute-start | bytes 786440 | tf_op jit(solution)/shard_map/ppermute | solution.py:25
  12.8 5.7 %collective-permute-done.7.refs_7_ = bf16[64,2048]{1,0:T(8,128)(2,1)S(1)} collective-permute-done((bf16[64,2048]{1,0:T(8,128)(2,1)S(1)}, bf16[64,2048]{1,0:T(8,128)(2,1)S(1)}, u32[]{:S(2)}, u32[]{:S(2)}) %collective-permute-start.7) | collective-permute-done | bytes 262176 | tf_op jit(solution)/shard_map/ppermute | solution.py:25
  19.4 3.1 %collective-permute-start.2 = (bf16[64,2048]{1,0:T(8,128)(2,1)S(1)}, bf16[64,2048]{1,0:T(8,128)(2,1)S(1)}, u32[]{:S(2)}, u32[]{:S(2)}) collective-permute-start(bf16[64,2048]{1,0:T(8,128)(2,1)S(1)} %get-tuple-element.60.refs_1_), channel_id=1, source_target_pairs={{0,8},{4,12},{8,0},{12,4},{16,24},{20,28},{24,16},{28,20},{1,9},{5... | collective-permute-start | bytes 786440 | tf_op jit(solution)/shard_map/ppermute | solution.py:25
  23.6 1.6 %collective-permute-start.5 = (bf16[144,256]{1,0:T(8,128)(2,1)S(1)}, bf16[144,256]{1,0:T(8,128)(2,1)S(1)}, u32[]{:S(2)}, u32[]{:S(2)}) collective-permute-start(bf16[144,256]{1,0:T(8,128)(2,1)S(1)} %get-tuple-element.58), channel_id=1, source_target_pairs={{0,4},{4,0},{8,12},{12,8},{16,20},{20,16},{24,28},{28,24},{1,5},{5... | collective-permute-start | bytes 221192 | tf_op jit(solution)/shard_map/ppermute | solution.py:25
  25.7 6.5 %collective-permute-done.8.refs_8_ = bf16[64,2048]{1,0:T(8,128)(2,1)S(1)} collective-permute-done((bf16[64,2048]{1,0:T(8,128)(2,1)S(1)}, bf16[64,2048]{1,0:T(8,128)(2,1)S(1)}, u32[]{:S(2)}, u32[]{:S(2)}) %collective-permute-start.8) | collective-permute-done | bytes 262176 | tf_op jit(solution)/shard_map/ppermute | solution.py:25
  35.5 1.6 %collective-permute-start.13 = (bf16[128,512]{1,0:T(8,128)(2,1)S(1)}, bf16[128,512]{1,0:T(8,128)(2,1)S(1)}, u32[]{:S(2)}, u32[]{:S(2)}) collective-permute-start(bf16[128,512]{1,0:T(8,128)(2,1)S(1)} %pad_maximum_fusion), channel_id=1, source_target_pairs={{0,2},{1,3},{2,0},{3,1},{4,6},{5,7},{6,4},{7,5},{8,10},{9,11},{10,... | collective-permute-start | bytes 393224 | tf_op jit(solution)/shard_map/ppermute | solution.py:25
  37.0 2.0 %collective-permute-done.14.refs_0_ = bf16[64,2048]{1,0:T(8,128)(2,1)S(1)} collective-permute-done((bf16[64,2048]{1,0:T(8,128)(2,1)S(1)}, bf16[64,2048]{1,0:T(8,128)(2,1)S(1)}, u32[]{:S(2)}, u32[]{:S(2)}) %collective-permute-start.14) | collective-permute-done | bytes 262176 | tf_op jit(solution)/shard_map/ppermute | solution.py:25
  39.5 1.9 %collective-permute-start.16 = (bf16[64,2048]{1,0:T(8,128)(2,1)S(1)}, bf16[64,2048]{1,0:T(8,128)(2,1)S(1)}, u32[]{:S(2)}, u32[]{:S(2)}) collective-permute-start(bf16[64,2048]{1,0:T(8,128)(2,1)S(1)} %collective-permute-done.14.refs_0_), channel_id=1, source_target_pairs={{0,8},{4,12},{8,0},{12,4},{16,24},{20,28},{24,16},{28,20},{1,9},{5... | collective-permute-start | bytes 786440 | tf_op jit(solution)/shard_map/ppermute | solution.py:25
  41.4 3.2 %collective-permute-done.6.refs_6_ = bf16[64,2048]{1,0:T(8,128)(2,1)S(1)} collective-permute-done((bf16[64,2048]{1,0:T(8,128)(2,1)S(1)}, bf16[64,2048]{1,0:T(8,128)(2,1)S(1)}, u32[]{:S(2)}, u32[]{:S(2)}) %collective-permute-start.6) | collective-permute-done | bytes 262176 | tf_op jit(solution)/shard_map/ppermute | solution.py:25
  45.2 5.4 %collective-permute-done.11.came = bf16[80,512]{1,0:T(8,128)(2,1)S(1)} collective-permute-done((bf16[80,512]{1,0:T(8,128)(2,1)S(1)}, bf16[80,512]{1,0:T(8,128)(2,1)S(1)}, u32[]{:S(2)}, u32[]{:S(2)}) %collective-permute-start.11) | collective-permute-done | bytes 81952 | tf_op jit(solution)/shard_map/ppermute | solution.py:25
  51.2 2.9 %shard_map.68 = (bf16[768,2048]{1,0:T(8,128)(2,1)S(1)}, bf16[64,768]{1,0:T(8,128)(2,1)S(1)}, bf16[16,768]{1,0:T(8,128)(2,1)S(1)}, f32[64,768]{1,0:T(8,128)S(1)},...) custom-call(s32[4]{0:T(128)S(1)} %pad_add_fusion.scalars, bf16[64,2048]{1,0:T(8,128)(2,1)S(1)} %get-tuple-element.102.refs_0_, ...), custom_call_target="tpu_custom_call" | custom-call | tf_op jit(solution)/shard_map/pallas_call | solution.py:313
  54.2 1.6 %shard_map.69 = (bf16[256,2048]{1,0:T(8,128)(2,1)S(1)}, bf16[64,256]{1,0:T(8,128)(2,1)S(1)}, bf16[16,256]{1,0:T(8,128)(2,1)S(1)}, f32[64,256]{1,0:T(8,128)S(1)},...) custom-call(s32[4]{0:T(128)S(1)} %pad_add_fusion.scalars, bf16[64,2048]{1,0:T(8,128)(2,1)S(1)} %collective-permute-done.14.refs_0_, ...), custom_call_target="tpu_custom_call" | custom-call | tf_op jit(solution)/shard_map/pallas_call | solution.py:313
  55.9 1.5 %collective-permute-done.18.came = bf16[128,1024]{1,0:T(8,128)(2,1)S(1)} collective-permute-done((bf16[128,1024]{1,0:T(8,128)(2,1)S(1)}, bf16[128,1024]{1,0:T(8,128)(2,1)S(1)}, u32[]{:S(2)}, u32[]{:S(2)}) %collective-permute-start.18) | collective-permute-done | bytes 262176 | tf_op jit(solution)/shard_map/ppermute | solution.py:25
  57.5 1.9 %shard_map.71 = (bf16[512,2048]{1,0:T(8,128)(2,1)S(1)}, bf16[128,512]{1,0:T(8,128)(2,1)S(1)}, bf16[512,2048]{1,0:T(8,128)(2,1)S(1)}, bf16[128,512]{1,0:T(8,128)(2,1)S(1)}) custom-call(s32[4]{0:T(128)S(1)} %pad_add_fusion.scalars, f32[2]{0:T(128)S(1)} %copy-done.2, bf16[768,2048]{1,0:T(8,128)(2,1)S(1)} %get-tuple-element.71.refs_0_, ...), custom_call_target="tpu_custom_call" | custom-call | tf_op jit(solution)/shard_map/pallas_call | solution.py:313
  59.6 1.5 %collective-permute-start.21 = (bf16[128,1024]{1,0:T(8,128)(2,1)S(1)}, bf16[128,1024]{1,0:T(8,128)(2,1)S(1)}, u32[]{:S(2)}, u32[]{:S(2)}) collective-permute-start(bf16[128,1024]{1,0:T(8,128)(2,1)S(1)} %get-tuple-element.92), channel_id=1, source_target_pairs={{0,2},{1,3},{2,0},{3,1},{4,6},{5,7},{6,4},{7,5},{8,10},{9,11},{10,... | collective-permute-start | bytes 786440 | tf_op jit(solution)/shard_map/ppermute | solution.py:25
  61.2 7.0 %collective-permute-done.21.came = bf16[128,1024]{1,0:T(8,128)(2,1)S(1)} collective-permute-done((bf16[128,1024]{1,0:T(8,128)(2,1)S(1)}, bf16[128,1024]{1,0:T(8,128)(2,1)S(1)}, u32[]{:S(2)}, u32[]{:S(2)}) %collective-permute-start.21) | collective-permute-done | bytes 262176 | tf_op jit(solution)/shard_map/ppermute | solution.py:25
  70.2 2.9 %shard_map.73 = (bf16[64,2048]{1,0:T(8,128)(2,1)S(1)}, f32[64,2048]{1,0:T(8,128)S(1)}) custom-call(s32[4]{0:T(128)S(1)} %pad_add_fusion.scalars, bf16[512,2048]{1,0:T(8,128)(2,1)S(1)} %get-tuple-element.88.refs_0_, bf16[128,512]{1,0:T(8,128)(2,1)S(1)} %get-tuple-element.89.refs_1_, bf16[512,2048]{1,0:T(8,128)(2,1)S(1)} %collective-permute-done.19.refs_2_, ...), custom_call_target="tpu_custom_call" | custom-call | tf_op jit(solution)/shard_map/pallas_call | solution.py:313
  73.1 1.6 %collective-permute-start.23 = (bf16[64,2048]{1,0:T(8,128)(2,1)S(1)}, bf16[64,2048]{1,0:T(8,128)(2,1)S(1)}, u32[]{:S(2)}, u32[]{:S(2)}) collective-permute-start(bf16[64,2048]{1,0:T(8,128)(2,1)S(1)} %get-tuple-element.96), channel_id=1, source_target_pairs={{0,2},{1,3},{2,0},{3,1},{4,6},{5,7},{6,4},{7,5},{8,10},{9,11},{10,... | collective-permute-start | bytes 786440 | tf_op jit(solution)/shard_map/ppermute | solution.py:25
  74.7 6.9 %collective-permute-done.23.refs_6_ = bf16[64,2048]{1,0:T(8,128)(2,1)S(1)} collective-permute-done((bf16[64,2048]{1,0:T(8,128)(2,1)S(1)}, bf16[64,2048]{1,0:T(8,128)(2,1)S(1)}, u32[]{:S(2)}, u32[]{:S(2)}) %collective-permute-start.23) | collective-permute-done | bytes 262176 | tf_op jit(solution)/shard_map/ppermute | solution.py:25
  81.5 2.9 %shard_map.74 = (bf16[64,1024]{1,0:T(8,128)(2,1)S(1)}, f32[64,1024]{1,0:T(8,128)S(1)}) custom-call(s32[4]{0:T(128)S(1)} %pad_add_fusion.scalars, bf16[512,2048]{1,0:T(8,128)(2,1)S(1)} %get-tuple-element.88.refs_0_, bf16[128,512]{1,0:T(8,128)(2,1)S(1)} %get-tuple-element.89.refs_1_, bf16[512,2048]{1,0:T(8,128)(2,1)S(1)} %collective-permute-done.19.refs_2_, ...), custom_call_target="tpu_custom_call" | custom-call | tf_op jit(solution)/shard_map/pallas_call | solution.py:313
  84.5 1.3 %collective-permute-done.24.came = bf16[64,1024]{1,0:T(8,128)(2,1)S(1)} collective-permute-done((bf16[64,1024]{1,0:T(8,128)(2,1)S(1)}, bf16[64,1024]{1,0:T(8,128)(2,1)S(1)}, u32[]{:S(2)}, u32[]{:S(2)}) %collective-permute-start.24) | collective-permute-done | bytes 131104 | tf_op jit(solution)/shard_map/ppermute | solution.py:25
  86.4 1.6 %collective-permute-start.25 = (bf16[64,512]{1,0:T(8,128)(2,1)S(1)}, bf16[64,512]{1,0:T(8,128)(2,1)S(1)}, u32[]{:S(2)}, u32[]{:S(2)}) collective-permute-start(bf16[64,512]{1,0:T(8,128)(2,1)S(1)} %get-tuple-element.100), channel_id=1, source_target_pairs={{0,2},{1,3},{2,0},{3,1},{4,6},{5,7},{6,4},{7,5},{8,10},{9,11},{10,... | collective-permute-start | bytes 196616 | tf_op jit(solution)/shard_map/ppermute | solution.py:25
  88.0 2.8 %collective-permute-done.25.came = bf16[64,512]{1,0:T(8,128)(2,1)S(1)} collective-permute-done((bf16[64,512]{1,0:T(8,128)(2,1)S(1)}, bf16[64,512]{1,0:T(8,128)(2,1)S(1)}, u32[]{:S(2)}, u32[]{:S(2)}) %collective-permute-start.25) | collective-permute-done | bytes 65568 | tf_op jit(solution)/shard_map/ppermute | solution.py:25
  90.8 3.0 %collective-permute-start.26 = (bf16[64,512]{1,0:T(8,128)(2,1)S(1)}, bf16[64,512]{1,0:T(8,128)(2,1)S(1)}, u32[]{:S(2)}, u32[]{:S(2)}) collective-permute-start(bf16[64,512]{1,0:T(8,128)(2,1)S(1)} %shard_map.76.refs_0_), channel_id=1, source_target_pairs={{0,28},{4,24},{8,20},{12,16},{16,12},{20,8},{24,4},{28,0},{1,29},{... | collective-permute-start | bytes 196616 | tf_op jit(solution)/shard_map/ppermute | solution.py:25
  93.8 1.8 %collective-permute-start.27 = (bf16[64,512]{1,0:T(8,128)(2,1)S(1)}, bf16[64,512]{1,0:T(8,128)(2,1)S(1)}, u32[]{:S(2)}, u32[]{:S(2)}) collective-permute-start(bf16[64,512]{1,0:T(8,128)(2,1)S(1)} %shard_map.76.refs_0_), channel_id=1, source_target_pairs={{0,24},{4,28},{8,16},{12,20},{16,8},{20,12},{24,0},{28,4},{1,25},{... | collective-permute-start | bytes 196616 | tf_op jit(solution)/shard_map/ppermute | solution.py:25
  95.6 1.7 %collective-permute-start.28 = (bf16[64,512]{1,0:T(8,128)(2,1)S(1)}, bf16[64,512]{1,0:T(8,128)(2,1)S(1)}, u32[]{:S(2)}, u32[]{:S(2)}) collective-permute-start(bf16[64,512]{1,0:T(8,128)(2,1)S(1)} %shard_map.76.refs_0_), channel_id=1, source_target_pairs={{0,20},{4,16},{8,28},{12,24},{16,4},{20,0},{24,12},{28,8},{1,21},{... | collective-permute-start | bytes 196616 | tf_op jit(solution)/shard_map/ppermute | solution.py:25
  98.5 2.2 %collective-permute-start.30 = (bf16[64,512]{1,0:T(8,128)(2,1)S(1)}, bf16[64,512]{1,0:T(8,128)(2,1)S(1)}, u32[]{:S(2)}, u32[]{:S(2)}) collective-permute-start(bf16[64,512]{1,0:T(8,128)(2,1)S(1)} %shard_map.76.refs_0_), channel_id=1, source_target_pairs={{0,12},{4,8},{8,4},{12,0},{16,28},{20,24},{24,20},{28,16},{1,13},{... | collective-permute-start | bytes 196616 | tf_op jit(solution)/shard_map/ppermute | solution.py:25
  100.7 3.2 %collective-permute-start.31 = (bf16[64,512]{1,0:T(8,128)(2,1)S(1)}, bf16[64,512]{1,0:T(8,128)(2,1)S(1)}, u32[]{:S(2)}, u32[]{:S(2)}) collective-permute-start(bf16[64,512]{1,0:T(8,128)(2,1)S(1)} %shard_map.76.refs_0_), channel_id=1, source_target_pairs={{0,8},{4,12},{8,0},{12,4},{16,24},{20,28},{24,16},{28,20},{1,9},{5... | collective-permute-start | bytes 196616 | tf_op jit(solution)/shard_map/ppermute | solution.py:25
  104.2 2.4 %collective-permute-done.28.refs_3_ = bf16[64,512]{1,0:T(8,128)(2,1)S(1)} collective-permute-done((bf16[64,512]{1,0:T(8,128)(2,1)S(1)}, bf16[64,512]{1,0:T(8,128)(2,1)S(1)}, u32[]{:S(2)}, u32[]{:S(2)}) %collective-permute-start.28) | collective-permute-done | bytes 65568 | tf_op jit(solution)/shard_map/ppermute | solution.py:25
  108.1 1.7 %shard_map.77 = f32[512,512]{1,0:T(8,128)} custom-call(s32[4]{0:T(128)S(1)} %pad_add_fusion.scalars, bf16[64,512]{1,0:T(8,128)(2,1)S(1)} %shard_map.76.refs_0_, bf16[64,512]{1,0:T(8,128)(2,1)S(1)} %collective-permute-done.26.refs_1_, bf16[64,512]{1,0:T(8,128)(2,1)S(1)} %collective-permute-done.27.refs_2_, ...), custom_call_target="tpu_custom_call" | custom-call | tf_op jit(solution)/shard_map/pallas_call | solution.py:313
  (60 shorter events, 18.1 us)
Async XLA Ops:
  0.0 22.5 %collective-permute-start = (bf16[128,2048]{1,0:T(8,128)(2,1)}, bf16[128,2048]{1,0:T(8,128)(2,1)S(1)}, u32[]{:S(2)}, u32[]{:S(2)}) collective-permute-start(bf16[128,2048]{1,0:T(8,128)(2,1)} %param.6), channel_id=1, source_target_pairs={{0,4},{4,0},{8,12},{12,8},{16,20},{20,16},{24,28},{28,24},{1,5},{5... | collective-permute-start | bytes 1572872 | tf_op jit(solution)/shard_map/ppermute | solution.py:25
  4.0 14.5 %collective-permute-start.7 = (bf16[64,2048]{1,0:T(8,128)(2,1)S(1)}, bf16[64,2048]{1,0:T(8,128)(2,1)S(1)}, u32[]{:S(2)}, u32[]{:S(2)}) collective-permute-start(bf16[64,2048]{1,0:T(8,128)(2,1)S(1)} %get-tuple-element.102.refs_0_), channel_id=1, source_target_pairs={{0,16},{4,20},{8,24},{12,28},{16,0},{20,4},{24,8},{28,12},{1,17},{... | collective-permute-start | bytes 786440 | tf_op jit(solution)/shard_map/ppermute | solution.py:25
  6.7 12.7 %collective-permute-start.1 = (bf16[64,2048]{1,0:T(8,128)(2,1)S(1)}, bf16[64,2048]{1,0:T(8,128)(2,1)S(1)}, u32[]{:S(2)}, u32[]{:S(2)}) collective-permute-start(bf16[64,2048]{1,0:T(8,128)(2,1)S(1)} %get-tuple-element.102.refs_0_), channel_id=1, source_target_pairs={{0,8},{4,12},{8,0},{12,4},{16,24},{20,28},{24,16},{28,20},{1,9},{5... | collective-permute-start | bytes 786440 | tf_op jit(solution)/shard_map/ppermute | solution.py:25
  12.3 10.2 %collective-permute-start.3 = (bf16[272,128]{1,0:T(8,128)(2,1)S(1)}, bf16[272,128]{1,0:T(8,128)(2,1)S(1)}, u32[]{:S(2)}, u32[]{:S(2)}) collective-permute-start(bf16[272,128]{1,0:T(8,128)(2,1)S(1)} %get-tuple-element.54), channel_id=1, source_target_pairs={{0,8},{4,12},{8,0},{12,4},{16,24},{20,28},{24,16},{28,20},{1,9},{5... | collective-permute-start | bytes 208904 | tf_op jit(solution)/shard_map/ppermute | solution.py:25
  18.5 13.7 %collective-permute-start.8 = (bf16[64,2048]{1,0:T(8,128)(2,1)S(1)}, bf16[64,2048]{1,0:T(8,128)(2,1)S(1)}, u32[]{:S(2)}, u32[]{:S(2)}) collective-permute-start(bf16[64,2048]{1,0:T(8,128)(2,1)S(1)} %get-tuple-element.60.refs_1_), channel_id=1, source_target_pairs={{0,16},{4,20},{8,24},{12,28},{16,0},{20,4},{24,8},{28,12},{1,17},{... | collective-permute-start | bytes 786440 | tf_op jit(solution)/shard_map/ppermute | solution.py:25
  19.4 14.0 %collective-permute-start.2 = (bf16[64,2048]{1,0:T(8,128)(2,1)S(1)}, bf16[64,2048]{1,0:T(8,128)(2,1)S(1)}, u32[]{:S(2)}, u32[]{:S(2)}) collective-permute-start(bf16[64,2048]{1,0:T(8,128)(2,1)S(1)} %get-tuple-element.60.refs_1_), channel_id=1, source_target_pairs={{0,8},{4,12},{8,0},{12,4},{16,24},{20,28},{24,16},{28,20},{1,9},{5... | collective-permute-start | bytes 786440 | tf_op jit(solution)/shard_map/ppermute | solution.py:25
  22.6 10.8 %collective-permute-start.4 = (bf16[64,2048]{1,0:T(8,128)(2,1)S(1)}, bf16[64,2048]{1,0:T(8,128)(2,1)S(1)}, u32[]{:S(2)}, u32[]{:S(2)}) collective-permute-start(bf16[64,2048]{1,0:T(8,128)(2,1)S(1)} %collective-permute-done.1.refs_3_), channel_id=1, source_target_pairs={{0,4},{4,0},{8,12},{12,8},{16,20},{20,16},{24,28},{28,24},{1,5},{5... | collective-permute-start | bytes 786440 | tf_op jit(solution)/shard_map/ppermute | solution.py:25
  23.6 9.7 %collective-permute-start.5 = (bf16[144,256]{1,0:T(8,128)(2,1)S(1)}, bf16[144,256]{1,0:T(8,128)(2,1)S(1)}, u32[]{:S(2)}, u32[]{:S(2)}) collective-permute-start(bf16[144,256]{1,0:T(8,128)(2,1)S(1)} %get-tuple-element.58), channel_id=1, source_target_pairs={{0,4},{4,0},{8,12},{12,8},{16,20},{20,16},{24,28},{28,24},{1,5},{5... | collective-permute-start | bytes 221192 | tf_op jit(solution)/shard_map/ppermute | solution.py:25
  25.2 13.8 %collective-permute-start.14 = (bf16[64,2048]{1,0:T(8,128)(2,1)S(1)}, bf16[64,2048]{1,0:T(8,128)(2,1)S(1)}, u32[]{:S(2)}, u32[]{:S(2)}) collective-permute-start(bf16[64,2048]{1,0:T(8,128)(2,1)S(1)} %collective-permute-done.7.refs_7_), channel_id=1, source_target_pairs={{0,4},{4,0},{8,12},{12,8},{16,20},{20,16},{24,28},{28,24},{1,5},{5... | collective-permute-start | bytes 786440 | tf_op jit(solution)/shard_map/ppermute | solution.py:25
  32.2 7.3 %collective-permute-start.10 = (bf16[64,2048]{1,0:T(8,128)(2,1)S(1)}, bf16[64,2048]{1,0:T(8,128)(2,1)S(1)}, u32[]{:S(2)}, u32[]{:S(2)}) collective-permute-start(bf16[64,2048]{1,0:T(8,128)(2,1)S(1)} %collective-permute-done.8.refs_8_), channel_id=1, source_target_pairs={{0,8},{4,12},{8,0},{12,4},{16,24},{20,28},{24,16},{28,20},{1,9},{5... | collective-permute-start | bytes 786440 | tf_op jit(solution)/shard_map/ppermute | solution.py:25
  33.4 11.2 %collective-permute-start.6 = (bf16[64,2048]{1,0:T(8,128)(2,1)S(1)}, bf16[64,2048]{1,0:T(8,128)(2,1)S(1)}, u32[]{:S(2)}, u32[]{:S(2)}) collective-permute-start(bf16[64,2048]{1,0:T(8,128)(2,1)S(1)} %collective-permute-done.2.refs_4_), channel_id=1, source_target_pairs={{0,4},{4,0},{8,12},{12,8},{16,20},{20,16},{24,28},{28,24},{1,5},{5... | collective-permute-start | bytes 786440 | tf_op jit(solution)/shard_map/ppermute | solution.py:25
  33.9 1.6 %collective-permute-start.12 = (bf16[64,512]{1,0:T(8,128)(2,1)S(1)}, bf16[64,512]{1,0:T(8,128)(2,1)S(1)}, u32[]{:S(2)}, u32[]{:S(2)}) collective-permute-start(bf16[64,512]{1,0:T(8,128)(2,1)S(1)} %get-tuple-element.70), channel_id=1, source_target_pairs={{0,1},{1,0},{2,3},{3,2},{4,5},{5,4},{6,7},{7,6},{8,9},{9,8},{10,11... | collective-permute-start | bytes 196616 | tf_op jit(solution)/shard_map/ppermute | solution.py:25
  34.5 16.8 %collective-permute-start.9 = (bf16[64,2048]{1,0:T(8,128)(2,1)S(1)}, bf16[64,2048]{1,0:T(8,128)(2,1)S(1)}, u32[]{:S(2)}, u32[]{:S(2)}) collective-permute-start(bf16[64,2048]{1,0:T(8,128)(2,1)S(1)} %collective-permute-done.7.refs_7_), channel_id=1, source_target_pairs={{0,8},{4,12},{8,0},{12,4},{16,24},{20,28},{24,16},{28,20},{1,9},{5... | collective-permute-start | bytes 786440 | tf_op jit(solution)/shard_map/ppermute | solution.py:25
  35.5 9.7 %collective-permute-start.13 = (bf16[128,512]{1,0:T(8,128)(2,1)S(1)}, bf16[128,512]{1,0:T(8,128)(2,1)S(1)}, u32[]{:S(2)}, u32[]{:S(2)}) collective-permute-start(bf16[128,512]{1,0:T(8,128)(2,1)S(1)} %pad_maximum_fusion), channel_id=1, source_target_pairs={{0,2},{1,3},{2,0},{3,1},{4,6},{5,7},{6,4},{7,5},{8,10},{9,11},{10,... | collective-permute-start | bytes 393224 | tf_op jit(solution)/shard_map/ppermute | solution.py:25
  39.0 15.1 %collective-permute-start.15 = (bf16[64,2048]{1,0:T(8,128)(2,1)S(1)}, bf16[64,2048]{1,0:T(8,128)(2,1)S(1)}, u32[]{:S(2)}, u32[]{:S(2)}) collective-permute-start(bf16[64,2048]{1,0:T(8,128)(2,1)S(1)} %collective-permute-done.8.refs_8_), channel_id=1, source_target_pairs={{0,4},{4,0},{8,12},{12,8},{16,20},{20,16},{24,28},{28,24},{1,5},{5... | collective-permute-start | bytes 786440 | tf_op jit(solution)/shard_map/ppermute | solution.py:25
  39.5 14.6 %collective-permute-start.16 = (bf16[64,2048]{1,0:T(8,128)(2,1)S(1)}, bf16[64,2048]{1,0:T(8,128)(2,1)S(1)}, u32[]{:S(2)}, u32[]{:S(2)}) collective-permute-start(bf16[64,2048]{1,0:T(8,128)(2,1)S(1)} %collective-permute-done.14.refs_0_), channel_id=1, source_target_pairs={{0,8},{4,12},{8,0},{12,4},{16,24},{20,28},{24,16},{28,20},{1,9},{5... | collective-permute-start | bytes 786440 | tf_op jit(solution)/shard_map/ppermute | solution.py:25
  44.6 9.6 %collective-permute-start.17 = (bf16[64,2048]{1,0:T(8,128)(2,1)S(1)}, bf16[64,2048]{1,0:T(8,128)(2,1)S(1)}, u32[]{:S(2)}, u32[]{:S(2)}) collective-permute-start(bf16[64,2048]{1,0:T(8,128)(2,1)S(1)} %collective-permute-done.10.refs_10_), channel_id=1, source_target_pairs={{0,4},{4,0},{8,12},{12,8},{16,20},{20,16},{24,28},{28,24},{1,5},{5... | collective-permute-start | bytes 786440 | tf_op jit(solution)/shard_map/ppermute | solution.py:25
  45.1 5.5 %collective-permute-start.11 = (bf16[80,512]{1,0:T(8,128)(2,1)S(1)}, bf16[80,512]{1,0:T(8,128)(2,1)S(1)}, u32[]{:S(2)}, u32[]{:S(2)}) collective-permute-start(bf16[80,512]{1,0:T(8,128)(2,1)S(1)} %get-tuple-element.66), channel_id=1, source_target_pairs={{0,16},{4,20},{8,24},{12,28},{16,0},{20,4},{24,8},{28,12},{1,17},{... | collective-permute-start | bytes 245768 | tf_op jit(solution)/shard_map/ppermute | solution.py:25
  55.8 1.6 %collective-permute-start.18 = (bf16[128,1024]{1,0:T(8,128)(2,1)S(1)}, bf16[128,1024]{1,0:T(8,128)(2,1)S(1)}, u32[]{:S(2)}, u32[]{:S(2)}) collective-permute-start(bf16[128,1024]{1,0:T(8,128)(2,1)S(1)} %get-tuple-element.80), channel_id=1, source_target_pairs={{0,1},{1,0},{2,3},{3,2},{4,5},{5,4},{6,7},{7,6},{8,9},{9,8},{10,11... | collective-permute-start | bytes 786440 | tf_op jit(solution)/shard_map/ppermute | solution.py:25
  59.4 10.9 %collective-permute-start.19 = (bf16[512,2048]{1,0:T(8,128)(2,1)S(1)}, bf16[512,2048]{1,0:T(8,128)(2,1)S(1)}, u32[]{:S(2)}, u32[]{:S(2)}) collective-permute-start(bf16[512,2048]{1,0:T(8,128)(2,1)S(1)} %get-tuple-element.90), channel_id=1, source_target_pairs={{0,1},{1,0},{2,3},{3,2},{4,5},{5,4},{6,7},{7,6},{8,9},{9,8},{10,11... | collective-permute-start | bytes 6291464 | tf_op jit(solution)/shard_map/ppermute | solution.py:25
  59.6 8.6 %collective-permute-start.21 = (bf16[128,1024]{1,0:T(8,128)(2,1)S(1)}, bf16[128,1024]{1,0:T(8,128)(2,1)S(1)}, u32[]{:S(2)}, u32[]{:S(2)}) collective-permute-start(bf16[128,1024]{1,0:T(8,128)(2,1)S(1)} %get-tuple-element.92), channel_id=1, source_target_pairs={{0,2},{1,3},{2,0},{3,1},{4,6},{5,7},{6,4},{7,5},{8,10},{9,11},{10,... | collective-permute-start | bytes 786440 | tf_op jit(solution)/shard_map/ppermute | solution.py:25
  61.1 7.8 %collective-permute-start.20 = (bf16[128,512]{1,0:T(8,128)(2,1)S(1)}, bf16[128,512]{1,0:T(8,128)(2,1)S(1)}, u32[]{:S(2)}, u32[]{:S(2)}) collective-permute-start(bf16[128,512]{1,0:T(8,128)(2,1)S(1)} %get-tuple-element.91), channel_id=1, source_target_pairs={{0,1},{1,0},{2,3},{3,2},{4,5},{5,4},{6,7},{7,6},{8,9},{9,8},{10,11... | collective-permute-start | bytes 393224 | tf_op jit(solution)/shard_map/ppermute | solution.py:25
  68.8 1.4 %collective-permute-start.22 = (bf16[64,1024]{1,0:T(8,128)(2,1)S(1)}, bf16[64,1024]{1,0:T(8,128)(2,1)S(1)}, u32[]{:S(2)}, u32[]{:S(2)}) collective-permute-start(bf16[64,1024]{1,0:T(8,128)(2,1)S(1)} %get-tuple-element.94), channel_id=1, source_target_pairs={{0,1},{1,0},{2,3},{3,2},{4,5},{5,4},{6,7},{7,6},{8,9},{9,8},{10,11... | collective-permute-start | bytes 393224 | tf_op jit(solution)/shard_map/ppermute | solution.py:25
  73.1 8.4 %collective-permute-start.23 = (bf16[64,2048]{1,0:T(8,128)(2,1)S(1)}, bf16[64,2048]{1,0:T(8,128)(2,1)S(1)}, u32[]{:S(2)}, u32[]{:S(2)}) collective-permute-start(bf16[64,2048]{1,0:T(8,128)(2,1)S(1)} %get-tuple-element.96), channel_id=1, source_target_pairs={{0,2},{1,3},{2,0},{3,1},{4,6},{5,7},{6,4},{7,5},{8,10},{9,11},{10,... | collective-permute-start | bytes 786440 | tf_op jit(solution)/shard_map/ppermute | solution.py:25
  86.4 4.3 %collective-permute-start.25 = (bf16[64,512]{1,0:T(8,128)(2,1)S(1)}, bf16[64,512]{1,0:T(8,128)(2,1)S(1)}, u32[]{:S(2)}, u32[]{:S(2)}) collective-permute-start(bf16[64,512]{1,0:T(8,128)(2,1)S(1)} %get-tuple-element.100), channel_id=1, source_target_pairs={{0,2},{1,3},{2,0},{3,1},{4,6},{5,7},{6,4},{7,5},{8,10},{9,11},{10,... | collective-permute-start | bytes 196616 | tf_op jit(solution)/shard_map/ppermute | solution.py:25
  90.8 9.9 %collective-permute-start.26 = (bf16[64,512]{1,0:T(8,128)(2,1)S(1)}, bf16[64,512]{1,0:T(8,128)(2,1)S(1)}, u32[]{:S(2)}, u32[]{:S(2)}) collective-permute-start(bf16[64,512]{1,0:T(8,128)(2,1)S(1)} %shard_map.76.refs_0_), channel_id=1, source_target_pairs={{0,28},{4,24},{8,20},{12,16},{16,12},{20,8},{24,4},{28,0},{1,29},{... | collective-permute-start | bytes 196616 | tf_op jit(solution)/shard_map/ppermute | solution.py:25
  93.8 10.1 %collective-permute-start.27 = (bf16[64,512]{1,0:T(8,128)(2,1)S(1)}, bf16[64,512]{1,0:T(8,128)(2,1)S(1)}, u32[]{:S(2)}, u32[]{:S(2)}) collective-permute-start(bf16[64,512]{1,0:T(8,128)(2,1)S(1)} %shard_map.76.refs_0_), channel_id=1, source_target_pairs={{0,24},{4,28},{8,16},{12,20},{16,8},{20,12},{24,0},{28,4},{1,25},{... | collective-permute-start | bytes 196616 | tf_op jit(solution)/shard_map/ppermute | solution.py:25
  95.6 11.1 %collective-permute-start.28 = (bf16[64,512]{1,0:T(8,128)(2,1)S(1)}, bf16[64,512]{1,0:T(8,128)(2,1)S(1)}, u32[]{:S(2)}, u32[]{:S(2)}) collective-permute-start(bf16[64,512]{1,0:T(8,128)(2,1)S(1)} %shard_map.76.refs_0_), channel_id=1, source_target_pairs={{0,20},{4,16},{8,28},{12,24},{16,4},{20,0},{24,12},{28,8},{1,21},{... | collective-permute-start | bytes 196616 | tf_op jit(solution)/shard_map/ppermute | solution.py:25
  97.2 9.4 %collective-permute-start.29 = (bf16[64,512]{1,0:T(8,128)(2,1)S(1)}, bf16[64,512]{1,0:T(8,128)(2,1)S(1)}, u32[]{:S(2)}, u32[]{:S(2)}) collective-permute-start(bf16[64,512]{1,0:T(8,128)(2,1)S(1)} %shard_map.76.refs_0_), channel_id=1, source_target_pairs={{0,16},{4,20},{8,24},{12,28},{16,0},{20,4},{24,8},{28,12},{1,17},{... | collective-permute-start | bytes 196616 | tf_op jit(solution)/shard_map/ppermute | solution.py:25
  98.5 8.2 %collective-permute-start.30 = (bf16[64,512]{1,0:T(8,128)(2,1)S(1)}, bf16[64,512]{1,0:T(8,128)(2,1)S(1)}, u32[]{:S(2)}, u32[]{:S(2)}) collective-permute-start(bf16[64,512]{1,0:T(8,128)(2,1)S(1)} %shard_map.76.refs_0_), channel_id=1, source_target_pairs={{0,12},{4,8},{8,4},{12,0},{16,28},{20,24},{24,20},{28,16},{1,13},{... | collective-permute-start | bytes 196616 | tf_op jit(solution)/shard_map/ppermute | solution.py:25
  100.7 6.4 %collective-permute-start.31 = (bf16[64,512]{1,0:T(8,128)(2,1)S(1)}, bf16[64,512]{1,0:T(8,128)(2,1)S(1)}, u32[]{:S(2)}, u32[]{:S(2)}) collective-permute-start(bf16[64,512]{1,0:T(8,128)(2,1)S(1)} %shard_map.76.refs_0_), channel_id=1, source_target_pairs={{0,8},{4,12},{8,0},{12,4},{16,24},{20,28},{24,16},{28,20},{1,9},{5... | collective-permute-start | bytes 196616 | tf_op jit(solution)/shard_map/ppermute | solution.py:25
  103.9 4.3 %collective-permute-start.32 = (bf16[64,512]{1,0:T(8,128)(2,1)S(1)}, bf16[64,512]{1,0:T(8,128)(2,1)S(1)}, u32[]{:S(2)}, u32[]{:S(2)}) collective-permute-start(bf16[64,512]{1,0:T(8,128)(2,1)S(1)} %shard_map.76.refs_0_), channel_id=1, source_target_pairs={{0,4},{4,0},{8,12},{12,8},{16,20},{20,16},{24,28},{28,24},{1,5},{5... | collective-permute-start | bytes 196616 | tf_op jit(solution)/shard_map/ppermute | solution.py:25
  (4 other events, 6.7 us)

commit v5 on v4

--- a/solution.py
+++ b/solution.py
@@ -69,25 +69,6 @@
             out[:, place] = term.astype(out.dtype)
 
 
-def in_tiles(held, sums, keep, body):
-    tile = min(held.shape[0], 1024)
-    if held.shape[0] == tile:
-        body(pl.ds(0, tile), None)
-        return
-    sums[...] = jnp.zeros_like(sums)
-    keep[...] = jnp.zeros_like(keep)
-
-    def step(i, none):
-        body(pl.ds(pl.multiple_of(i * tile, tile), tile), (sums, keep))
-
-    lax.fori_loop(0, held.shape[0] // tile, step, None)
-
-
-def of_copy(value, hots):
-    wide = value.shape[0] // len(hots)
-    return sum(value[c * wide : (c + 1) * wide] * hot for c, hot in enumerate(hots))
-
-
 def by_copy(delta, hots):
     delta = delta.astype(F32)
     return jnp.concatenate([delta * hot for hot in hots], 0).astype(BF)
@@ -127,58 +108,98 @@
         sent[0][pl.ds(half // 2, 16), :] = new_labels[...]
 
 
-def first_kernel(sizes, places, last, scalars, *refs):
-    part, pairs, copies, length = sizes
-    refs, outs = refs[:-6], refs[-6:]
-    before, refs = (refs[-2:], refs[:-2]) if last else (None, refs)
-    pieces, (all_up, all_labels, weight) = refs[:-3], refs[-3:]
-    held, up, labels, primal_out, sums, keep = outs
-    quarter = scalars[1]
-    wide = up.shape[0]
+def put_together(pieces, held):
     row = 0
     for piece in pieces:
         held[pl.ds(row, piece.shape[0]), :] = piece[...]
         row += piece.shape[0]
-    rows = held.shape[0] // len(places)
+
+
+def times_weight(quarter, part, weight, held, rows):
+    wide = weight.shape[0] * part // held.shape[1]
+    total = None
+    for i in range(weight.shape[0] // wide):
+        columns = pl.ds(pl.multiple_of((quarter ^ i) * part, part), part)
+        term = lax.dot_general(
+            weight[pl.ds(i * wide, wide), :],
+            held[rows, columns],
+            (((1,), (1,)), ((), ())),
+            preferred_element_type=F32,
+        )
+        total = term if total is None else total + term
+    return total
+
+
+def tiles_of(held, body):
+    tile = min(held.shape[0], 1024)
+    if held.shape[0] == tile:
+        body(pl.ds(0, tile), False)
+        return
+
+    def step(i, none):
+        body(pl.ds(pl.multiple_of(i * tile, tile), tile), True)
+
+    lax.fori_loop(0, held.shape[0] // tile, step, None)
+
+
+def primal_kernel(part, scalars, *refs):
+    pieces, (weight, held, primal) = refs[:-3], refs[-3:]
+    put_together(pieces, held)
+
+    def body(rows, _):
+        primal[:, rows] = times_weight(scalars[1], part, weight, held, rows)
+
+    tiles_of(held, body)
+
+
+def first_kernel(sizes, places, scalars, *refs):
+    part, pairs, copies, length = sizes
+    pieces, refs = refs[:-12], refs[-12:]
+    all_up, all_labels, weight, held_early, primal_early, *refs = refs
+    held_late, primal_late, up, labels, send, keep, sums = refs
+    quarter = scalars[1]
+    put_together(pieces, held_late)
+    primal_late[...] = times_weight(quarter, part, weight, held_late, pl.ds(0, held_late.shape[0]))
+    rows = up.shape[1] // len(places)
     for i, place in enumerate(places):
         up[:, pl.ds(i * rows, rows)] = all_up[:, pl.ds(place * rows, rows)]
         labels[:, pl.ds(i * rows, rows)] = all_labels[:, pl.ds(place * rows, rows)]
 
-    def body(rows, prior):
-        primal = None
-        for i in range(2 * pairs):
-            columns = pl.ds(pl.multiple_of((quarter ^ i) * part, part), part)
-            term = lax.dot_general(
-                weight[pl.ds(i * wide, wide), :],
-                held[rows, columns],
-                (((1,), (1,)), ((), ())),
-                preferred_element_type=F32,
-            )
-            primal = term if primal is None else primal + term
-        primal_out[:, rows] = primal
-        hots = onehots(labels[:, rows], copies)
-        forget = labels[0:1, rows].astype(F32)
-        delta = (forget * up[:, rows].astype(F32) * first_slope(primal) / length).astype(BF)
-        contract(quarter % 2, part, pairs, by_copy(delta, hots), held, rows, sums, keep, prior)
-
-    if last:
-        body(pl.ds(0, held.shape[0]), before)
-    else:
-        in_tiles(held, sums, keep, body)
+    def terms(held, primal, rows, start, send, before):
+        lanes = pl.ds(start + rows.start, rows.size)
+        hots = onehots(labels[:, lanes], copies)
+        forget = labels[0:1, lanes].astype(F32)
+        slope = first_slope(primal[:, rows])
+        delta = (forget * up[:, lanes].astype(F32) * slope / length).astype(BF)
+        contract(quarter % 2, part, pairs, by_copy(delta, hots), held, rows, send, keep, before)
+
+    if held_early.shape[0] > 1024:
+        sums[...] = jnp.zeros_like(sums)
+        keep[...] = jnp.zeros_like(keep)
+
+    def body(rows, more):
+        terms(held_early, primal_early, rows, 0, sums, (sums, keep) if more else None)
+
+    tiles_of(held_early, body)
+    every = pl.ds(0, held_late.shape[0])
+    terms(held_late, primal_late, every, held_early.shape[0], send, (sums, keep))
 
 
 def sort_kernel(sizes, rows, scalars, rate, *refs):
     part, pairs, copies, length = sizes
-    early, late, (own, own_side, sent, sent_side) = refs[:4], refs[4:8], refs[8:]
+    early, late, (up, labels, own, own_side, sent_side, *refs) = refs[:2], refs[2:4], refs[4:]
+    pieces, sent = refs[:-1], refs[-1]
     core = scalars[1] % 2
-    wide = late[1].shape[0]
+    wide = up.shape[0]
     counts = [jnp.int32(0), jnp.int32(0)]
-    for held, up, labels, primal in (early, late):
+    start = 0
+    for held, primal in (early, late):
         for i in range(held.shape[0] // rows):
             place = pl.ds(i * rows, rows)
-            label = labels[:, place].astype(F32)
+            label = labels[:, pl.ds(start, rows)].astype(F32)
             forget, copy = label[0:1, :], label[1:2, :]
-            upward = up[:, place].astype(F32)
+            upward = up[:, pl.ds(start, rows)].astype(F32)
+            start += rows
             own_rate = sum((copy == float(c)).astype(F32) * rate[c] for c in range(copies))
             factor = own_rate * (forget * upward * second_slope(primal[:, place]) / length)
             signed = (1.0 - 2.0 * forget) * upward
@@ -194,6 +215,8 @@
                     side[pl.ds(wide, wide), at] = factor.astype(BF)
 
                 counts[k] = counts[k] + here
+    for i, piece in enumerate(pieces):
+        piece[...] = sent[pl.ds(i * piece.shape[0], piece.shape[0]), :]
 
 
 def in_tiles_of(parts, out, body):
@@ -218,8 +241,10 @@
 
 def second_kernel(sizes, scalars, *refs):
     part, pairs, copies, length = sizes
-    early, late, (mine, other, send, keep) = refs[:2], refs[2:4], refs[4:]
+    early, pieces, (side, mine, other, held, send, keep) = refs[:2], refs[2:-6], refs[-6:]
+    late = (held, side)
     core = scalars[1] % 2
+    put_together(pieces, held)
 
     def body(tokens, rows, keep, more):
         held, side = tokens
@@ -288,21 +313,12 @@
 
 
 def place_kernel(order, scalars, *refs):
-    blocks, out = refs[:-1], refs[-1]
+    blocks, (out, joined) = refs[:-2], refs[-2:]
     me = scalars[0]
     wide = blocks[0].shape[0]
-    flat = []
-    for ref in blocks:
-        flat += [ref[pl.ds(row, wide), :].astype(F32) for row in range(0, ref.shape[0], wide)]
-    where = {r: flat[i] for i, r in enumerate(order)}
-    for r in order:
-        if r % 2:
-            continue
-        low, high = where[r], where[r ^ 1]
-        odd = me % 2 == 1
-        pair = jnp.concatenate([jnp.where(odd, high, low), jnp.where(odd, low, high)], 0)
-        columns = pl.ds(pl.multiple_of(((me ^ r) // 2) * 128, 128), 128)
-        out[:, columns] = pair.T
+    for r, block in zip(order, blocks):
+        joined[pl.ds(pl.multiple_of((me ^ r) * wide, wide), wide), :] = block[...]
+    out[...] = joined[...].T.astype(F32)
 
 
 def run(kernel, scalars, arrays, outs, scratch=()):
@@ -418,42 +434,53 @@
 
     sizes = (part, pairs, copies, seq_length)
     stacked = (copies * wide, features // 2)
-
-    def put_together(blocks, before):
-        count = len(blocks) * rows
-        shapes = [((count, features), BF), ((wide, count), BF), ((16, count), BF), ((wide, count), F32)]
-        shapes += [(stacked, BF if before else F32), (stacked, F32)]
-        places = [order.index(r) for r in blocks]
-        return run(
-            functools.partial(first_kernel, sizes, places, bool(before)),
-            [scalars],
-            pieces_of(blocks) + [up, labels, weight] + before,
-            shapes,
-        )
-
-    *tokens_early, primal_early, sums, keep = put_together(early, [])
-    *tokens_late, primal_late, send, keep = put_together(late, [sums, keep])
+    count = rows * len(early)
+    held_early, primal_early = run(
+        functools.partial(primal_kernel, part),
+        [scalars],
+        pieces_of(early) + [weight],
+        [((count, features), BF), ((wide, count), F32)],
+    )
+    count = rows * len(late)
+    held_late, primal_late, up, labels, send, keep = run(
+        functools.partial(first_kernel, sizes, [order.index(r) for r in early + late]),
+        [scalars],
+        pieces_of(late) + [up, labels, weight, held_early, primal_early],
+        [
+            ((count, features), BF),
+            ((wide, count), F32),
+            ((wide, dp * rows), BF),
+            ((16, dp * rows), BF),
+            (stacked, BF),
+            (stacked, F32),
+        ],
+        [(stacked, F32)],
+    )
     summed, came = total(keep, swap(send, "fsdp", 1), far_bits)
-    tokens_early[2] = after(tokens_early[2], summed)
+    labels = after(labels, summed)
     taken = ((dp // 2 * rows, features), BF)
     beside = ((2 * wide, dp // 2 * rows), BF)
-    own, own_side, sent, sent_side = run(
+    cut = ((half_rows, features), BF)
+    own, own_side, sent_side, *sent = run(
         functools.partial(sort_kernel, sizes, rows),
         [scalars, adv_rate],
-        [*tokens_early, primal_early, *tokens_late, primal_late],
-        [taken, beside, taken, beside],
-    )
-    mine = [own, own_side, swap(sent, "fsdp", 1), swap(sent_side, "fsdp", 1)]
+        [held_early, primal_early, held_late, primal_late, up, labels],
+        [taken, beside, beside] + [cut] * dp,
+        [taken],
+    )
+    came_side = swap(sent_side, "fsdp", 1)
+    came_pieces = [swap(piece, "fsdp", 1) for piece in sent]
     half, full = (wide, features // 2), (wide, features)
     attacked, sent = run(
         attack_kernel, [scalars, adv_rate], [summed, came, weight], [(half, BF), (half, BF)]
     )
-    send, keep = run(
+    held, send, keep = run(
         functools.partial(second_kernel, sizes),
         [scalars],
-        [*mine, attacked, swap(sent, "fsdp", 1)],
-        [(full, BF), (full, F32)],
-    )
+        [own, own_side, *came_pieces, came_side, attacked, swap(sent, "fsdp", 1)],
+        [taken, (full, BF), (full, F32)],
+    )
+    mine = [own, own_side, held, came_side]
     send, keep = run(
         functools.partial(third_kernel, sizes),
         [scalars],
@@ -477,19 +504,16 @@
     (result,) = run(
         functools.partial(result_kernel, scale), [], [keep, came], [((wide, part), BF)]
     )
-    blocks = [result]
-    came_order = [0]
-    for r in range(dp - 1, 0, -1):
-        came_order.append(r)
-        blocks.append(swap(result, "dp", r))
-    if 2 * wide == 128:
-        (placed,) = run(
-            functools.partial(place_kernel, came_order), [scalars], blocks, [((part, outs), F32)]
-        )
-        return placed
-    result = jnp.concatenate(blocks).reshape(dp, wide, part)
-    result = result[jnp.argsort(me ^ jnp.array(came_order))]
-    return result.reshape(outs, part).T.astype(F32)
+    came_order = sorted(range(dp), key=lambda r: format(r, f"0{len(dp_bits)}b")[::-1])
+    blocks = [swap(result, "dp", r) if r else result for r in came_order]
+    (placed,) = run(
+        functools.partial(place_kernel, came_order),
+        [scalars],
+        blocks,
+        [((part, outs), F32)],
+        [((outs, part), BF)],
+    )
+    return placed
 
 
 def solution(mesh):

time: 110 us -> 108 us (0.982)
  waiting for transfers between devices: 49.6 us -> 47 us
    ppermute x33 -> x40, waiting for transfers between devices: 49.6 us -> 47 us  [swap(): lax.ppermute(value, axis, [(i, i ^ bit) for i in range(lax.axis_size(axis...]
    ppermute x33 -> x40, starting transfers between devices: 38.1 us -> 38.8 us  [swap(): lax.ppermute(value, axis, [(i, i ^ bit) for i in range(lax.axis_size(axis...]
  transfers between devices with their start and end apart: 33 -> 40, of which waited for: 17 -> 20; matrix products, arithmetic and copies ran while one was open for 1% -> 1% of each run, Pallas kernels for 5% -> 6%
where the time goes in v5:
time: 108 us; the launch traced here: 107 us
  waiting for transfers between devices  47 us (44%)
  starting transfers between devices  38.8 us (36%)
  Pallas kernels  17 us (16%)
  local copies, waits for them, and re-layouts  3.04 us (3%)
  between operations  1.49 us (1%)
    ppermute x40, waiting for transfers between devices, swap(): lax.ppermute(value, axis, [(i, i ^ bit) for i in range(lax.axis_size(axis...  47 us
    ppermute x40, starting transfers between devices, swap(): lax.ppermute(value, axis, [(i, i ^ bit) for i in range(lax.axis_size(axis...  38.8 us
    pallas_call x14, Pallas kernels, run(): pl.pallas_call(kernel, out_shape=[jax.ShapeDtypeStruct(s, t) for s, t in...  17 us
  transfers between devices with their start and end apart: 40, of which 20 were waited for; matrix products, arithmetic and copies ran while one was open for 1% of the time, Pallas kernels for 6%

profile of v5, /device:TPU:0, one launch (start us, length us, event | category | flops | bytes accessed | tf_op | source)
XLA Modules:
  0.0 107.5 jit_solution(5807658821658971217)
XLA Ops:
  0.0 3.0 %collective-permute-start = (bf16[128,2048]{1,0:T(8,128)(2,1)}, bf16[128,2048]{1,0:T(8,128)(2,1)S(1)}, u32[]{:S(2)}, u32[]{:S(2)}) collective-permute-start(bf16[128,2048]{1,0:T(8,128)(2,1)} %param.6), channel_id=1, source_target_pairs={{0,4},{4,0},{8,12},{12,8},{16,20},{20,16},{24,28},{28,24},{1,5},{5... | collective-permute-start | bytes 1572872 | tf_op jit(solution)/shard_map/ppermute | solution.py:25
  4.0 2.7 %collective-permute-start.7 = (bf16[64,2048]{1,0:T(8,128)(2,1)S(1)}, bf16[64,2048]{1,0:T(8,128)(2,1)S(1)}, u32[]{:S(2)}, u32[]{:S(2)}) collective-permute-start(bf16[64,2048]{1,0:T(8,128)(2,1)S(1)} %get-tuple-element.110.refs_0_), channel_id=1, source_target_pairs={{0,16},{4,20},{8,24},{12,28},{16,0},{20,4},{24,8},{28,12},{1,17},{... | collective-permute-start | bytes 786440 | tf_op jit(solution)/shard_map/ppermute | solution.py:25
  6.7 1.6 %collective-permute-start.1 = (bf16[64,2048]{1,0:T(8,128)(2,1)S(1)}, bf16[64,2048]{1,0:T(8,128)(2,1)S(1)}, u32[]{:S(2)}, u32[]{:S(2)}) collective-permute-start(bf16[64,2048]{1,0:T(8,128)(2,1)S(1)} %get-tuple-element.110.refs_0_), channel_id=1, source_target_pairs={{0,8},{4,12},{8,0},{12,4},{16,24},{20,28},{24,16},{28,20},{1,9},{5... | collective-permute-start | bytes 786440 | tf_op jit(solution)/shard_map/ppermute | solution.py:25
  12.8 5.7 %collective-permute-done.7.refs_7_ = bf16[64,2048]{1,0:T(8,128)(2,1)S(1)} collective-permute-done((bf16[64,2048]{1,0:T(8,128)(2,1)S(1)}, bf16[64,2048]{1,0:T(8,128)(2,1)S(1)}, u32[]{:S(2)}, u32[]{:S(2)}) %collective-permute-start.7) | collective-permute-done | bytes 262176 | tf_op jit(solution)/shard_map/ppermute | solution.py:25
  19.4 3.1 %collective-permute-start.2 = (bf16[64,2048]{1,0:T(8,128)(2,1)S(1)}, bf16[64,2048]{1,0:T(8,128)(2,1)S(1)}, u32[]{:S(2)}, u32[]{:S(2)}) collective-permute-start(bf16[64,2048]{1,0:T(8,128)(2,1)S(1)} %get-tuple-element.64.refs_1_), channel_id=1, source_target_pairs={{0,8},{4,12},{8,0},{12,4},{16,24},{20,28},{24,16},{28,20},{1,9},{5... | collective-permute-start | bytes 786440 | tf_op jit(solution)/shard_map/ppermute | solution.py:25
  23.6 1.6 %collective-permute-start.5 = (bf16[144,256]{1,0:T(8,128)(2,1)S(1)}, bf16[144,256]{1,0:T(8,128)(2,1)S(1)}, u32[]{:S(2)}, u32[]{:S(2)}) collective-permute-start(bf16[144,256]{1,0:T(8,128)(2,1)S(1)} %get-tuple-element.62), channel_id=1, source_target_pairs={{0,4},{4,0},{8,12},{12,8},{16,20},{20,16},{24,28},{28,24},{1,5},{5... | collective-permute-start | bytes 221192 | tf_op jit(solution)/shard_map/ppermute | solution.py:25
  25.7 6.5 %collective-permute-done.8.refs_8_ = bf16[64,2048]{1,0:T(8,128)(2,1)S(1)} collective-permute-done((bf16[64,2048]{1,0:T(8,128)(2,1)S(1)}, bf16[64,2048]{1,0:T(8,128)(2,1)S(1)}, u32[]{:S(2)}, u32[]{:S(2)}) %collective-permute-start.8) | collective-permute-done | bytes 262176 | tf_op jit(solution)/shard_map/ppermute | solution.py:25
  35.5 1.6 %collective-permute-start.12 = (bf16[128,512]{1,0:T(8,128)(2,1)S(1)}, bf16[128,512]{1,0:T(8,128)(2,1)S(1)}, u32[]{:S(2)}, u32[]{:S(2)}) collective-permute-start(bf16[128,512]{1,0:T(8,128)(2,1)S(1)} %pad_maximum_fusion), channel_id=1, source_target_pairs={{0,2},{1,3},{2,0},{3,1},{4,6},{5,7},{6,4},{7,5},{8,10},{9,11},{10,... | collective-permute-start | bytes 393224 | tf_op jit(solution)/shard_map/ppermute | solution.py:25
  37.0 2.0 %collective-permute-done.13.refs_0_ = bf16[64,2048]{1,0:T(8,128)(2,1)S(1)} collective-permute-done((bf16[64,2048]{1,0:T(8,128)(2,1)S(1)}, bf16[64,2048]{1,0:T(8,128)(2,1)S(1)}, u32[]{:S(2)}, u32[]{:S(2)}) %collective-permute-start.13) | collective-permute-done | bytes 262176 | tf_op jit(solution)/shard_map/ppermute | solution.py:25
  39.5 1.9 %collective-permute-start.15 = (bf16[64,2048]{1,0:T(8,128)(2,1)S(1)}, bf16[64,2048]{1,0:T(8,128)(2,1)S(1)}, u32[]{:S(2)}, u32[]{:S(2)}) collective-permute-start(bf16[64,2048]{1,0:T(8,128)(2,1)S(1)} %collective-permute-done.13.refs_0_), channel_id=1, source_target_pairs={{0,8},{4,12},{8,0},{12,4},{16,24},{20,28},{24,16},{28,20},{1,9},{5... | collective-permute-start | bytes 786440 | tf_op jit(solution)/shard_map/ppermute | solution.py:25
  41.4 3.2 %collective-permute-done.6.refs_6_ = bf16[64,2048]{1,0:T(8,128)(2,1)S(1)} collective-permute-done((bf16[64,2048]{1,0:T(8,128)(2,1)S(1)}, bf16[64,2048]{1,0:T(8,128)(2,1)S(1)}, u32[]{:S(2)}, u32[]{:S(2)}) %collective-permute-start.6) | collective-permute-done | bytes 262176 | tf_op jit(solution)/shard_map/ppermute | solution.py:25
  45.2 5.4 %collective-permute-done.17.came = bf16[80,512]{1,0:T(8,128)(2,1)S(1)} collective-permute-done((bf16[80,512]{1,0:T(8,128)(2,1)S(1)}, bf16[80,512]{1,0:T(8,128)(2,1)S(1)}, u32[]{:S(2)}, u32[]{:S(2)}) %collective-permute-start.17) | collective-permute-done | bytes 81952 | tf_op jit(solution)/shard_map/ppermute | solution.py:25
  51.2 1.8 %shard_map.66 = (bf16[768,2048]{1,0:T(8,128)(2,1)S(1)}, f32[64,768]{1,0:T(8,128)S(1)}) custom-call(s32[4]{0:T(128)S(1)} %pad_add_fusion.scalars, bf16[64,2048]{1,0:T(8,128)(2,1)S(1)} %get-tuple-element.110.refs_0_, bf16[64,2048]{1,0:T(8,128)(2,1)S(1)} %get-tuple-element.64.refs_1_, bf16[128,2048]{1,0:T(8,128)(2,1)S(1)} %collective-permute-done.refs_2_, ...), custom_call_target="tpu_custom_call" | custom-call | tf_op jit(solution)/shard_map/pallas_call | solution.py:329
  54.2 1.7 %shard_map.69 = (bf16[256,2048]{1,0:T(8,128)(2,1)S(1)}, f32[64,256]{1,0:T(8,128)S(1)}, bf16[64,1024]{1,0:T(8,128)(2,1)S(1)}, bf16[16,1024]{1,0:T(8,128)(2,1)S(1)...) custom-call(s32[4]{0:T(128)S(1)} %pad_add_fusion.scalars, ...), custom_call_target="tpu_custom_call" | custom-call | tf_op jit(solution)/shard_map/pallas_call | solution.py:329
  56.0 1.5 %collective-permute-done.18.came = bf16[128,1024]{1,0:T(8,128)(2,1)S(1)} collective-permute-done((bf16[128,1024]{1,0:T(8,128)(2,1)S(1)}, bf16[128,1024]{1,0:T(8,128)(2,1)S(1)}, u32[]{:S(2)}, u32[]{:S(2)}) %collective-permute-start.18) | collective-permute-done | bytes 262176 | tf_op jit(solution)/shard_map/ppermute | solution.py:25
  57.6 1.6 %collective-permute-start.28 = (bf16[128,1024]{1,0:T(8,128)(2,1)S(1)}, bf16[128,1024]{1,0:T(8,128)(2,1)S(1)}, u32[]{:S(2)}, u32[]{:S(2)}) collective-permute-start(bf16[128,1024]{1,0:T(8,128)(2,1)S(1)} %get-tuple-element.99), channel_id=1, source_target_pairs={{0,2},{1,3},{2,0},{3,1},{4,6},{5,7},{6,4},{7,5},{8,10},{9,11},{10,... | collective-permute-start | bytes 786440 | tf_op jit(solution)/shard_map/ppermute | solution.py:25
  59.2 2.0 %shard_map.71 = (bf16[512,2048]{1,0:T(8,128)(2,1)S(1)}, bf16[128,512]{1,0:T(8,128)(2,1)S(1)}, bf16[128,512]{1,0:T(8,128)(2,1)S(1)}, bf16[64,2048]{1,0:T(8,128)(2...) custom-call(s32[4]{0:T(128)S(1)} %pad_add_fusion.scalars, ...), custom_call_target="tpu_custom_call" | custom-call | tf_op jit(solution)/shard_map/pallas_call | solution.py:329
  63.5 2.5 %collective-permute-done.28.came = bf16[128,1024]{1,0:T(8,128)(2,1)S(1)} collective-permute-done((bf16[128,1024]{1,0:T(8,128)(2,1)S(1)}, bf16[128,1024]{1,0:T(8,128)(2,1)S(1)}, u32[]{:S(2)}, u32[]{:S(2)}) %collective-permute-start.28) | collective-permute-done | bytes 262176 | tf_op jit(solution)/shard_map/ppermute | solution.py:25
  69.1 3.0 %shard_map.73 = (bf16[512,2048]{1,0:T(8,128)(2,1)S(1)}, bf16[64,2048]{1,0:T(8,128)(2,1)S(1)}, f32[64,2048]{1,0:T(8,128)S(1)}) custom-call(s32[4]{0:T(128)S(1)} %pad_add_fusion.scalars, bf16[512,2048]{1,0:T(8,128)(2,1)S(1)} %get-tuple-element.88.refs_0_, bf16[128,512]{1,0:T(8,128)(2,1)S(1)} %get-tuple-element.89.refs_1_, ...), custom_call_target="tpu_custom_call" | custom-call | tf_op jit(solution)/shard_map/pallas_call | solution.py:329
  72.1 1.6 %collective-permute-start.30 = (bf16[64,2048]{1,0:T(8,128)(2,1)S(1)}, bf16[64,2048]{1,0:T(8,128)(2,1)S(1)}, u32[]{:S(2)}, u32[]{:S(2)}) collective-permute-start(bf16[64,2048]{1,0:T(8,128)(2,1)S(1)} %get-tuple-element.104), channel_id=1, source_target_pairs={{0,2},{1,3},{2,0},{3,1},{4,6},{5,7},{6,4},{7,5},{8,10},{9,11},{10,... | collective-permute-start | bytes 786440 | tf_op jit(solution)/shard_map/ppermute | solution.py:25
  73.7 6.9 %collective-permute-done.30.refs_6_ = bf16[64,2048]{1,0:T(8,128)(2,1)S(1)} collective-permute-done((bf16[64,2048]{1,0:T(8,128)(2,1)S(1)}, bf16[64,2048]{1,0:T(8,128)(2,1)S(1)}, u32[]{:S(2)}, u32[]{:S(2)}) %collective-permute-start.30) | collective-permute-done | bytes 262176 | tf_op jit(solution)/shard_map/ppermute | solution.py:25
  80.6 2.9 %shard_map.74 = (bf16[64,1024]{1,0:T(8,128)(2,1)S(1)}, f32[64,1024]{1,0:T(8,128)S(1)}) custom-call(s32[4]{0:T(128)S(1)} %pad_add_fusion.scalars, bf16[512,2048]{1,0:T(8,128)(2,1)S(1)} %get-tuple-element.88.refs_0_, bf16[128,512]{1,0:T(8,128)(2,1)S(1)} %get-tuple-element.89.refs_1_, bf16[512,2048]{1,0:T(8,128)(2,1)S(1)} %get-tuple-element.102.refs_2_, ...), custom_call_target="tpu_custom_call" | custom-call | tf_op jit(solution)/shard_map/pallas_call | solution.py:329
  85.5 1.6 %collective-permute-start.32 = (bf16[64,512]{1,0:T(8,128)(2,1)S(1)}, bf16[64,512]{1,0:T(8,128)(2,1)S(1)}, u32[]{:S(2)}, u32[]{:S(2)}) collective-permute-start(bf16[64,512]{1,0:T(8,128)(2,1)S(1)} %get-tuple-element.108), channel_id=1, source_target_pairs={{0,2},{1,3},{2,0},{3,1},{4,6},{5,7},{6,4},{7,5},{8,10},{9,11},{10,... | collective-permute-start | bytes 196616 | tf_op jit(solution)/shard_map/ppermute | solution.py:25
  87.0 2.8 %collective-permute-done.32.came = bf16[64,512]{1,0:T(8,128)(2,1)S(1)} collective-permute-done((bf16[64,512]{1,0:T(8,128)(2,1)S(1)}, bf16[64,512]{1,0:T(8,128)(2,1)S(1)}, u32[]{:S(2)}, u32[]{:S(2)}) %collective-permute-start.32) | collective-permute-done | bytes 65568 | tf_op jit(solution)/shard_map/ppermute | solution.py:25
  89.8 2.3 %collective-permute-start.33 = (bf16[64,512]{1,0:T(8,128)(2,1)S(1)}, bf16[64,512]{1,0:T(8,128)(2,1)S(1)}, u32[]{:S(2)}, u32[]{:S(2)}) collective-permute-start(bf16[64,512]{1,0:T(8,128)(2,1)S(1)} %shard_map.76.refs_0_), channel_id=1, source_target_pairs={{0,16},{4,20},{8,24},{12,28},{16,0},{20,4},{24,8},{28,12},{1,17},{... | collective-permute-start | bytes 196616 | tf_op jit(solution)/shard_map/ppermute | solution.py:25
  92.9 2.3 %collective-permute-start.35 = (bf16[64,512]{1,0:T(8,128)(2,1)S(1)}, bf16[64,512]{1,0:T(8,128)(2,1)S(1)}, u32[]{:S(2)}, u32[]{:S(2)}) collective-permute-start(bf16[64,512]{1,0:T(8,128)(2,1)S(1)} %shard_map.76.refs_0_), channel_id=1, source_target_pairs={{0,24},{4,28},{8,16},{12,20},{16,8},{20,12},{24,0},{28,4},{1,25},{... | collective-permute-start | bytes 196616 | tf_op jit(solution)/shard_map/ppermute | solution.py:25
  95.7 1.5 %collective-permute-start.37 = (bf16[64,512]{1,0:T(8,128)(2,1)S(1)}, bf16[64,512]{1,0:T(8,128)(2,1)S(1)}, u32[]{:S(2)}, u32[]{:S(2)}) collective-permute-start(bf16[64,512]{1,0:T(8,128)(2,1)S(1)} %shard_map.76.refs_0_), channel_id=1, source_target_pairs={{0,20},{4,16},{8,28},{12,24},{16,4},{20,0},{24,12},{28,8},{1,21},{... | collective-permute-start | bytes 196616 | tf_op jit(solution)/shard_map/ppermute | solution.py:25
  97.2 1.5 %collective-permute-start.38 = (bf16[64,512]{1,0:T(8,128)(2,1)S(1)}, bf16[64,512]{1,0:T(8,128)(2,1)S(1)}, u32[]{:S(2)}, u32[]{:S(2)}) collective-permute-start(bf16[64,512]{1,0:T(8,128)(2,1)S(1)} %shard_map.76.refs_0_), channel_id=1, source_target_pairs={{0,12},{4,8},{8,4},{12,0},{16,28},{20,24},{24,20},{28,16},{1,13},{... | collective-permute-start | bytes 196616 | tf_op jit(solution)/shard_map/ppermute | solution.py:25
  98.7 3.2 %collective-permute-start.39 = (bf16[64,512]{1,0:T(8,128)(2,1)S(1)}, bf16[64,512]{1,0:T(8,128)(2,1)S(1)}, u32[]{:S(2)}, u32[]{:S(2)}) collective-permute-start(bf16[64,512]{1,0:T(8,128)(2,1)S(1)} %shard_map.76.refs_0_), channel_id=1, source_target_pairs={{0,28},{4,24},{8,20},{12,16},{16,12},{20,8},{24,4},{28,0},{1,29},{... | collective-permute-start | bytes 196616 | tf_op jit(solution)/shard_map/ppermute | solution.py:25
  102.0 1.4 %collective-permute-done.37.refs_5_ = bf16[64,512]{1,0:T(8,128)(2,1)S(1)} collective-permute-done((bf16[64,512]{1,0:T(8,128)(2,1)S(1)}, bf16[64,512]{1,0:T(8,128)(2,1)S(1)}, u32[]{:S(2)}, u32[]{:S(2)}) %collective-permute-start.37) | collective-permute-done | bytes 65568 | tf_op jit(solution)/shard_map/ppermute | solution.py:25
  103.4 2.3 %collective-permute-done.39.refs_7_ = bf16[64,512]{1,0:T(8,128)(2,1)S(1)} collective-permute-done((bf16[64,512]{1,0:T(8,128)(2,1)S(1)}, bf16[64,512]{1,0:T(8,128)(2,1)S(1)}, u32[]{:S(2)}, u32[]{:S(2)}) %collective-permute-start.39) | collective-permute-done | bytes 65568 | tf_op jit(solution)/shard_map/ppermute | solution.py:25
  105.7 1.8 %shard_map.77 = f32[512,512]{1,0:T(8,128)} custom-call(s32[4]{0:T(128)S(1)} %pad_add_fusion.scalars, bf16[64,512]{1,0:T(8,128)(2,1)S(1)} %shard_map.76.refs_0_, bf16[64,512]{1,0:T(8,128)(2,1)S(1)} %collective-permute-done.33.refs_1_, bf16[64,512]{1,0:T(8,128)(2,1)S(1)} %collective-permute-done.34.refs_2_, ...), custom_call_target="tpu_custom_call" | custom-call | tf_op jit(solution)/shard_map/pallas_call | solution.py:329
  (74 shorter events, 21.8 us)
Async XLA Ops:
  0.0 22.5 %collective-permute-start = (bf16[128,2048]{1,0:T(8,128)(2,1)}, bf16[128,2048]{1,0:T(8,128)(2,1)S(1)}, u32[]{:S(2)}, u32[]{:S(2)}) collective-permute-start(bf16[128,2048]{1,0:T(8,128)(2,1)} %param.6), channel_id=1, source_target_pairs={{0,4},{4,0},{8,12},{12,8},{16,20},{20,16},{24,28},{28,24},{1,5},{5... | collective-permute-start | bytes 1572872 | tf_op jit(solution)/shard_map/ppermute | solution.py:25
  4.0 14.5 %collective-permute-start.7 = (bf16[64,2048]{1,0:T(8,128)(2,1)S(1)}, bf16[64,2048]{1,0:T(8,128)(2,1)S(1)}, u32[]{:S(2)}, u32[]{:S(2)}) collective-permute-start(bf16[64,2048]{1,0:T(8,128)(2,1)S(1)} %get-tuple-element.110.refs_0_), channel_id=1, source_target_pairs={{0,16},{4,20},{8,24},{12,28},{16,0},{20,4},{24,8},{28,12},{1,17},{... | collective-permute-start | bytes 786440 | tf_op jit(solution)/shard_map/ppermute | solution.py:25
  6.7 12.7 %collective-permute-start.1 = (bf16[64,2048]{1,0:T(8,128)(2,1)S(1)}, bf16[64,2048]{1,0:T(8,128)(2,1)S(1)}, u32[]{:S(2)}, u32[]{:S(2)}) collective-permute-start(bf16[64,2048]{1,0:T(8,128)(2,1)S(1)} %get-tuple-element.110.refs_0_), channel_id=1, source_target_pairs={{0,8},{4,12},{8,0},{12,4},{16,24},{20,28},{24,16},{28,20},{1,9},{5... | collective-permute-start | bytes 786440 | tf_op jit(solution)/shard_map/ppermute | solution.py:25
  12.3 10.2 %collective-permute-start.3 = (bf16[272,128]{1,0:T(8,128)(2,1)S(1)}, bf16[272,128]{1,0:T(8,128)(2,1)S(1)}, u32[]{:S(2)}, u32[]{:S(2)}) collective-permute-start(bf16[272,128]{1,0:T(8,128)(2,1)S(1)} %get-tuple-element.58), channel_id=1, source_target_pairs={{0,8},{4,12},{8,0},{12,4},{16,24},{20,28},{24,16},{28,20},{1,9},{5... | collective-permute-start | bytes 208904 | tf_op jit(solution)/shard_map/ppermute | solution.py:25
  18.5 13.7 %collective-permute-start.8 = (bf16[64,2048]{1,0:T(8,128)(2,1)S(1)}, bf16[64,2048]{1,0:T(8,128)(2,1)S(1)}, u32[]{:S(2)}, u32[]{:S(2)}) collective-permute-start(bf16[64,2048]{1,0:T(8,128)(2,1)S(1)} %get-tuple-element.64.refs_1_), channel_id=1, source_target_pairs={{0,16},{4,20},{8,24},{12,28},{16,0},{20,4},{24,8},{28,12},{1,17},{... | collective-permute-start | bytes 786440 | tf_op jit(solution)/shard_map/ppermute | solution.py:25
  19.4 14.0 %collective-permute-start.2 = (bf16[64,2048]{1,0:T(8,128)(2,1)S(1)}, bf16[64,2048]{1,0:T(8,128)(2,1)S(1)}, u32[]{:S(2)}, u32[]{:S(2)}) collective-permute-start(bf16[64,2048]{1,0:T(8,128)(2,1)S(1)} %get-tuple-element.64.refs_1_), channel_id=1, source_target_pairs={{0,8},{4,12},{8,0},{12,4},{16,24},{20,28},{24,16},{28,20},{1,9},{5... | collective-permute-start | bytes 786440 | tf_op jit(solution)/shard_map/ppermute | solution.py:25
  22.6 10.8 %collective-permute-start.4 = (bf16[64,2048]{1,0:T(8,128)(2,1)S(1)}, bf16[64,2048]{1,0:T(8,128)(2,1)S(1)}, u32[]{:S(2)}, u32[]{:S(2)}) collective-permute-start(bf16[64,2048]{1,0:T(8,128)(2,1)S(1)} %collective-permute-done.1.refs_3_), channel_id=1, source_target_pairs={{0,4},{4,0},{8,12},{12,8},{16,20},{20,16},{24,28},{28,24},{1,5},{5... | collective-permute-start | bytes 786440 | tf_op jit(solution)/shard_map/ppermute | solution.py:25
  23.6 9.7 %collective-permute-start.5 = (bf16[144,256]{1,0:T(8,128)(2,1)S(1)}, bf16[144,256]{1,0:T(8,128)(2,1)S(1)}, u32[]{:S(2)}, u32[]{:S(2)}) collective-permute-start(bf16[144,256]{1,0:T(8,128)(2,1)S(1)} %get-tuple-element.62), channel_id=1, source_target_pairs={{0,4},{4,0},{8,12},{12,8},{16,20},{20,16},{24,28},{28,24},{1,5},{5... | collective-permute-start | bytes 221192 | tf_op jit(solution)/shard_map/ppermute | solution.py:25
  25.2 13.8 %collective-permute-start.13 = (bf16[64,2048]{1,0:T(8,128)(2,1)S(1)}, bf16[64,2048]{1,0:T(8,128)(2,1)S(1)}, u32[]{:S(2)}, u32[]{:S(2)}) collective-permute-start(bf16[64,2048]{1,0:T(8,128)(2,1)S(1)} %collective-permute-done.7.refs_7_), channel_id=1, source_target_pairs={{0,4},{4,0},{8,12},{12,8},{16,20},{20,16},{24,28},{28,24},{1,5},{5... | collective-permute-start | bytes 786440 | tf_op jit(solution)/shard_map/ppermute | solution.py:25
  32.2 7.3 %collective-permute-start.10 = (bf16[64,2048]{1,0:T(8,128)(2,1)S(1)}, bf16[64,2048]{1,0:T(8,128)(2,1)S(1)}, u32[]{:S(2)}, u32[]{:S(2)}) collective-permute-start(bf16[64,2048]{1,0:T(8,128)(2,1)S(1)} %collective-permute-done.8.refs_8_), channel_id=1, source_target_pairs={{0,8},{4,12},{8,0},{12,4},{16,24},{20,28},{24,16},{28,20},{1,9},{5... | collective-permute-start | bytes 786440 | tf_op jit(solution)/shard_map/ppermute | solution.py:25
  33.4 11.2 %collective-permute-start.6 = (bf16[64,2048]{1,0:T(8,128)(2,1)S(1)}, bf16[64,2048]{1,0:T(8,128)(2,1)S(1)}, u32[]{:S(2)}, u32[]{:S(2)}) collective-permute-start(bf16[64,2048]{1,0:T(8,128)(2,1)S(1)} %collective-permute-done.2.refs_4_), channel_id=1, source_target_pairs={{0,4},{4,0},{8,12},{12,8},{16,20},{20,16},{24,28},{28,24},{1,5},{5... | collective-permute-start | bytes 786440 | tf_op jit(solution)/shard_map/ppermute | solution.py:25
  34.5 16.8 %collective-permute-start.9 = (bf16[64,2048]{1,0:T(8,128)(2,1)S(1)}, bf16[64,2048]{1,0:T(8,128)(2,1)S(1)}, u32[]{:S(2)}, u32[]{:S(2)}) collective-permute-start(bf16[64,2048]{1,0:T(8,128)(2,1)S(1)} %collective-permute-done.7.refs_7_), channel_id=1, source_target_pairs={{0,8},{4,12},{8,0},{12,4},{16,24},{20,28},{24,16},{28,20},{1,9},{5... | collective-permute-start | bytes 786440 | tf_op jit(solution)/shard_map/ppermute | solution.py:25
  35.5 9.7 %collective-permute-start.12 = (bf16[128,512]{1,0:T(8,128)(2,1)S(1)}, bf16[128,512]{1,0:T(8,128)(2,1)S(1)}, u32[]{:S(2)}, u32[]{:S(2)}) collective-permute-start(bf16[128,512]{1,0:T(8,128)(2,1)S(1)} %pad_maximum_fusion), channel_id=1, source_target_pairs={{0,2},{1,3},{2,0},{3,1},{4,6},{5,7},{6,4},{7,5},{8,10},{9,11},{10,... | collective-permute-start | bytes 393224 | tf_op jit(solution)/shard_map/ppermute | solution.py:25
  39.0 14.1 %collective-permute-start.14 = (bf16[64,2048]{1,0:T(8,128)(2,1)S(1)}, bf16[64,2048]{1,0:T(8,128)(2,1)S(1)}, u32[]{:S(2)}, u32[]{:S(2)}) collective-permute-start(bf16[64,2048]{1,0:T(8,128)(2,1)S(1)} %collective-permute-done.8.refs_8_), channel_id=1, source_target_pairs={{0,4},{4,0},{8,12},{12,8},{16,20},{20,16},{24,28},{28,24},{1,5},{5... | collective-permute-start | bytes 786440 | tf_op jit(solution)/shard_map/ppermute | solution.py:25
  39.5 13.6 %collective-permute-start.15 = (bf16[64,2048]{1,0:T(8,128)(2,1)S(1)}, bf16[64,2048]{1,0:T(8,128)(2,1)S(1)}, u32[]{:S(2)}, u32[]{:S(2)}) collective-permute-start(bf16[64,2048]{1,0:T(8,128)(2,1)S(1)} %collective-permute-done.13.refs_0_), channel_id=1, source_target_pairs={{0,8},{4,12},{8,0},{12,4},{16,24},{20,28},{24,16},{28,20},{1,9},{5... | collective-permute-start | bytes 786440 | tf_op jit(solution)/shard_map/ppermute | solution.py:25
  44.6 9.6 %collective-permute-start.16 = (bf16[64,2048]{1,0:T(8,128)(2,1)S(1)}, bf16[64,2048]{1,0:T(8,128)(2,1)S(1)}, u32[]{:S(2)}, u32[]{:S(2)}) collective-permute-start(bf16[64,2048]{1,0:T(8,128)(2,1)S(1)} %collective-permute-done.10.refs_10_), channel_id=1, source_target_pairs={{0,4},{4,0},{8,12},{12,8},{16,20},{20,16},{24,28},{28,24},{1,5},{5... | collective-permute-start | bytes 786440 | tf_op jit(solution)/shard_map/ppermute | solution.py:25
  45.1 5.5 %collective-permute-start.17 = (bf16[80,512]{1,0:T(8,128)(2,1)S(1)}, bf16[80,512]{1,0:T(8,128)(2,1)S(1)}, u32[]{:S(2)}, u32[]{:S(2)}) collective-permute-start(bf16[80,512]{1,0:T(8,128)(2,1)S(1)} %get-tuple-element.77), channel_id=1, source_target_pairs={{0,16},{4,20},{8,24},{12,28},{16,0},{20,4},{24,8},{28,12},{1,17},{... | collective-permute-start | bytes 245768 | tf_op jit(solution)/shard_map/ppermute | solution.py:25
  57.6 8.4 %collective-permute-start.28 = (bf16[128,1024]{1,0:T(8,128)(2,1)S(1)}, bf16[128,1024]{1,0:T(8,128)(2,1)S(1)}, u32[]{:S(2)}, u32[]{:S(2)}) collective-permute-start(bf16[128,1024]{1,0:T(8,128)(2,1)S(1)} %get-tuple-element.99), channel_id=1, source_target_pairs={{0,2},{1,3},{2,0},{3,1},{4,6},{5,7},{6,4},{7,5},{8,10},{9,11},{10,... | collective-permute-start | bytes 786440 | tf_op jit(solution)/shard_map/ppermute | solution.py:25
  61.2 4.8 %collective-permute-start.19 = (bf16[64,2048]{1,0:T(8,128)(2,1)S(1)}, bf16[64,2048]{1,0:T(8,128)(2,1)S(1)}, u32[]{:S(2)}, u32[]{:S(2)}) collective-permute-start(bf16[64,2048]{1,0:T(8,128)(2,1)S(1)} %get-tuple-element.90), channel_id=1, source_target_pairs={{0,1},{1,0},{2,3},{3,2},{4,5},{5,4},{6,7},{7,6},{8,9},{9,8},{10,11... | collective-permute-start | bytes 786440 | tf_op jit(solution)/shard_map/ppermute | solution.py:25
  61.3 5.3 %collective-permute-start.20 = (bf16[64,2048]{1,0:T(8,128)(2,1)S(1)}, bf16[64,2048]{1,0:T(8,128)(2,1)S(1)}, u32[]{:S(2)}, u32[]{:S(2)}) collective-permute-start(bf16[64,2048]{1,0:T(8,128)(2,1)S(1)} %get-tuple-element.91), channel_id=1, source_target_pairs={{0,1},{1,0},{2,3},{3,2},{4,5},{5,4},{6,7},{7,6},{8,9},{9,8},{10,11... | collective-permute-start | bytes 786440 | tf_op jit(solution)/shard_map/ppermute | solution.py:25
  61.9 4.8 %collective-permute-start.21 = (bf16[64,2048]{1,0:T(8,128)(2,1)S(1)}, bf16[64,2048]{1,0:T(8,128)(2,1)S(1)}, u32[]{:S(2)}, u32[]{:S(2)}) collective-permute-start(bf16[64,2048]{1,0:T(8,128)(2,1)S(1)} %get-tuple-element.92), channel_id=1, source_target_pairs={{0,1},{1,0},{2,3},{3,2},{4,5},{5,4},{6,7},{7,6},{8,9},{9,8},{10,11... | collective-permute-start | bytes 786440 | tf_op jit(solution)/shard_map/ppermute | solution.py:25
  63.4 4.4 %collective-permute-start.22 = (bf16[64,2048]{1,0:T(8,128)(2,1)S(1)}, bf16[64,2048]{1,0:T(8,128)(2,1)S(1)}, u32[]{:S(2)}, u32[]{:S(2)}) collective-permute-start(bf16[64,2048]{1,0:T(8,128)(2,1)S(1)} %get-tuple-element.93), channel_id=1, source_target_pairs={{0,1},{1,0},{2,3},{3,2},{4,5},{5,4},{6,7},{7,6},{8,9},{9,8},{10,11... | collective-permute-start | bytes 786440 | tf_op jit(solution)/shard_map/ppermute | solution.py:25
  66.6 2.1 %collective-permute-start.26 = (bf16[64,2048]{1,0:T(8,128)(2,1)S(1)}, bf16[64,2048]{1,0:T(8,128)(2,1)S(1)}, u32[]{:S(2)}, u32[]{:S(2)}) collective-permute-start(bf16[64,2048]{1,0:T(8,128)(2,1)S(1)} %get-tuple-element.97), channel_id=1, source_target_pairs={{0,1},{1,0},{2,3},{3,2},{4,5},{5,4},{6,7},{7,6},{8,9},{9,8},{10,11... | collective-permute-start | bytes 786440 | tf_op jit(solution)/shard_map/ppermute | solution.py:25
  72.1 8.4 %collective-permute-start.30 = (bf16[64,2048]{1,0:T(8,128)(2,1)S(1)}, bf16[64,2048]{1,0:T(8,128)(2,1)S(1)}, u32[]{:S(2)}, u32[]{:S(2)}) collective-permute-start(bf16[64,2048]{1,0:T(8,128)(2,1)S(1)} %get-tuple-element.104), channel_id=1, source_target_pairs={{0,2},{1,3},{2,0},{3,1},{4,6},{5,7},{6,4},{7,5},{8,10},{9,11},{10,... | collective-permute-start | bytes 786440 | tf_op jit(solution)/shard_map/ppermute | solution.py:25
  85.5 4.3 %collective-permute-start.32 = (bf16[64,512]{1,0:T(8,128)(2,1)S(1)}, bf16[64,512]{1,0:T(8,128)(2,1)S(1)}, u32[]{:S(2)}, u32[]{:S(2)}) collective-permute-start(bf16[64,512]{1,0:T(8,128)(2,1)S(1)} %get-tuple-element.108), channel_id=1, source_target_pairs={{0,2},{1,3},{2,0},{3,1},{4,6},{5,7},{6,4},{7,5},{8,10},{9,11},{10,... | collective-permute-start | bytes 196616 | tf_op jit(solution)/shard_map/ppermute | solution.py:25
  89.8 7.4 %collective-permute-start.33 = (bf16[64,512]{1,0:T(8,128)(2,1)S(1)}, bf16[64,512]{1,0:T(8,128)(2,1)S(1)}, u32[]{:S(2)}, u32[]{:S(2)}) collective-permute-start(bf16[64,512]{1,0:T(8,128)(2,1)S(1)} %shard_map.76.refs_0_), channel_id=1, source_target_pairs={{0,16},{4,20},{8,24},{12,28},{16,0},{20,4},{24,8},{28,12},{1,17},{... | collective-permute-start | bytes 196616 | tf_op jit(solution)/shard_map/ppermute | solution.py:25
  92.1 6.6 %collective-permute-start.34 = (bf16[64,512]{1,0:T(8,128)(2,1)S(1)}, bf16[64,512]{1,0:T(8,128)(2,1)S(1)}, u32[]{:S(2)}, u32[]{:S(2)}) collective-permute-start(bf16[64,512]{1,0:T(8,128)(2,1)S(1)} %shard_map.76.refs_0_), channel_id=1, source_target_pairs={{0,8},{4,12},{8,0},{12,4},{16,24},{20,28},{24,16},{28,20},{1,9},{5... | collective-permute-start | bytes 196616 | tf_op jit(solution)/shard_map/ppermute | solution.py:25
  92.9 9.0 %collective-permute-start.35 = (bf16[64,512]{1,0:T(8,128)(2,1)S(1)}, bf16[64,512]{1,0:T(8,128)(2,1)S(1)}, u32[]{:S(2)}, u32[]{:S(2)}) collective-permute-start(bf16[64,512]{1,0:T(8,128)(2,1)S(1)} %shard_map.76.refs_0_), channel_id=1, source_target_pairs={{0,24},{4,28},{8,16},{12,20},{16,8},{20,12},{24,0},{28,4},{1,25},{... | collective-permute-start | bytes 196616 | tf_op jit(solution)/shard_map/ppermute | solution.py:25
  95.2 6.8 %collective-permute-start.36 = (bf16[64,512]{1,0:T(8,128)(2,1)S(1)}, bf16[64,512]{1,0:T(8,128)(2,1)S(1)}, u32[]{:S(2)}, u32[]{:S(2)}) collective-permute-start(bf16[64,512]{1,0:T(8,128)(2,1)S(1)} %shard_map.76.refs_0_), channel_id=1, source_target_pairs={{0,4},{4,0},{8,12},{12,8},{16,20},{20,16},{24,28},{28,24},{1,5},{5... | collective-permute-start | bytes 196616 | tf_op jit(solution)/shard_map/ppermute | solution.py:25
  95.7 7.7 %collective-permute-start.37 = (bf16[64,512]{1,0:T(8,128)(2,1)S(1)}, bf16[64,512]{1,0:T(8,128)(2,1)S(1)}, u32[]{:S(2)}, u32[]{:S(2)}) collective-permute-start(bf16[64,512]{1,0:T(8,128)(2,1)S(1)} %shard_map.76.refs_0_), channel_id=1, source_target_pairs={{0,20},{4,16},{8,28},{12,24},{16,4},{20,0},{24,12},{28,8},{1,21},{... | collective-permute-start | bytes 196616 | tf_op jit(solution)/shard_map/ppermute | solution.py:25
  97.2 6.2 %collective-permute-start.38 = (bf16[64,512]{1,0:T(8,128)(2,1)S(1)}, bf16[64,512]{1,0:T(8,128)(2,1)S(1)}, u32[]{:S(2)}, u32[]{:S(2)}) collective-permute-start(bf16[64,512]{1,0:T(8,128)(2,1)S(1)} %shard_map.76.refs_0_), channel_id=1, source_target_pairs={{0,12},{4,8},{8,4},{12,0},{16,28},{20,24},{24,20},{28,16},{1,13},{... | collective-permute-start | bytes 196616 | tf_op jit(solution)/shard_map/ppermute | solution.py:25
  98.7 7.0 %collective-permute-start.39 = (bf16[64,512]{1,0:T(8,128)(2,1)S(1)}, bf16[64,512]{1,0:T(8,128)(2,1)S(1)}, u32[]{:S(2)}, u32[]{:S(2)}) collective-permute-start(bf16[64,512]{1,0:T(8,128)(2,1)S(1)} %shard_map.76.refs_0_), channel_id=1, source_target_pairs={{0,28},{4,24},{8,20},{12,16},{16,12},{20,8},{24,4},{28,0},{1,29},{... | collective-permute-start | bytes 196616 | tf_op jit(solution)/shard_map/ppermute | solution.py:25
  (11 other events, 20.0 us)

commit v6 on v5

--- a/solution.py
+++ b/solution.py
@@ -385,7 +385,7 @@
     top_bit = dp_bits[0]
     for step, up_bit in enumerate(up_bits, 1):
         if step == len(dp_bits) and step > 1:
-            sent = after(sent, second[top_bit])
+            sent = after(sent, first[top_bit | up_bits[0]])
         came_up = swap(sent, "dp", up_bit)
         ready = [r for r in range(2, dp) if bin(r).count("1") == step]
         firsts, seconds = {}, {}
@@ -504,7 +504,8 @@
     (result,) = run(
         functools.partial(result_kernel, scale), [], [keep, came], [((wide, part), BF)]
     )
-    came_order = sorted(range(dp), key=lambda r: format(r, f"0{len(dp_bits)}b")[::-1])
+    upper = [i ^ (i >> 1) for i in range(dp // 2)][::-1]
+    came_order = [0] + [2 * i for i in upper if i] + [2 * i + 1 for i in upper]
     blocks = [swap(result, "dp", r) if r else result for r in came_order]
     (placed,) = run(
         functools.partial(place_kernel, came_order),

time: 108 us -> 106 us (0.981)
  waiting for transfers between devices: 47 us -> 38.2 us
  starting transfers between devices: 38.8 us -> 46.2 us
    ppermute x40, waiting for transfers between devices: 47 us -> 38.2 us  [swap(): lax.ppermute(value, axis, [(i, i ^ bit) for i in range(lax.axis_size(axis...]
    ppermute x40, starting transfers between devices: 38.8 us -> 46.2 us  [swap(): lax.ppermute(value, axis, [(i, i ^ bit) for i in range(lax.axis_size(axis...]
  transfers between devices with their start and end apart: 40 -> 40, of which waited for: 20 -> 20; matrix products, arithmetic and copies ran while one was open for 1% -> 1% of each run, Pallas kernels for 6% -> 7%
where the time goes in v6:
time: 106 us
  starting transfers between devices  46.2 us (44%)
  waiting for transfers between devices  38.2 us (36%)
  Pallas kernels  17 us (16%)
  local copies, waits for them, and re-layouts  3.04 us (3%)
  between operations  1.49 us (1%)
    ppermute x40, starting transfers between devices, swap(): lax.ppermute(value, axis, [(i, i ^ bit) for i in range(lax.axis_size(axis...  46.2 us
    ppermute x40, waiting for transfers between devices, swap(): lax.ppermute(value, axis, [(i, i ^ bit) for i in range(lax.axis_size(axis...  38.2 us
    pallas_call x14, Pallas kernels, run(): pl.pallas_call(kernel, out_shape=[jax.ShapeDtypeStruct(s, t) for s, t in...  17 us
  transfers between devices with their start and end apart: 40, of which 20 were waited for; matrix products, arithmetic and copies ran while one was open for 1% of the time, Pallas kernels for 7%

profile of v6, /device:TPU:0, one launch (start us, length us, event | category | flops | bytes accessed | tf_op | source)
XLA Modules:
  0.0 106.1 jit_solution(18252216347858710711)
XLA Ops:
  0.0 3.0 %collective-permute-start = (bf16[128,2048]{1,0:T(8,128)(2,1)}, bf16[128,2048]{1,0:T(8,128)(2,1)S(1)}, u32[]{:S(2)}, u32[]{:S(2)}) collective-permute-start(bf16[128,2048]{1,0:T(8,128)(2,1)} %param.6), channel_id=1, source_target_pairs={{0,4},{4,0},{8,12},{12,8},{16,20},{20,16},{24,28},{28,24},{1,5},{5... | collective-permute-start | bytes 1572872 | tf_op jit(solution)/shard_map/ppermute | solution.py:25
  4.0 1.6 %collective-permute-start.1 = (bf16[64,2048]{1,0:T(8,128)(2,1)S(1)}, bf16[64,2048]{1,0:T(8,128)(2,1)S(1)}, u32[]{:S(2)}, u32[]{:S(2)}) collective-permute-start(bf16[64,2048]{1,0:T(8,128)(2,1)S(1)} %get-tuple-element.110.refs_0_), channel_id=1, source_target_pairs={{0,8},{4,12},{8,0},{12,4},{16,24},{20,28},{24,16},{28,20},{1,9},{5... | collective-permute-start | bytes 786440 | tf_op jit(solution)/shard_map/ppermute | solution.py:25
  5.7 2.6 %collective-permute-start.7 = (bf16[64,2048]{1,0:T(8,128)(2,1)S(1)}, bf16[64,2048]{1,0:T(8,128)(2,1)S(1)}, u32[]{:S(2)}, u32[]{:S(2)}) collective-permute-start(bf16[64,2048]{1,0:T(8,128)(2,1)S(1)} %get-tuple-element.110.refs_0_), channel_id=1, source_target_pairs={{0,16},{4,20},{8,24},{12,28},{16,0},{20,4},{24,8},{28,12},{1,17},{... | collective-permute-start | bytes 786440 | tf_op jit(solution)/shard_map/ppermute | solution.py:25
  12.8 5.3 %collective-permute-done.1.refs_3_ = bf16[64,2048]{1,0:T(8,128)(2,1)S(1)} collective-permute-done((bf16[64,2048]{1,0:T(8,128)(2,1)S(1)}, bf16[64,2048]{1,0:T(8,128)(2,1)S(1)}, u32[]{:S(2)}, u32[]{:S(2)}) %collective-permute-start.1) | collective-permute-done | bytes 262176 | tf_op jit(solution)/shard_map/ppermute | solution.py:25
  18.4 4.0 %collective-permute-start.8 = (bf16[64,2048]{1,0:T(8,128)(2,1)S(1)}, bf16[64,2048]{1,0:T(8,128)(2,1)S(1)}, u32[]{:S(2)}, u32[]{:S(2)}) collective-permute-start(bf16[64,2048]{1,0:T(8,128)(2,1)S(1)} %get-tuple-element.64.refs_1_), channel_id=1, source_target_pairs={{0,16},{4,20},{8,24},{12,28},{16,0},{20,4},{24,8},{28,12},{1,17},{... | collective-permute-start | bytes 786440 | tf_op jit(solution)/shard_map/ppermute | solution.py:25
  23.5 1.6 %collective-permute-start.5 = (bf16[144,256]{1,0:T(8,128)(2,1)S(1)}, bf16[144,256]{1,0:T(8,128)(2,1)S(1)}, u32[]{:S(2)}, u32[]{:S(2)}) collective-permute-start(bf16[144,256]{1,0:T(8,128)(2,1)S(1)} %get-tuple-element.62), channel_id=1, source_target_pairs={{0,4},{4,0},{8,12},{12,8},{16,20},{20,16},{24,28},{28,24},{1,5},{5... | collective-permute-start | bytes 221192 | tf_op jit(solution)/shard_map/ppermute | solution.py:25
  25.6 3.8 %collective-permute-done.8.refs_8_ = bf16[64,2048]{1,0:T(8,128)(2,1)S(1)} collective-permute-done((bf16[64,2048]{1,0:T(8,128)(2,1)S(1)}, bf16[64,2048]{1,0:T(8,128)(2,1)S(1)}, u32[]{:S(2)}, u32[]{:S(2)}) %collective-permute-start.8) | collective-permute-done | bytes 262176 | tf_op jit(solution)/shard_map/ppermute | solution.py:25
  29.4 3.5 %collective-permute-start.10 = (bf16[64,2048]{1,0:T(8,128)(2,1)S(1)}, bf16[64,2048]{1,0:T(8,128)(2,1)S(1)}, u32[]{:S(2)}, u32[]{:S(2)}) collective-permute-start(bf16[64,2048]{1,0:T(8,128)(2,1)S(1)} %collective-permute-done.8.refs_8_), channel_id=1, source_target_pairs={{0,8},{4,12},{8,0},{12,4},{16,24},{20,28},{24,16},{28,20},{1,9},{5... | collective-permute-start | bytes 786440 | tf_op jit(solution)/shard_map/ppermute | solution.py:25
  34.8 1.6 %collective-permute-start.12 = (bf16[128,512]{1,0:T(8,128)(2,1)S(1)}, bf16[128,512]{1,0:T(8,128)(2,1)S(1)}, u32[]{:S(2)}, u32[]{:S(2)}) collective-permute-start(bf16[128,512]{1,0:T(8,128)(2,1)S(1)} %pad_maximum_fusion), channel_id=1, source_target_pairs={{0,2},{1,3},{2,0},{3,1},{4,6},{5,7},{6,4},{7,5},{8,10},{9,11},{10,... | collective-permute-start | bytes 393224 | tf_op jit(solution)/shard_map/ppermute | solution.py:25
  38.6 2.5 %collective-permute-start.15 = (bf16[64,2048]{1,0:T(8,128)(2,1)S(1)}, bf16[64,2048]{1,0:T(8,128)(2,1)S(1)}, u32[]{:S(2)}, u32[]{:S(2)}) collective-permute-start(bf16[64,2048]{1,0:T(8,128)(2,1)S(1)} %collective-permute-done.13.refs_0_), channel_id=1, source_target_pairs={{0,8},{4,12},{8,0},{12,4},{16,24},{20,28},{24,16},{28,20},{1,9},{5... | collective-permute-start | bytes 786440 | tf_op jit(solution)/shard_map/ppermute | solution.py:25
  41.1 3.1 %collective-permute-done.9.refs_9_ = bf16[64,2048]{1,0:T(8,128)(2,1)S(1)} collective-permute-done((bf16[64,2048]{1,0:T(8,128)(2,1)S(1)}, bf16[64,2048]{1,0:T(8,128)(2,1)S(1)}, u32[]{:S(2)}, u32[]{:S(2)}) %collective-permute-start.9) | collective-permute-done | bytes 262176 | tf_op jit(solution)/shard_map/ppermute | solution.py:25
  44.2 2.7 %collective-permute-start.17 = (bf16[80,512]{1,0:T(8,128)(2,1)S(1)}, bf16[80,512]{1,0:T(8,128)(2,1)S(1)}, u32[]{:S(2)}, u32[]{:S(2)}) collective-permute-start(bf16[80,512]{1,0:T(8,128)(2,1)S(1)} %get-tuple-element.77), channel_id=1, source_target_pairs={{0,16},{4,20},{8,24},{12,28},{16,0},{20,4},{24,8},{28,12},{1,17},{... | collective-permute-start | bytes 245768 | tf_op jit(solution)/shard_map/ppermute | solution.py:25
  46.9 2.9 %collective-permute-done.17.came = bf16[80,512]{1,0:T(8,128)(2,1)S(1)} collective-permute-done((bf16[80,512]{1,0:T(8,128)(2,1)S(1)}, bf16[80,512]{1,0:T(8,128)(2,1)S(1)}, u32[]{:S(2)}, u32[]{:S(2)}) %collective-permute-start.17) | collective-permute-done | bytes 81952 | tf_op jit(solution)/shard_map/ppermute | solution.py:25
  50.4 1.8 %shard_map.66 = (bf16[768,2048]{1,0:T(8,128)(2,1)S(1)}, f32[64,768]{1,0:T(8,128)S(1)}) custom-call(s32[4]{0:T(128)S(1)} %pad_add_fusion.scalars, bf16[64,2048]{1,0:T(8,128)(2,1)S(1)} %get-tuple-element.110.refs_0_, bf16[64,2048]{1,0:T(8,128)(2,1)S(1)} %get-tuple-element.64.refs_1_, bf16[128,2048]{1,0:T(8,128)(2,1)S(1)} %collective-permute-done.refs_2_, ...), custom_call_target="tpu_custom_call" | custom-call | tf_op jit(solution)/shard_map/pallas_call | solution.py:329
  52.2 1.7 %shard_map.69 = (bf16[256,2048]{1,0:T(8,128)(2,1)S(1)}, f32[64,256]{1,0:T(8,128)S(1)}, bf16[64,1024]{1,0:T(8,128)(2,1)S(1)}, bf16[16,1024]{1,0:T(8,128)(2,1)S(1)...) custom-call(s32[4]{0:T(128)S(1)} %pad_add_fusion.scalars, ...), custom_call_target="tpu_custom_call" | custom-call | tf_op jit(solution)/shard_map/pallas_call | solution.py:329
  54.0 1.5 %collective-permute-done.18.came = bf16[128,1024]{1,0:T(8,128)(2,1)S(1)} collective-permute-done((bf16[128,1024]{1,0:T(8,128)(2,1)S(1)}, bf16[128,1024]{1,0:T(8,128)(2,1)S(1)}, u32[]{:S(2)}, u32[]{:S(2)}) %collective-permute-start.18) | collective-permute-done | bytes 262176 | tf_op jit(solution)/shard_map/ppermute | solution.py:25
  55.6 1.6 %collective-permute-start.28 = (bf16[128,1024]{1,0:T(8,128)(2,1)S(1)}, bf16[128,1024]{1,0:T(8,128)(2,1)S(1)}, u32[]{:S(2)}, u32[]{:S(2)}) collective-permute-start(bf16[128,1024]{1,0:T(8,128)(2,1)S(1)} %get-tuple-element.99), channel_id=1, source_target_pairs={{0,2},{1,3},{2,0},{3,1},{4,6},{5,7},{6,4},{7,5},{8,10},{9,11},{10,... | collective-permute-start | bytes 786440 | tf_op jit(solution)/shard_map/ppermute | solution.py:25
  57.2 2.0 %shard_map.71 = (bf16[512,2048]{1,0:T(8,128)(2,1)S(1)}, bf16[128,512]{1,0:T(8,128)(2,1)S(1)}, bf16[128,512]{1,0:T(8,128)(2,1)S(1)}, bf16[64,2048]{1,0:T(8,128)(2...) custom-call(s32[4]{0:T(128)S(1)} %pad_add_fusion.scalars, ...), custom_call_target="tpu_custom_call" | custom-call | tf_op jit(solution)/shard_map/pallas_call | solution.py:329
  61.5 2.5 %collective-permute-done.28.came = bf16[128,1024]{1,0:T(8,128)(2,1)S(1)} collective-permute-done((bf16[128,1024]{1,0:T(8,128)(2,1)S(1)}, bf16[128,1024]{1,0:T(8,128)(2,1)S(1)}, u32[]{:S(2)}, u32[]{:S(2)}) %collective-permute-start.28) | collective-permute-done | bytes 262176 | tf_op jit(solution)/shard_map/ppermute | solution.py:25
  67.2 3.0 %shard_map.73 = (bf16[512,2048]{1,0:T(8,128)(2,1)S(1)}, bf16[64,2048]{1,0:T(8,128)(2,1)S(1)}, f32[64,2048]{1,0:T(8,128)S(1)}) custom-call(s32[4]{0:T(128)S(1)} %pad_add_fusion.scalars, bf16[512,2048]{1,0:T(8,128)(2,1)S(1)} %get-tuple-element.88.refs_0_, bf16[128,512]{1,0:T(8,128)(2,1)S(1)} %get-tuple-element.89.refs_1_, ...), custom_call_target="tpu_custom_call" | custom-call | tf_op jit(solution)/shard_map/pallas_call | solution.py:329
  70.2 1.6 %collective-permute-start.30 = (bf16[64,2048]{1,0:T(8,128)(2,1)S(1)}, bf16[64,2048]{1,0:T(8,128)(2,1)S(1)}, u32[]{:S(2)}, u32[]{:S(2)}) collective-permute-start(bf16[64,2048]{1,0:T(8,128)(2,1)S(1)} %get-tuple-element.104), channel_id=1, source_target_pairs={{0,2},{1,3},{2,0},{3,1},{4,6},{5,7},{6,4},{7,5},{8,10},{9,11},{10,... | collective-permute-start | bytes 786440 | tf_op jit(solution)/shard_map/ppermute | solution.py:25
  71.7 6.9 %collective-permute-done.30.refs_6_ = bf16[64,2048]{1,0:T(8,128)(2,1)S(1)} collective-permute-done((bf16[64,2048]{1,0:T(8,128)(2,1)S(1)}, bf16[64,2048]{1,0:T(8,128)(2,1)S(1)}, u32[]{:S(2)}, u32[]{:S(2)}) %collective-permute-start.30) | collective-permute-done | bytes 262176 | tf_op jit(solution)/shard_map/ppermute | solution.py:25
  78.6 2.9 %shard_map.74 = (bf16[64,1024]{1,0:T(8,128)(2,1)S(1)}, f32[64,1024]{1,0:T(8,128)S(1)}) custom-call(s32[4]{0:T(128)S(1)} %pad_add_fusion.scalars, bf16[512,2048]{1,0:T(8,128)(2,1)S(1)} %get-tuple-element.88.refs_0_, bf16[128,512]{1,0:T(8,128)(2,1)S(1)} %get-tuple-element.89.refs_1_, bf16[512,2048]{1,0:T(8,128)(2,1)S(1)} %get-tuple-element.102.refs_2_, ...), custom_call_target="tpu_custom_call" | custom-call | tf_op jit(solution)/shard_map/pallas_call | solution.py:329
  83.5 1.6 %collective-permute-start.32 = (bf16[64,512]{1,0:T(8,128)(2,1)S(1)}, bf16[64,512]{1,0:T(8,128)(2,1)S(1)}, u32[]{:S(2)}, u32[]{:S(2)}) collective-permute-start(bf16[64,512]{1,0:T(8,128)(2,1)S(1)} %get-tuple-element.108), channel_id=1, source_target_pairs={{0,2},{1,3},{2,0},{3,1},{4,6},{5,7},{6,4},{7,5},{8,10},{9,11},{10,... | collective-permute-start | bytes 196616 | tf_op jit(solution)/shard_map/ppermute | solution.py:25
  85.0 2.8 %collective-permute-done.32.came = bf16[64,512]{1,0:T(8,128)(2,1)S(1)} collective-permute-done((bf16[64,512]{1,0:T(8,128)(2,1)S(1)}, bf16[64,512]{1,0:T(8,128)(2,1)S(1)}, u32[]{:S(2)}, u32[]{:S(2)}) %collective-permute-start.32) | collective-permute-done | bytes 65568 | tf_op jit(solution)/shard_map/ppermute | solution.py:25
  87.8 3.5 %collective-permute-start.33 = (bf16[64,512]{1,0:T(8,128)(2,1)S(1)}, bf16[64,512]{1,0:T(8,128)(2,1)S(1)}, u32[]{:S(2)}, u32[]{:S(2)}) collective-permute-start(bf16[64,512]{1,0:T(8,128)(2,1)S(1)} %shard_map.76.refs_0_), channel_id=1, source_target_pairs={{0,16},{4,20},{8,24},{12,28},{16,0},{20,4},{24,8},{28,12},{1,17},{... | collective-permute-start | bytes 196616 | tf_op jit(solution)/shard_map/ppermute | solution.py:25
  91.4 2.0 %collective-permute-start.34 = (bf16[64,512]{1,0:T(8,128)(2,1)S(1)}, bf16[64,512]{1,0:T(8,128)(2,1)S(1)}, u32[]{:S(2)}, u32[]{:S(2)}) collective-permute-start(bf16[64,512]{1,0:T(8,128)(2,1)S(1)} %shard_map.76.refs_0_), channel_id=1, source_target_pairs={{0,24},{4,28},{8,16},{12,20},{16,8},{20,12},{24,0},{28,4},{1,25},{... | collective-permute-start | bytes 196616 | tf_op jit(solution)/shard_map/ppermute | solution.py:25
  93.6 2.1 %collective-permute-start.36 = (bf16[64,512]{1,0:T(8,128)(2,1)S(1)}, bf16[64,512]{1,0:T(8,128)(2,1)S(1)}, u32[]{:S(2)}, u32[]{:S(2)}) collective-permute-start(bf16[64,512]{1,0:T(8,128)(2,1)S(1)} %shard_map.76.refs_0_), channel_id=1, source_target_pairs={{0,20},{4,16},{8,28},{12,24},{16,4},{20,0},{24,12},{28,8},{1,21},{... | collective-permute-start | bytes 196616 | tf_op jit(solution)/shard_map/ppermute | solution.py:25
  95.7 3.0 %collective-permute-start.37 = (bf16[64,512]{1,0:T(8,128)(2,1)S(1)}, bf16[64,512]{1,0:T(8,128)(2,1)S(1)}, u32[]{:S(2)}, u32[]{:S(2)}) collective-permute-start(bf16[64,512]{1,0:T(8,128)(2,1)S(1)} %shard_map.76.refs_0_), channel_id=1, source_target_pairs={{0,28},{4,24},{8,20},{12,16},{16,12},{20,8},{24,4},{28,0},{1,29},{... | collective-permute-start | bytes 196616 | tf_op jit(solution)/shard_map/ppermute | solution.py:25
  98.7 1.5 %collective-permute-start.39 = (bf16[64,512]{1,0:T(8,128)(2,1)S(1)}, bf16[64,512]{1,0:T(8,128)(2,1)S(1)}, u32[]{:S(2)}, u32[]{:S(2)}) collective-permute-start(bf16[64,512]{1,0:T(8,128)(2,1)S(1)} %shard_map.76.refs_0_), channel_id=1, source_target_pairs={{0,4},{4,0},{8,12},{12,8},{16,20},{20,16},{24,28},{28,24},{1,5},{5... | collective-permute-start | bytes 196616 | tf_op jit(solution)/shard_map/ppermute | solution.py:25
  100.3 2.7 %collective-permute-done.36.refs_4_ = bf16[64,512]{1,0:T(8,128)(2,1)S(1)} collective-permute-done((bf16[64,512]{1,0:T(8,128)(2,1)S(1)}, bf16[64,512]{1,0:T(8,128)(2,1)S(1)}, u32[]{:S(2)}, u32[]{:S(2)}) %collective-permute-start.36) | collective-permute-done | bytes 65568 | tf_op jit(solution)/shard_map/ppermute | solution.py:25
  104.3 1.8 %shard_map.77 = f32[512,512]{1,0:T(8,128)} custom-call(s32[4]{0:T(128)S(1)} %pad_add_fusion.scalars, bf16[64,512]{1,0:T(8,128)(2,1)S(1)} %shard_map.76.refs_0_, bf16[64,512]{1,0:T(8,128)(2,1)S(1)} %collective-permute-done.33.refs_1_, bf16[64,512]{1,0:T(8,128)(2,1)S(1)} %collective-permute-done.34.refs_2_, ...), custom_call_target="tpu_custom_call" | custom-call | tf_op jit(solution)/shard_map/pallas_call | solution.py:329
  (74 shorter events, 20.0 us)
Async XLA Ops:
  0.0 22.4 %collective-permute-start = (bf16[128,2048]{1,0:T(8,128)(2,1)}, bf16[128,2048]{1,0:T(8,128)(2,1)S(1)}, u32[]{:S(2)}, u32[]{:S(2)}) collective-permute-start(bf16[128,2048]{1,0:T(8,128)(2,1)} %param.6), channel_id=1, source_target_pairs={{0,4},{4,0},{8,12},{12,8},{16,20},{20,16},{24,28},{28,24},{1,5},{5... | collective-permute-start | bytes 1572872 | tf_op jit(solution)/shard_map/ppermute | solution.py:25
  4.0 14.1 %collective-permute-start.1 = (bf16[64,2048]{1,0:T(8,128)(2,1)S(1)}, bf16[64,2048]{1,0:T(8,128)(2,1)S(1)}, u32[]{:S(2)}, u32[]{:S(2)}) collective-permute-start(bf16[64,2048]{1,0:T(8,128)(2,1)S(1)} %get-tuple-element.110.refs_0_), channel_id=1, source_target_pairs={{0,8},{4,12},{8,0},{12,4},{16,24},{20,28},{24,16},{28,20},{1,9},{5... | collective-permute-start | bytes 786440 | tf_op jit(solution)/shard_map/ppermute | solution.py:25
  5.7 12.8 %collective-permute-start.7 = (bf16[64,2048]{1,0:T(8,128)(2,1)S(1)}, bf16[64,2048]{1,0:T(8,128)(2,1)S(1)}, u32[]{:S(2)}, u32[]{:S(2)}) collective-permute-start(bf16[64,2048]{1,0:T(8,128)(2,1)S(1)} %get-tuple-element.110.refs_0_), channel_id=1, source_target_pairs={{0,16},{4,20},{8,24},{12,28},{16,0},{20,4},{24,8},{28,12},{1,17},{... | collective-permute-start | bytes 786440 | tf_op jit(solution)/shard_map/ppermute | solution.py:25
  12.3 10.1 %collective-permute-start.3 = (bf16[272,128]{1,0:T(8,128)(2,1)S(1)}, bf16[272,128]{1,0:T(8,128)(2,1)S(1)}, u32[]{:S(2)}, u32[]{:S(2)}) collective-permute-start(bf16[272,128]{1,0:T(8,128)(2,1)S(1)} %get-tuple-element.58), channel_id=1, source_target_pairs={{0,8},{4,12},{8,0},{12,4},{16,24},{20,28},{24,16},{28,20},{1,9},{5... | collective-permute-start | bytes 208904 | tf_op jit(solution)/shard_map/ppermute | solution.py:25
  18.1 14.8 %collective-permute-start.2 = (bf16[64,2048]{1,0:T(8,128)(2,1)S(1)}, bf16[64,2048]{1,0:T(8,128)(2,1)S(1)}, u32[]{:S(2)}, u32[]{:S(2)}) collective-permute-start(bf16[64,2048]{1,0:T(8,128)(2,1)S(1)} %get-tuple-element.64.refs_1_), channel_id=1, source_target_pairs={{0,8},{4,12},{8,0},{12,4},{16,24},{20,28},{24,16},{28,20},{1,9},{5... | collective-permute-start | bytes 786440 | tf_op jit(solution)/shard_map/ppermute | solution.py:25
  18.4 11.0 %collective-permute-start.8 = (bf16[64,2048]{1,0:T(8,128)(2,1)S(1)}, bf16[64,2048]{1,0:T(8,128)(2,1)S(1)}, u32[]{:S(2)}, u32[]{:S(2)}) collective-permute-start(bf16[64,2048]{1,0:T(8,128)(2,1)S(1)} %get-tuple-element.64.refs_1_), channel_id=1, source_target_pairs={{0,16},{4,20},{8,24},{12,28},{16,0},{20,4},{24,8},{28,12},{1,17},{... | collective-permute-start | bytes 786440 | tf_op jit(solution)/shard_map/ppermute | solution.py:25
  22.4 10.5 %collective-permute-start.4 = (bf16[64,2048]{1,0:T(8,128)(2,1)S(1)}, bf16[64,2048]{1,0:T(8,128)(2,1)S(1)}, u32[]{:S(2)}, u32[]{:S(2)}) collective-permute-start(bf16[64,2048]{1,0:T(8,128)(2,1)S(1)} %collective-permute-done.1.refs_3_), channel_id=1, source_target_pairs={{0,4},{4,0},{8,12},{12,8},{16,20},{20,16},{24,28},{28,24},{1,5},{5... | collective-permute-start | bytes 786440 | tf_op jit(solution)/shard_map/ppermute | solution.py:25
  23.5 9.4 %collective-permute-start.5 = (bf16[144,256]{1,0:T(8,128)(2,1)S(1)}, bf16[144,256]{1,0:T(8,128)(2,1)S(1)}, u32[]{:S(2)}, u32[]{:S(2)}) collective-permute-start(bf16[144,256]{1,0:T(8,128)(2,1)S(1)} %get-tuple-element.62), channel_id=1, source_target_pairs={{0,4},{4,0},{8,12},{12,8},{16,20},{20,16},{24,28},{28,24},{1,5},{5... | collective-permute-start | bytes 221192 | tf_op jit(solution)/shard_map/ppermute | solution.py:25
  25.1 11.3 %collective-permute-start.13 = (bf16[64,2048]{1,0:T(8,128)(2,1)S(1)}, bf16[64,2048]{1,0:T(8,128)(2,1)S(1)}, u32[]{:S(2)}, u32[]{:S(2)}) collective-permute-start(bf16[64,2048]{1,0:T(8,128)(2,1)S(1)} %collective-permute-done.7.refs_7_), channel_id=1, source_target_pairs={{0,4},{4,0},{8,12},{12,8},{16,20},{20,16},{24,28},{28,24},{1,5},{5... | collective-permute-start | bytes 786440 | tf_op jit(solution)/shard_map/ppermute | solution.py:25
  29.4 9.2 %collective-permute-start.10 = (bf16[64,2048]{1,0:T(8,128)(2,1)S(1)}, bf16[64,2048]{1,0:T(8,128)(2,1)S(1)}, u32[]{:S(2)}, u32[]{:S(2)}) collective-permute-start(bf16[64,2048]{1,0:T(8,128)(2,1)S(1)} %collective-permute-done.8.refs_8_), channel_id=1, source_target_pairs={{0,8},{4,12},{8,0},{12,4},{16,24},{20,28},{24,16},{28,20},{1,9},{5... | collective-permute-start | bytes 786440 | tf_op jit(solution)/shard_map/ppermute | solution.py:25
  32.9 8.1 %collective-permute-start.6 = (bf16[64,2048]{1,0:T(8,128)(2,1)S(1)}, bf16[64,2048]{1,0:T(8,128)(2,1)S(1)}, u32[]{:S(2)}, u32[]{:S(2)}) collective-permute-start(bf16[64,2048]{1,0:T(8,128)(2,1)S(1)} %collective-permute-done.2.refs_4_), channel_id=1, source_target_pairs={{0,4},{4,0},{8,12},{12,8},{16,20},{20,16},{24,28},{28,24},{1,5},{5... | collective-permute-start | bytes 786440 | tf_op jit(solution)/shard_map/ppermute | solution.py:25
  34.1 10.1 %collective-permute-start.9 = (bf16[64,2048]{1,0:T(8,128)(2,1)S(1)}, bf16[64,2048]{1,0:T(8,128)(2,1)S(1)}, u32[]{:S(2)}, u32[]{:S(2)}) collective-permute-start(bf16[64,2048]{1,0:T(8,128)(2,1)S(1)} %collective-permute-done.7.refs_7_), channel_id=1, source_target_pairs={{0,8},{4,12},{8,0},{12,4},{16,24},{20,28},{24,16},{28,20},{1,9},{5... | collective-permute-start | bytes 786440 | tf_op jit(solution)/shard_map/ppermute | solution.py:25
  34.8 12.1 %collective-permute-start.12 = (bf16[128,512]{1,0:T(8,128)(2,1)S(1)}, bf16[128,512]{1,0:T(8,128)(2,1)S(1)}, u32[]{:S(2)}, u32[]{:S(2)}) collective-permute-start(bf16[128,512]{1,0:T(8,128)(2,1)S(1)} %pad_maximum_fusion), channel_id=1, source_target_pairs={{0,2},{1,3},{2,0},{3,1},{4,6},{5,7},{6,4},{7,5},{8,10},{9,11},{10,... | collective-permute-start | bytes 393224 | tf_op jit(solution)/shard_map/ppermute | solution.py:25
  36.3 15.9 %collective-permute-start.14 = (bf16[64,2048]{1,0:T(8,128)(2,1)S(1)}, bf16[64,2048]{1,0:T(8,128)(2,1)S(1)}, u32[]{:S(2)}, u32[]{:S(2)}) collective-permute-start(bf16[64,2048]{1,0:T(8,128)(2,1)S(1)} %collective-permute-done.8.refs_8_), channel_id=1, source_target_pairs={{0,4},{4,0},{8,12},{12,8},{16,20},{20,16},{24,28},{28,24},{1,5},{5... | collective-permute-start | bytes 786440 | tf_op jit(solution)/shard_map/ppermute | solution.py:25
  38.6 13.6 %collective-permute-start.15 = (bf16[64,2048]{1,0:T(8,128)(2,1)S(1)}, bf16[64,2048]{1,0:T(8,128)(2,1)S(1)}, u32[]{:S(2)}, u32[]{:S(2)}) collective-permute-start(bf16[64,2048]{1,0:T(8,128)(2,1)S(1)} %collective-permute-done.13.refs_0_), channel_id=1, source_target_pairs={{0,8},{4,12},{8,0},{12,4},{16,24},{20,28},{24,16},{28,20},{1,9},{5... | collective-permute-start | bytes 786440 | tf_op jit(solution)/shard_map/ppermute | solution.py:25
  41.0 11.2 %collective-permute-start.16 = (bf16[64,2048]{1,0:T(8,128)(2,1)S(1)}, bf16[64,2048]{1,0:T(8,128)(2,1)S(1)}, u32[]{:S(2)}, u32[]{:S(2)}) collective-permute-start(bf16[64,2048]{1,0:T(8,128)(2,1)S(1)} %collective-permute-done.10.refs_10_), channel_id=1, source_target_pairs={{0,4},{4,0},{8,12},{12,8},{16,20},{20,16},{24,28},{28,24},{1,5},{5... | collective-permute-start | bytes 786440 | tf_op jit(solution)/shard_map/ppermute | solution.py:25
  44.2 5.6 %collective-permute-start.17 = (bf16[80,512]{1,0:T(8,128)(2,1)S(1)}, bf16[80,512]{1,0:T(8,128)(2,1)S(1)}, u32[]{:S(2)}, u32[]{:S(2)}) collective-permute-start(bf16[80,512]{1,0:T(8,128)(2,1)S(1)} %get-tuple-element.77), channel_id=1, source_target_pairs={{0,16},{4,20},{8,24},{12,28},{16,0},{20,4},{24,8},{28,12},{1,17},{... | collective-permute-start | bytes 245768 | tf_op jit(solution)/shard_map/ppermute | solution.py:25
  55.6 8.4 %collective-permute-start.28 = (bf16[128,1024]{1,0:T(8,128)(2,1)S(1)}, bf16[128,1024]{1,0:T(8,128)(2,1)S(1)}, u32[]{:S(2)}, u32[]{:S(2)}) collective-permute-start(bf16[128,1024]{1,0:T(8,128)(2,1)S(1)} %get-tuple-element.99), channel_id=1, source_target_pairs={{0,2},{1,3},{2,0},{3,1},{4,6},{5,7},{6,4},{7,5},{8,10},{9,11},{10,... | collective-permute-start | bytes 786440 | tf_op jit(solution)/shard_map/ppermute | solution.py:25
  59.2 4.8 %collective-permute-start.19 = (bf16[64,2048]{1,0:T(8,128)(2,1)S(1)}, bf16[64,2048]{1,0:T(8,128)(2,1)S(1)}, u32[]{:S(2)}, u32[]{:S(2)}) collective-permute-start(bf16[64,2048]{1,0:T(8,128)(2,1)S(1)} %get-tuple-element.90), channel_id=1, source_target_pairs={{0,1},{1,0},{2,3},{3,2},{4,5},{5,4},{6,7},{7,6},{8,9},{9,8},{10,11... | collective-permute-start | bytes 786440 | tf_op jit(solution)/shard_map/ppermute | solution.py:25
  59.3 5.3 %collective-permute-start.20 = (bf16[64,2048]{1,0:T(8,128)(2,1)S(1)}, bf16[64,2048]{1,0:T(8,128)(2,1)S(1)}, u32[]{:S(2)}, u32[]{:S(2)}) collective-permute-start(bf16[64,2048]{1,0:T(8,128)(2,1)S(1)} %get-tuple-element.91), channel_id=1, source_target_pairs={{0,1},{1,0},{2,3},{3,2},{4,5},{5,4},{6,7},{7,6},{8,9},{9,8},{10,11... | collective-permute-start | bytes 786440 | tf_op jit(solution)/shard_map/ppermute | solution.py:25
  59.9 4.8 %collective-permute-start.21 = (bf16[64,2048]{1,0:T(8,128)(2,1)S(1)}, bf16[64,2048]{1,0:T(8,128)(2,1)S(1)}, u32[]{:S(2)}, u32[]{:S(2)}) collective-permute-start(bf16[64,2048]{1,0:T(8,128)(2,1)S(1)} %get-tuple-element.92), channel_id=1, source_target_pairs={{0,1},{1,0},{2,3},{3,2},{4,5},{5,4},{6,7},{7,6},{8,9},{9,8},{10,11... | collective-permute-start | bytes 786440 | tf_op jit(solution)/shard_map/ppermute | solution.py:25
  61.4 4.4 %collective-permute-start.22 = (bf16[64,2048]{1,0:T(8,128)(2,1)S(1)}, bf16[64,2048]{1,0:T(8,128)(2,1)S(1)}, u32[]{:S(2)}, u32[]{:S(2)}) collective-permute-start(bf16[64,2048]{1,0:T(8,128)(2,1)S(1)} %get-tuple-element.93), channel_id=1, source_target_pairs={{0,1},{1,0},{2,3},{3,2},{4,5},{5,4},{6,7},{7,6},{8,9},{9,8},{10,11... | collective-permute-start | bytes 786440 | tf_op jit(solution)/shard_map/ppermute | solution.py:25
  64.6 2.1 %collective-permute-start.26 = (bf16[64,2048]{1,0:T(8,128)(2,1)S(1)}, bf16[64,2048]{1,0:T(8,128)(2,1)S(1)}, u32[]{:S(2)}, u32[]{:S(2)}) collective-permute-start(bf16[64,2048]{1,0:T(8,128)(2,1)S(1)} %get-tuple-element.97), channel_id=1, source_target_pairs={{0,1},{1,0},{2,3},{3,2},{4,5},{5,4},{6,7},{7,6},{8,9},{9,8},{10,11... | collective-permute-start | bytes 786440 | tf_op jit(solution)/shard_map/ppermute | solution.py:25
  70.2 8.4 %collective-permute-start.30 = (bf16[64,2048]{1,0:T(8,128)(2,1)S(1)}, bf16[64,2048]{1,0:T(8,128)(2,1)S(1)}, u32[]{:S(2)}, u32[]{:S(2)}) collective-permute-start(bf16[64,2048]{1,0:T(8,128)(2,1)S(1)} %get-tuple-element.104), channel_id=1, source_target_pairs={{0,2},{1,3},{2,0},{3,1},{4,6},{5,7},{6,4},{7,5},{8,10},{9,11},{10,... | collective-permute-start | bytes 786440 | tf_op jit(solution)/shard_map/ppermute | solution.py:25
  83.5 4.3 %collective-permute-start.32 = (bf16[64,512]{1,0:T(8,128)(2,1)S(1)}, bf16[64,512]{1,0:T(8,128)(2,1)S(1)}, u32[]{:S(2)}, u32[]{:S(2)}) collective-permute-start(bf16[64,512]{1,0:T(8,128)(2,1)S(1)} %get-tuple-element.108), channel_id=1, source_target_pairs={{0,2},{1,3},{2,0},{3,1},{4,6},{5,7},{6,4},{7,5},{8,10},{9,11},{10,... | collective-permute-start | bytes 196616 | tf_op jit(solution)/shard_map/ppermute | solution.py:25
  87.8 10.8 %collective-permute-start.33 = (bf16[64,512]{1,0:T(8,128)(2,1)S(1)}, bf16[64,512]{1,0:T(8,128)(2,1)S(1)}, u32[]{:S(2)}, u32[]{:S(2)}) collective-permute-start(bf16[64,512]{1,0:T(8,128)(2,1)S(1)} %shard_map.76.refs_0_), channel_id=1, source_target_pairs={{0,16},{4,20},{8,24},{12,28},{16,0},{20,4},{24,8},{28,12},{1,17},{... | collective-permute-start | bytes 196616 | tf_op jit(solution)/shard_map/ppermute | solution.py:25
  91.4 7.3 %collective-permute-start.34 = (bf16[64,512]{1,0:T(8,128)(2,1)S(1)}, bf16[64,512]{1,0:T(8,128)(2,1)S(1)}, u32[]{:S(2)}, u32[]{:S(2)}) collective-permute-start(bf16[64,512]{1,0:T(8,128)(2,1)S(1)} %shard_map.76.refs_0_), channel_id=1, source_target_pairs={{0,24},{4,28},{8,16},{12,20},{16,8},{20,12},{24,0},{28,4},{1,25},{... | collective-permute-start | bytes 196616 | tf_op jit(solution)/shard_map/ppermute | solution.py:25
  93.4 6.9 %collective-permute-start.35 = (bf16[64,512]{1,0:T(8,128)(2,1)S(1)}, bf16[64,512]{1,0:T(8,128)(2,1)S(1)}, u32[]{:S(2)}, u32[]{:S(2)}) collective-permute-start(bf16[64,512]{1,0:T(8,128)(2,1)S(1)} %shard_map.76.refs_0_), channel_id=1, source_target_pairs={{0,8},{4,12},{8,0},{12,4},{16,24},{20,28},{24,16},{28,20},{1,9},{5... | collective-permute-start | bytes 196616 | tf_op jit(solution)/shard_map/ppermute | solution.py:25
  93.6 9.4 %collective-permute-start.36 = (bf16[64,512]{1,0:T(8,128)(2,1)S(1)}, bf16[64,512]{1,0:T(8,128)(2,1)S(1)}, u32[]{:S(2)}, u32[]{:S(2)}) collective-permute-start(bf16[64,512]{1,0:T(8,128)(2,1)S(1)} %shard_map.76.refs_0_), channel_id=1, source_target_pairs={{0,20},{4,16},{8,28},{12,24},{16,4},{20,0},{24,12},{28,8},{1,21},{... | collective-permute-start | bytes 196616 | tf_op jit(solution)/shard_map/ppermute | solution.py:25
  95.7 7.3 %collective-permute-start.37 = (bf16[64,512]{1,0:T(8,128)(2,1)S(1)}, bf16[64,512]{1,0:T(8,128)(2,1)S(1)}, u32[]{:S(2)}, u32[]{:S(2)}) collective-permute-start(bf16[64,512]{1,0:T(8,128)(2,1)S(1)} %shard_map.76.refs_0_), channel_id=1, source_target_pairs={{0,28},{4,24},{8,20},{12,16},{16,12},{20,8},{24,4},{28,0},{1,29},{... | collective-permute-start | bytes 196616 | tf_op jit(solution)/shard_map/ppermute | solution.py:25
  98.7 5.2 %collective-permute-start.38 = (bf16[64,512]{1,0:T(8,128)(2,1)S(1)}, bf16[64,512]{1,0:T(8,128)(2,1)S(1)}, u32[]{:S(2)}, u32[]{:S(2)}) collective-permute-start(bf16[64,512]{1,0:T(8,128)(2,1)S(1)} %shard_map.76.refs_0_), channel_id=1, source_target_pairs={{0,12},{4,8},{8,4},{12,0},{16,28},{20,24},{24,20},{28,16},{1,13},{... | collective-permute-start | bytes 196616 | tf_op jit(solution)/shard_map/ppermute | solution.py:25
  98.7 5.6 %collective-permute-start.39 = (bf16[64,512]{1,0:T(8,128)(2,1)S(1)}, bf16[64,512]{1,0:T(8,128)(2,1)S(1)}, u32[]{:S(2)}, u32[]{:S(2)}) collective-permute-start(bf16[64,512]{1,0:T(8,128)(2,1)S(1)} %shard_map.76.refs_0_), channel_id=1, source_target_pairs={{0,4},{4,0},{8,12},{12,8},{16,20},{20,16},{24,28},{28,24},{1,5},{5... | collective-permute-start | bytes 196616 | tf_op jit(solution)/shard_map/ppermute | solution.py:25
  (11 other events, 19.7 us)

commit v7 on v6

--- a/solution.py
+++ b/solution.py
@@ -460,12 +460,12 @@
     labels = after(labels, summed)
     taken = ((dp // 2 * rows, features), BF)
     beside = ((2 * wide, dp // 2 * rows), BF)
-    cut = ((half_rows, features), BF)
+    cut = ((rows, features), BF)
     own, own_side, sent_side, *sent = run(
         functools.partial(sort_kernel, sizes, rows),
         [scalars, adv_rate],
         [held_early, primal_early, held_late, primal_late, up, labels],
-        [taken, beside, beside] + [cut] * dp,
+        [taken, beside, beside] + [cut] * (dp // 2),
         [taken],
     )
     came_side = swap(sent_side, "fsdp", 1)

time: 106 us -> 106 us (level)
  starting transfers between devices: 46.2 us -> 45.1 us
    ppermute x40 -> x36, starting transfers between devices: 46.2 us -> 45.1 us  [swap(): lax.ppermute(value, axis, [(i, i ^ bit) for i in range(lax.axis_size(axis...]
    ppermute x40 -> x36, waiting for transfers between devices: 38.2 us -> 39 us  [swap(): lax.ppermute(value, axis, [(i, i ^ bit) for i in range(lax.axis_size(axis...]
  transfers between devices with their start and end apart: 40 -> 36, of which waited for: 20 -> 17; matrix products, arithmetic and copies ran while one was open for 1% -> 1% of each run, Pallas kernels for 7% -> 7%
where the time goes in v7:
time: 106 us
  starting transfers between devices  45.1 us (43%)
  waiting for transfers between devices  39 us (37%)
  Pallas kernels  17 us (16%)
  local copies, waits for them, and re-layouts  3.04 us (3%)
  between operations  1.49 us (1%)
    ppermute x36, starting transfers between devices, swap(): lax.ppermute(value, axis, [(i, i ^ bit) for i in range(lax.axis_size(axis...  45.1 us
    ppermute x36, waiting for transfers between devices, swap(): lax.ppermute(value, axis, [(i, i ^ bit) for i in range(lax.axis_size(axis...  39 us
    pallas_call x14, Pallas kernels, run(): pl.pallas_call(kernel, out_shape=[jax.ShapeDtypeStruct(s, t) for s, t in...  17 us
  transfers between devices with their start and end apart: 36, of which 17 were waited for; matrix products, arithmetic and copies ran while one was open for 1% of the time, Pallas kernels for 7%

profile of v7, /device:TPU:0, one launch (start us, length us, event | category | flops | bytes accessed | tf_op | source)
XLA Modules:
  0.0 105.6 jit_solution(2925993832205245149)
XLA Ops:
  0.0 3.0 %collective-permute-start = (bf16[128,2048]{1,0:T(8,128)(2,1)}, bf16[128,2048]{1,0:T(8,128)(2,1)S(1)}, u32[]{:S(2)}, u32[]{:S(2)}) collective-permute-start(bf16[128,2048]{1,0:T(8,128)(2,1)} %param.6), channel_id=1, source_target_pairs={{0,4},{4,0},{8,12},{12,8},{16,20},{20,16},{24,28},{28,24},{1,5},{5... | collective-permute-start | bytes 1572872 | tf_op jit(solution)/shard_map/ppermute | solution.py:25
  4.0 1.6 %collective-permute-start.1 = (bf16[64,2048]{1,0:T(8,128)(2,1)S(1)}, bf16[64,2048]{1,0:T(8,128)(2,1)S(1)}, u32[]{:S(2)}, u32[]{:S(2)}) collective-permute-start(bf16[64,2048]{1,0:T(8,128)(2,1)S(1)} %get-tuple-element.102.refs_0_), channel_id=1, source_target_pairs={{0,8},{4,12},{8,0},{12,4},{16,24},{20,28},{24,16},{28,20},{1,9},{5... | collective-permute-start | bytes 786440 | tf_op jit(solution)/shard_map/ppermute | solution.py:25
  5.7 2.6 %collective-permute-start.7 = (bf16[64,2048]{1,0:T(8,128)(2,1)S(1)}, bf16[64,2048]{1,0:T(8,128)(2,1)S(1)}, u32[]{:S(2)}, u32[]{:S(2)}) collective-permute-start(bf16[64,2048]{1,0:T(8,128)(2,1)S(1)} %get-tuple-element.102.refs_0_), channel_id=1, source_target_pairs={{0,16},{4,20},{8,24},{12,28},{16,0},{20,4},{24,8},{28,12},{1,17},{... | collective-permute-start | bytes 786440 | tf_op jit(solution)/shard_map/ppermute | solution.py:25
  12.8 5.3 %collective-permute-done.1.refs_3_ = bf16[64,2048]{1,0:T(8,128)(2,1)S(1)} collective-permute-done((bf16[64,2048]{1,0:T(8,128)(2,1)S(1)}, bf16[64,2048]{1,0:T(8,128)(2,1)S(1)}, u32[]{:S(2)}, u32[]{:S(2)}) %collective-permute-start.1) | collective-permute-done | bytes 262176 | tf_op jit(solution)/shard_map/ppermute | solution.py:25
  18.4 4.0 %collective-permute-start.8 = (bf16[64,2048]{1,0:T(8,128)(2,1)S(1)}, bf16[64,2048]{1,0:T(8,128)(2,1)S(1)}, u32[]{:S(2)}, u32[]{:S(2)}) collective-permute-start(bf16[64,2048]{1,0:T(8,128)(2,1)S(1)} %get-tuple-element.60.refs_1_), channel_id=1, source_target_pairs={{0,16},{4,20},{8,24},{12,28},{16,0},{20,4},{24,8},{28,12},{1,17},{... | collective-permute-start | bytes 786440 | tf_op jit(solution)/shard_map/ppermute | solution.py:25
  23.5 1.6 %collective-permute-start.5 = (bf16[144,256]{1,0:T(8,128)(2,1)S(1)}, bf16[144,256]{1,0:T(8,128)(2,1)S(1)}, u32[]{:S(2)}, u32[]{:S(2)}) collective-permute-start(bf16[144,256]{1,0:T(8,128)(2,1)S(1)} %get-tuple-element.58), channel_id=1, source_target_pairs={{0,4},{4,0},{8,12},{12,8},{16,20},{20,16},{24,28},{28,24},{1,5},{5... | collective-permute-start | bytes 221192 | tf_op jit(solution)/shard_map/ppermute | solution.py:25
  25.6 3.8 %collective-permute-done.8.refs_8_ = bf16[64,2048]{1,0:T(8,128)(2,1)S(1)} collective-permute-done((bf16[64,2048]{1,0:T(8,128)(2,1)S(1)}, bf16[64,2048]{1,0:T(8,128)(2,1)S(1)}, u32[]{:S(2)}, u32[]{:S(2)}) %collective-permute-start.8) | collective-permute-done | bytes 262176 | tf_op jit(solution)/shard_map/ppermute | solution.py:25
  29.4 3.5 %collective-permute-start.10 = (bf16[64,2048]{1,0:T(8,128)(2,1)S(1)}, bf16[64,2048]{1,0:T(8,128)(2,1)S(1)}, u32[]{:S(2)}, u32[]{:S(2)}) collective-permute-start(bf16[64,2048]{1,0:T(8,128)(2,1)S(1)} %collective-permute-done.8.refs_8_), channel_id=1, source_target_pairs={{0,8},{4,12},{8,0},{12,4},{16,24},{20,28},{24,16},{28,20},{1,9},{5... | collective-permute-start | bytes 786440 | tf_op jit(solution)/shard_map/ppermute | solution.py:25
  34.8 1.6 %collective-permute-start.12 = (bf16[128,512]{1,0:T(8,128)(2,1)S(1)}, bf16[128,512]{1,0:T(8,128)(2,1)S(1)}, u32[]{:S(2)}, u32[]{:S(2)}) collective-permute-start(bf16[128,512]{1,0:T(8,128)(2,1)S(1)} %pad_maximum_fusion), channel_id=1, source_target_pairs={{0,2},{1,3},{2,0},{3,1},{4,6},{5,7},{6,4},{7,5},{8,10},{9,11},{10,... | collective-permute-start | bytes 393224 | tf_op jit(solution)/shard_map/ppermute | solution.py:25
  38.6 2.5 %collective-permute-start.15 = (bf16[64,2048]{1,0:T(8,128)(2,1)S(1)}, bf16[64,2048]{1,0:T(8,128)(2,1)S(1)}, u32[]{:S(2)}, u32[]{:S(2)}) collective-permute-start(bf16[64,2048]{1,0:T(8,128)(2,1)S(1)} %collective-permute-done.13.refs_0_), channel_id=1, source_target_pairs={{0,8},{4,12},{8,0},{12,4},{16,24},{20,28},{24,16},{28,20},{1,9},{5... | collective-permute-start | bytes 786440 | tf_op jit(solution)/shard_map/ppermute | solution.py:25
  41.1 3.1 %collective-permute-done.9.refs_9_ = bf16[64,2048]{1,0:T(8,128)(2,1)S(1)} collective-permute-done((bf16[64,2048]{1,0:T(8,128)(2,1)S(1)}, bf16[64,2048]{1,0:T(8,128)(2,1)S(1)}, u32[]{:S(2)}, u32[]{:S(2)}) %collective-permute-start.9) | collective-permute-done | bytes 262176 | tf_op jit(solution)/shard_map/ppermute | solution.py:25
  44.2 2.7 %collective-permute-start.17 = (bf16[80,512]{1,0:T(8,128)(2,1)S(1)}, bf16[80,512]{1,0:T(8,128)(2,1)S(1)}, u32[]{:S(2)}, u32[]{:S(2)}) collective-permute-start(bf16[80,512]{1,0:T(8,128)(2,1)S(1)} %get-tuple-element.73), channel_id=1, source_target_pairs={{0,16},{4,20},{8,24},{12,28},{16,0},{20,4},{24,8},{28,12},{1,17},{... | collective-permute-start | bytes 245768 | tf_op jit(solution)/shard_map/ppermute | solution.py:25
  46.9 2.9 %collective-permute-done.17.came = bf16[80,512]{1,0:T(8,128)(2,1)S(1)} collective-permute-done((bf16[80,512]{1,0:T(8,128)(2,1)S(1)}, bf16[80,512]{1,0:T(8,128)(2,1)S(1)}, u32[]{:S(2)}, u32[]{:S(2)}) %collective-permute-start.17) | collective-permute-done | bytes 81952 | tf_op jit(solution)/shard_map/ppermute | solution.py:25
  50.4 1.8 %shard_map.66 = (bf16[768,2048]{1,0:T(8,128)(2,1)S(1)}, f32[64,768]{1,0:T(8,128)S(1)}) custom-call(s32[4]{0:T(128)S(1)} %pad_add_fusion.scalars, bf16[64,2048]{1,0:T(8,128)(2,1)S(1)} %get-tuple-element.102.refs_0_, bf16[64,2048]{1,0:T(8,128)(2,1)S(1)} %get-tuple-element.60.refs_1_, bf16[128,2048]{1,0:T(8,128)(2,1)S(1)} %collective-permute-done.refs_2_, ...), custom_call_target="tpu_custom_call" | custom-call | tf_op jit(solution)/shard_map/pallas_call | solution.py:329
  52.2 1.7 %shard_map.69 = (bf16[256,2048]{1,0:T(8,128)(2,1)S(1)}, f32[64,256]{1,0:T(8,128)S(1)}, bf16[64,1024]{1,0:T(8,128)(2,1)S(1)}, bf16[16,1024]{1,0:T(8,128)(2,1)S(1)...) custom-call(s32[4]{0:T(128)S(1)} %pad_add_fusion.scalars, ...), custom_call_target="tpu_custom_call" | custom-call | tf_op jit(solution)/shard_map/pallas_call | solution.py:329
  54.0 1.5 %collective-permute-done.18.came = bf16[128,1024]{1,0:T(8,128)(2,1)S(1)} collective-permute-done((bf16[128,1024]{1,0:T(8,128)(2,1)S(1)}, bf16[128,1024]{1,0:T(8,128)(2,1)S(1)}, u32[]{:S(2)}, u32[]{:S(2)}) %collective-permute-start.18) | collective-permute-done | bytes 262176 | tf_op jit(solution)/shard_map/ppermute | solution.py:25
  55.6 1.6 %collective-permute-start.24 = (bf16[128,1024]{1,0:T(8,128)(2,1)S(1)}, bf16[128,1024]{1,0:T(8,128)(2,1)S(1)}, u32[]{:S(2)}, u32[]{:S(2)}) collective-permute-start(bf16[128,1024]{1,0:T(8,128)(2,1)S(1)} %get-tuple-element.91), channel_id=1, source_target_pairs={{0,2},{1,3},{2,0},{3,1},{4,6},{5,7},{6,4},{7,5},{8,10},{9,11},{10,... | collective-permute-start | bytes 786440 | tf_op jit(solution)/shard_map/ppermute | solution.py:25
  57.2 2.0 %shard_map.71 = (bf16[512,2048]{1,0:T(8,128)(2,1)S(1)}, bf16[128,512]{1,0:T(8,128)(2,1)S(1)}, bf16[128,512]{1,0:T(8,128)(2,1)S(1)}, bf16[128,2048]{1,0:T(8,128)(...) custom-call(s32[4]{0:T(128)S(1)} %pad_add_fusion.scalars, ...), custom_call_target="tpu_custom_call" | custom-call | tf_op jit(solution)/shard_map/pallas_call | solution.py:329
  60.3 3.8 %collective-permute-done.24.came = bf16[128,1024]{1,0:T(8,128)(2,1)S(1)} collective-permute-done((bf16[128,1024]{1,0:T(8,128)(2,1)S(1)}, bf16[128,1024]{1,0:T(8,128)(2,1)S(1)}, u32[]{:S(2)}, u32[]{:S(2)}) %collective-permute-start.24) | collective-permute-done | bytes 262176 | tf_op jit(solution)/shard_map/ppermute | solution.py:25
  66.8 3.0 %shard_map.73 = (bf16[512,2048]{1,0:T(8,128)(2,1)S(1)}, bf16[64,2048]{1,0:T(8,128)(2,1)S(1)}, f32[64,2048]{1,0:T(8,128)S(1)}) custom-call(s32[4]{0:T(128)S(1)} %pad_add_fusion.scalars, bf16[512,2048]{1,0:T(8,128)(2,1)S(1)} %get-tuple-element.84.refs_0_, bf16[128,512]{1,0:T(8,128)(2,1)S(1)} %get-tuple-element.85.refs_1_, ...), custom_call_target="tpu_custom_call" | custom-call | tf_op jit(solution)/shard_map/pallas_call | solution.py:329
  69.8 1.6 %collective-permute-start.26 = (bf16[64,2048]{1,0:T(8,128)(2,1)S(1)}, bf16[64,2048]{1,0:T(8,128)(2,1)S(1)}, u32[]{:S(2)}, u32[]{:S(2)}) collective-permute-start(bf16[64,2048]{1,0:T(8,128)(2,1)S(1)} %get-tuple-element.96), channel_id=1, source_target_pairs={{0,2},{1,3},{2,0},{3,1},{4,6},{5,7},{6,4},{7,5},{8,10},{9,11},{10,... | collective-permute-start | bytes 786440 | tf_op jit(solution)/shard_map/ppermute | solution.py:25
  71.3 6.9 %collective-permute-done.26.refs_6_ = bf16[64,2048]{1,0:T(8,128)(2,1)S(1)} collective-permute-done((bf16[64,2048]{1,0:T(8,128)(2,1)S(1)}, bf16[64,2048]{1,0:T(8,128)(2,1)S(1)}, u32[]{:S(2)}, u32[]{:S(2)}) %collective-permute-start.26) | collective-permute-done | bytes 262176 | tf_op jit(solution)/shard_map/ppermute | solution.py:25
  78.2 2.9 %shard_map.74 = (bf16[64,1024]{1,0:T(8,128)(2,1)S(1)}, f32[64,1024]{1,0:T(8,128)S(1)}) custom-call(s32[4]{0:T(128)S(1)} %pad_add_fusion.scalars, bf16[512,2048]{1,0:T(8,128)(2,1)S(1)} %get-tuple-element.84.refs_0_, bf16[128,512]{1,0:T(8,128)(2,1)S(1)} %get-tuple-element.85.refs_1_, bf16[512,2048]{1,0:T(8,128)(2,1)S(1)} %get-tuple-element.94.refs_2_, ...), custom_call_target="tpu_custom_call" | custom-call | tf_op jit(solution)/shard_map/pallas_call | solution.py:329
  83.1 1.6 %collective-permute-start.28 = (bf16[64,512]{1,0:T(8,128)(2,1)S(1)}, bf16[64,512]{1,0:T(8,128)(2,1)S(1)}, u32[]{:S(2)}, u32[]{:S(2)}) collective-permute-start(bf16[64,512]{1,0:T(8,128)(2,1)S(1)} %get-tuple-element.100), channel_id=1, source_target_pairs={{0,2},{1,3},{2,0},{3,1},{4,6},{5,7},{6,4},{7,5},{8,10},{9,11},{10,... | collective-permute-start | bytes 196616 | tf_op jit(solution)/shard_map/ppermute | solution.py:25
  84.6 2.8 %collective-permute-done.28.came = bf16[64,512]{1,0:T(8,128)(2,1)S(1)} collective-permute-done((bf16[64,512]{1,0:T(8,128)(2,1)S(1)}, bf16[64,512]{1,0:T(8,128)(2,1)S(1)}, u32[]{:S(2)}, u32[]{:S(2)}) %collective-permute-start.28) | collective-permute-done | bytes 65568 | tf_op jit(solution)/shard_map/ppermute | solution.py:25
  87.4 3.5 %collective-permute-start.29 = (bf16[64,512]{1,0:T(8,128)(2,1)S(1)}, bf16[64,512]{1,0:T(8,128)(2,1)S(1)}, u32[]{:S(2)}, u32[]{:S(2)}) collective-permute-start(bf16[64,512]{1,0:T(8,128)(2,1)S(1)} %shard_map.76.refs_0_), channel_id=1, source_target_pairs={{0,16},{4,20},{8,24},{12,28},{16,0},{20,4},{24,8},{28,12},{1,17},{... | collective-permute-start | bytes 196616 | tf_op jit(solution)/shard_map/ppermute | solution.py:25
  91.0 2.0 %collective-permute-start.30 = (bf16[64,512]{1,0:T(8,128)(2,1)S(1)}, bf16[64,512]{1,0:T(8,128)(2,1)S(1)}, u32[]{:S(2)}, u32[]{:S(2)}) collective-permute-start(bf16[64,512]{1,0:T(8,128)(2,1)S(1)} %shard_map.76.refs_0_), channel_id=1, source_target_pairs={{0,24},{4,28},{8,16},{12,20},{16,8},{20,12},{24,0},{28,4},{1,25},{... | collective-permute-start | bytes 196616 | tf_op jit(solution)/shard_map/ppermute | solution.py:25
  93.2 2.1 %collective-permute-start.32 = (bf16[64,512]{1,0:T(8,128)(2,1)S(1)}, bf16[64,512]{1,0:T(8,128)(2,1)S(1)}, u32[]{:S(2)}, u32[]{:S(2)}) collective-permute-start(bf16[64,512]{1,0:T(8,128)(2,1)S(1)} %shard_map.76.refs_0_), channel_id=1, source_target_pairs={{0,20},{4,16},{8,28},{12,24},{16,4},{20,0},{24,12},{28,8},{1,21},{... | collective-permute-start | bytes 196616 | tf_op jit(solution)/shard_map/ppermute | solution.py:25
  95.3 3.0 %collective-permute-start.33 = (bf16[64,512]{1,0:T(8,128)(2,1)S(1)}, bf16[64,512]{1,0:T(8,128)(2,1)S(1)}, u32[]{:S(2)}, u32[]{:S(2)}) collective-permute-start(bf16[64,512]{1,0:T(8,128)(2,1)S(1)} %shard_map.76.refs_0_), channel_id=1, source_target_pairs={{0,28},{4,24},{8,20},{12,16},{16,12},{20,8},{24,4},{28,0},{1,29},{... | collective-permute-start | bytes 196616 | tf_op jit(solution)/shard_map/ppermute | solution.py:25
  98.3 1.5 %collective-permute-start.35 = (bf16[64,512]{1,0:T(8,128)(2,1)S(1)}, bf16[64,512]{1,0:T(8,128)(2,1)S(1)}, u32[]{:S(2)}, u32[]{:S(2)}) collective-permute-start(bf16[64,512]{1,0:T(8,128)(2,1)S(1)} %shard_map.76.refs_0_), channel_id=1, source_target_pairs={{0,4},{4,0},{8,12},{12,8},{16,20},{20,16},{24,28},{28,24},{1,5},{5... | collective-permute-start | bytes 196616 | tf_op jit(solution)/shard_map/ppermute | solution.py:25
  99.9 2.7 %collective-permute-done.32.refs_4_ = bf16[64,512]{1,0:T(8,128)(2,1)S(1)} collective-permute-done((bf16[64,512]{1,0:T(8,128)(2,1)S(1)}, bf16[64,512]{1,0:T(8,128)(2,1)S(1)}, u32[]{:S(2)}, u32[]{:S(2)}) %collective-permute-start.32) | collective-permute-done | bytes 65568 | tf_op jit(solution)/shard_map/ppermute | solution.py:25
  103.9 1.8 %shard_map.77 = f32[512,512]{1,0:T(8,128)} custom-call(s32[4]{0:T(128)S(1)} %pad_add_fusion.scalars, bf16[64,512]{1,0:T(8,128)(2,1)S(1)} %shard_map.76.refs_0_, bf16[64,512]{1,0:T(8,128)(2,1)S(1)} %collective-permute-done.29.refs_1_, bf16[64,512]{1,0:T(8,128)(2,1)S(1)} %collective-permute-done.30.refs_2_, ...), custom_call_target="tpu_custom_call" | custom-call | tf_op jit(solution)/shard_map/pallas_call | solution.py:329
  (66 shorter events, 18.5 us)
Async XLA Ops:
  0.0 22.4 %collective-permute-start = (bf16[128,2048]{1,0:T(8,128)(2,1)}, bf16[128,2048]{1,0:T(8,128)(2,1)S(1)}, u32[]{:S(2)}, u32[]{:S(2)}) collective-permute-start(bf16[128,2048]{1,0:T(8,128)(2,1)} %param.6), channel_id=1, source_target_pairs={{0,4},{4,0},{8,12},{12,8},{16,20},{20,16},{24,28},{28,24},{1,5},{5... | collective-permute-start | bytes 1572872 | tf_op jit(solution)/shard_map/ppermute | solution.py:25
  4.0 14.1 %collective-permute-start.1 = (bf16[64,2048]{1,0:T(8,128)(2,1)S(1)}, bf16[64,2048]{1,0:T(8,128)(2,1)S(1)}, u32[]{:S(2)}, u32[]{:S(2)}) collective-permute-start(bf16[64,2048]{1,0:T(8,128)(2,1)S(1)} %get-tuple-element.102.refs_0_), channel_id=1, source_target_pairs={{0,8},{4,12},{8,0},{12,4},{16,24},{20,28},{24,16},{28,20},{1,9},{5... | collective-permute-start | bytes 786440 | tf_op jit(solution)/shard_map/ppermute | solution.py:25
  5.7 12.8 %collective-permute-start.7 = (bf16[64,2048]{1,0:T(8,128)(2,1)S(1)}, bf16[64,2048]{1,0:T(8,128)(2,1)S(1)}, u32[]{:S(2)}, u32[]{:S(2)}) collective-permute-start(bf16[64,2048]{1,0:T(8,128)(2,1)S(1)} %get-tuple-element.102.refs_0_), channel_id=1, source_target_pairs={{0,16},{4,20},{8,24},{12,28},{16,0},{20,4},{24,8},{28,12},{1,17},{... | collective-permute-start | bytes 786440 | tf_op jit(solution)/shard_map/ppermute | solution.py:25
  12.3 10.1 %collective-permute-start.3 = (bf16[272,128]{1,0:T(8,128)(2,1)S(1)}, bf16[272,128]{1,0:T(8,128)(2,1)S(1)}, u32[]{:S(2)}, u32[]{:S(2)}) collective-permute-start(bf16[272,128]{1,0:T(8,128)(2,1)S(1)} %get-tuple-element.54), channel_id=1, source_target_pairs={{0,8},{4,12},{8,0},{12,4},{16,24},{20,28},{24,16},{28,20},{1,9},{5... | collective-permute-start | bytes 208904 | tf_op jit(solution)/shard_map/ppermute | solution.py:25
  18.1 14.8 %collective-permute-start.2 = (bf16[64,2048]{1,0:T(8,128)(2,1)S(1)}, bf16[64,2048]{1,0:T(8,128)(2,1)S(1)}, u32[]{:S(2)}, u32[]{:S(2)}) collective-permute-start(bf16[64,2048]{1,0:T(8,128)(2,1)S(1)} %get-tuple-element.60.refs_1_), channel_id=1, source_target_pairs={{0,8},{4,12},{8,0},{12,4},{16,24},{20,28},{24,16},{28,20},{1,9},{5... | collective-permute-start | bytes 786440 | tf_op jit(solution)/shard_map/ppermute | solution.py:25
  18.4 11.0 %collective-permute-start.8 = (bf16[64,2048]{1,0:T(8,128)(2,1)S(1)}, bf16[64,2048]{1,0:T(8,128)(2,1)S(1)}, u32[]{:S(2)}, u32[]{:S(2)}) collective-permute-start(bf16[64,2048]{1,0:T(8,128)(2,1)S(1)} %get-tuple-element.60.refs_1_), channel_id=1, source_target_pairs={{0,16},{4,20},{8,24},{12,28},{16,0},{20,4},{24,8},{28,12},{1,17},{... | collective-permute-start | bytes 786440 | tf_op jit(solution)/shard_map/ppermute | solution.py:25
  22.4 10.5 %collective-permute-start.4 = (bf16[64,2048]{1,0:T(8,128)(2,1)S(1)}, bf16[64,2048]{1,0:T(8,128)(2,1)S(1)}, u32[]{:S(2)}, u32[]{:S(2)}) collective-permute-start(bf16[64,2048]{1,0:T(8,128)(2,1)S(1)} %collective-permute-done.1.refs_3_), channel_id=1, source_target_pairs={{0,4},{4,0},{8,12},{12,8},{16,20},{20,16},{24,28},{28,24},{1,5},{5... | collective-permute-start | bytes 786440 | tf_op jit(solution)/shard_map/ppermute | solution.py:25
  23.5 9.4 %collective-permute-start.5 = (bf16[144,256]{1,0:T(8,128)(2,1)S(1)}, bf16[144,256]{1,0:T(8,128)(2,1)S(1)}, u32[]{:S(2)}, u32[]{:S(2)}) collective-permute-start(bf16[144,256]{1,0:T(8,128)(2,1)S(1)} %get-tuple-element.58), channel_id=1, source_target_pairs={{0,4},{4,0},{8,12},{12,8},{16,20},{20,16},{24,28},{28,24},{1,5},{5... | collective-permute-start | bytes 221192 | tf_op jit(solution)/shard_map/ppermute | solution.py:25
  25.1 11.3 %collective-permute-start.13 = (bf16[64,2048]{1,0:T(8,128)(2,1)S(1)}, bf16[64,2048]{1,0:T(8,128)(2,1)S(1)}, u32[]{:S(2)}, u32[]{:S(2)}) collective-permute-start(bf16[64,2048]{1,0:T(8,128)(2,1)S(1)} %collective-permute-done.7.refs_7_), channel_id=1, source_target_pairs={{0,4},{4,0},{8,12},{12,8},{16,20},{20,16},{24,28},{28,24},{1,5},{5... | collective-permute-start | bytes 786440 | tf_op jit(solution)/shard_map/ppermute | solution.py:25
  29.4 9.2 %collective-permute-start.10 = (bf16[64,2048]{1,0:T(8,128)(2,1)S(1)}, bf16[64,2048]{1,0:T(8,128)(2,1)S(1)}, u32[]{:S(2)}, u32[]{:S(2)}) collective-permute-start(bf16[64,2048]{1,0:T(8,128)(2,1)S(1)} %collective-permute-done.8.refs_8_), channel_id=1, source_target_pairs={{0,8},{4,12},{8,0},{12,4},{16,24},{20,28},{24,16},{28,20},{1,9},{5... | collective-permute-start | bytes 786440 | tf_op jit(solution)/shard_map/ppermute | solution.py:25
  32.9 8.1 %collective-permute-start.6 = (bf16[64,2048]{1,0:T(8,128)(2,1)S(1)}, bf16[64,2048]{1,0:T(8,128)(2,1)S(1)}, u32[]{:S(2)}, u32[]{:S(2)}) collective-permute-start(bf16[64,2048]{1,0:T(8,128)(2,1)S(1)} %collective-permute-done.2.refs_4_), channel_id=1, source_target_pairs={{0,4},{4,0},{8,12},{12,8},{16,20},{20,16},{24,28},{28,24},{1,5},{5... | collective-permute-start | bytes 786440 | tf_op jit(solution)/shard_map/ppermute | solution.py:25
  34.1 10.1 %collective-permute-start.9 = (bf16[64,2048]{1,0:T(8,128)(2,1)S(1)}, bf16[64,2048]{1,0:T(8,128)(2,1)S(1)}, u32[]{:S(2)}, u32[]{:S(2)}) collective-permute-start(bf16[64,2048]{1,0:T(8,128)(2,1)S(1)} %collective-permute-done.7.refs_7_), channel_id=1, source_target_pairs={{0,8},{4,12},{8,0},{12,4},{16,24},{20,28},{24,16},{28,20},{1,9},{5... | collective-permute-start | bytes 786440 | tf_op jit(solution)/shard_map/ppermute | solution.py:25
  34.8 12.1 %collective-permute-start.12 = (bf16[128,512]{1,0:T(8,128)(2,1)S(1)}, bf16[128,512]{1,0:T(8,128)(2,1)S(1)}, u32[]{:S(2)}, u32[]{:S(2)}) collective-permute-start(bf16[128,512]{1,0:T(8,128)(2,1)S(1)} %pad_maximum_fusion), channel_id=1, source_target_pairs={{0,2},{1,3},{2,0},{3,1},{4,6},{5,7},{6,4},{7,5},{8,10},{9,11},{10,... | collective-permute-start | bytes 393224 | tf_op jit(solution)/shard_map/ppermute | solution.py:25
  36.3 15.9 %collective-permute-start.14 = (bf16[64,2048]{1,0:T(8,128)(2,1)S(1)}, bf16[64,2048]{1,0:T(8,128)(2,1)S(1)}, u32[]{:S(2)}, u32[]{:S(2)}) collective-permute-start(bf16[64,2048]{1,0:T(8,128)(2,1)S(1)} %collective-permute-done.8.refs_8_), channel_id=1, source_target_pairs={{0,4},{4,0},{8,12},{12,8},{16,20},{20,16},{24,28},{28,24},{1,5},{5... | collective-permute-start | bytes 786440 | tf_op jit(solution)/shard_map/ppermute | solution.py:25
  38.6 13.6 %collective-permute-start.15 = (bf16[64,2048]{1,0:T(8,128)(2,1)S(1)}, bf16[64,2048]{1,0:T(8,128)(2,1)S(1)}, u32[]{:S(2)}, u32[]{:S(2)}) collective-permute-start(bf16[64,2048]{1,0:T(8,128)(2,1)S(1)} %collective-permute-done.13.refs_0_), channel_id=1, source_target_pairs={{0,8},{4,12},{8,0},{12,4},{16,24},{20,28},{24,16},{28,20},{1,9},{5... | collective-permute-start | bytes 786440 | tf_op jit(solution)/shard_map/ppermute | solution.py:25
  41.0 11.2 %collective-permute-start.16 = (bf16[64,2048]{1,0:T(8,128)(2,1)S(1)}, bf16[64,2048]{1,0:T(8,128)(2,1)S(1)}, u32[]{:S(2)}, u32[]{:S(2)}) collective-permute-start(bf16[64,2048]{1,0:T(8,128)(2,1)S(1)} %collective-permute-done.10.refs_10_), channel_id=1, source_target_pairs={{0,4},{4,0},{8,12},{12,8},{16,20},{20,16},{24,28},{28,24},{1,5},{5... | collective-permute-start | bytes 786440 | tf_op jit(solution)/shard_map/ppermute | solution.py:25
  44.2 5.6 %collective-permute-start.17 = (bf16[80,512]{1,0:T(8,128)(2,1)S(1)}, bf16[80,512]{1,0:T(8,128)(2,1)S(1)}, u32[]{:S(2)}, u32[]{:S(2)}) collective-permute-start(bf16[80,512]{1,0:T(8,128)(2,1)S(1)} %get-tuple-element.73), channel_id=1, source_target_pairs={{0,16},{4,20},{8,24},{12,28},{16,0},{20,4},{24,8},{28,12},{1,17},{... | collective-permute-start | bytes 245768 | tf_op jit(solution)/shard_map/ppermute | solution.py:25
  54.0 1.6 %collective-permute-start.18 = (bf16[128,1024]{1,0:T(8,128)(2,1)S(1)}, bf16[128,1024]{1,0:T(8,128)(2,1)S(1)}, u32[]{:S(2)}, u32[]{:S(2)}) collective-permute-start(bf16[128,1024]{1,0:T(8,128)(2,1)S(1)} %get-tuple-element.81), channel_id=1, source_target_pairs={{0,1},{1,0},{2,3},{3,2},{4,5},{5,4},{6,7},{7,6},{8,9},{9,8},{10,11... | collective-permute-start | bytes 786440 | tf_op jit(solution)/shard_map/ppermute | solution.py:25
  55.6 8.4 %collective-permute-start.24 = (bf16[128,1024]{1,0:T(8,128)(2,1)S(1)}, bf16[128,1024]{1,0:T(8,128)(2,1)S(1)}, u32[]{:S(2)}, u32[]{:S(2)}) collective-permute-start(bf16[128,1024]{1,0:T(8,128)(2,1)S(1)} %get-tuple-element.91), channel_id=1, source_target_pairs={{0,2},{1,3},{2,0},{3,1},{4,6},{5,7},{6,4},{7,5},{8,10},{9,11},{10,... | collective-permute-start | bytes 786440 | tf_op jit(solution)/shard_map/ppermute | solution.py:25
  59.2 7.5 %collective-permute-start.19 = (bf16[128,2048]{1,0:T(8,128)(2,1)S(1)}, bf16[128,2048]{1,0:T(8,128)(2,1)S(1)}, u32[]{:S(2)}, u32[]{:S(2)}) collective-permute-start(bf16[128,2048]{1,0:T(8,128)(2,1)S(1)} %get-tuple-element.86), channel_id=1, source_target_pairs={{0,1},{1,0},{2,3},{3,2},{4,5},{5,4},{6,7},{7,6},{8,9},{9,8},{10,11... | collective-permute-start | bytes 1572872 | tf_op jit(solution)/shard_map/ppermute | solution.py:25
  59.3 7.5 %collective-permute-start.20 = (bf16[128,2048]{1,0:T(8,128)(2,1)S(1)}, bf16[128,2048]{1,0:T(8,128)(2,1)S(1)}, u32[]{:S(2)}, u32[]{:S(2)}) collective-permute-start(bf16[128,2048]{1,0:T(8,128)(2,1)S(1)} %get-tuple-element.87), channel_id=1, source_target_pairs={{0,1},{1,0},{2,3},{3,2},{4,5},{5,4},{6,7},{7,6},{8,9},{9,8},{10,11... | collective-permute-start | bytes 1572872 | tf_op jit(solution)/shard_map/ppermute | solution.py:25
  59.8 7.0 %collective-permute-start.21 = (bf16[128,2048]{1,0:T(8,128)(2,1)S(1)}, bf16[128,2048]{1,0:T(8,128)(2,1)S(1)}, u32[]{:S(2)}, u32[]{:S(2)}) collective-permute-start(bf16[128,2048]{1,0:T(8,128)(2,1)S(1)} %get-tuple-element.88), channel_id=1, source_target_pairs={{0,1},{1,0},{2,3},{3,2},{4,5},{5,4},{6,7},{7,6},{8,9},{9,8},{10,11... | collective-permute-start | bytes 1572872 | tf_op jit(solution)/shard_map/ppermute | solution.py:25
  59.9 6.9 %collective-permute-start.22 = (bf16[128,2048]{1,0:T(8,128)(2,1)S(1)}, bf16[128,2048]{1,0:T(8,128)(2,1)S(1)}, u32[]{:S(2)}, u32[]{:S(2)}) collective-permute-start(bf16[128,2048]{1,0:T(8,128)(2,1)S(1)} %get-tuple-element.89), channel_id=1, source_target_pairs={{0,1},{1,0},{2,3},{3,2},{4,5},{5,4},{6,7},{7,6},{8,9},{9,8},{10,11... | collective-permute-start | bytes 1572872 | tf_op jit(solution)/shard_map/ppermute | solution.py:25
  69.8 8.4 %collective-permute-start.26 = (bf16[64,2048]{1,0:T(8,128)(2,1)S(1)}, bf16[64,2048]{1,0:T(8,128)(2,1)S(1)}, u32[]{:S(2)}, u32[]{:S(2)}) collective-permute-start(bf16[64,2048]{1,0:T(8,128)(2,1)S(1)} %get-tuple-element.96), channel_id=1, source_target_pairs={{0,2},{1,3},{2,0},{3,1},{4,6},{5,7},{6,4},{7,5},{8,10},{9,11},{10,... | collective-permute-start | bytes 786440 | tf_op jit(solution)/shard_map/ppermute | solution.py:25
  83.1 4.3 %collective-permute-start.28 = (bf16[64,512]{1,0:T(8,128)(2,1)S(1)}, bf16[64,512]{1,0:T(8,128)(2,1)S(1)}, u32[]{:S(2)}, u32[]{:S(2)}) collective-permute-start(bf16[64,512]{1,0:T(8,128)(2,1)S(1)} %get-tuple-element.100), channel_id=1, source_target_pairs={{0,2},{1,3},{2,0},{3,1},{4,6},{5,7},{6,4},{7,5},{8,10},{9,11},{10,... | collective-permute-start | bytes 196616 | tf_op jit(solution)/shard_map/ppermute | solution.py:25
  87.4 10.8 %collective-permute-start.29 = (bf16[64,512]{1,0:T(8,128)(2,1)S(1)}, bf16[64,512]{1,0:T(8,128)(2,1)S(1)}, u32[]{:S(2)}, u32[]{:S(2)}) collective-permute-start(bf16[64,512]{1,0:T(8,128)(2,1)S(1)} %shard_map.76.refs_0_), channel_id=1, source_target_pairs={{0,16},{4,20},{8,24},{12,28},{16,0},{20,4},{24,8},{28,12},{1,17},{... | collective-permute-start | bytes 196616 | tf_op jit(solution)/shard_map/ppermute | solution.py:25
  91.0 7.4 %collective-permute-start.30 = (bf16[64,512]{1,0:T(8,128)(2,1)S(1)}, bf16[64,512]{1,0:T(8,128)(2,1)S(1)}, u32[]{:S(2)}, u32[]{:S(2)}) collective-permute-start(bf16[64,512]{1,0:T(8,128)(2,1)S(1)} %shard_map.76.refs_0_), channel_id=1, source_target_pairs={{0,24},{4,28},{8,16},{12,20},{16,8},{20,12},{24,0},{28,4},{1,25},{... | collective-permute-start | bytes 196616 | tf_op jit(solution)/shard_map/ppermute | solution.py:25
  93.0 6.9 %collective-permute-start.31 = (bf16[64,512]{1,0:T(8,128)(2,1)S(1)}, bf16[64,512]{1,0:T(8,128)(2,1)S(1)}, u32[]{:S(2)}, u32[]{:S(2)}) collective-permute-start(bf16[64,512]{1,0:T(8,128)(2,1)S(1)} %shard_map.76.refs_0_), channel_id=1, source_target_pairs={{0,8},{4,12},{8,0},{12,4},{16,24},{20,28},{24,16},{28,20},{1,9},{5... | collective-permute-start | bytes 196616 | tf_op jit(solution)/shard_map/ppermute | solution.py:25
  93.2 9.3 %collective-permute-start.32 = (bf16[64,512]{1,0:T(8,128)(2,1)S(1)}, bf16[64,512]{1,0:T(8,128)(2,1)S(1)}, u32[]{:S(2)}, u32[]{:S(2)}) collective-permute-start(bf16[64,512]{1,0:T(8,128)(2,1)S(1)} %shard_map.76.refs_0_), channel_id=1, source_target_pairs={{0,20},{4,16},{8,28},{12,24},{16,4},{20,0},{24,12},{28,8},{1,21},{... | collective-permute-start | bytes 196616 | tf_op jit(solution)/shard_map/ppermute | solution.py:25
  95.3 7.2 %collective-permute-start.33 = (bf16[64,512]{1,0:T(8,128)(2,1)S(1)}, bf16[64,512]{1,0:T(8,128)(2,1)S(1)}, u32[]{:S(2)}, u32[]{:S(2)}) collective-permute-start(bf16[64,512]{1,0:T(8,128)(2,1)S(1)} %shard_map.76.refs_0_), channel_id=1, source_target_pairs={{0,28},{4,24},{8,20},{12,16},{16,12},{20,8},{24,4},{28,0},{1,29},{... | collective-permute-start | bytes 196616 | tf_op jit(solution)/shard_map/ppermute | solution.py:25
  98.3 5.2 %collective-permute-start.34 = (bf16[64,512]{1,0:T(8,128)(2,1)S(1)}, bf16[64,512]{1,0:T(8,128)(2,1)S(1)}, u32[]{:S(2)}, u32[]{:S(2)}) collective-permute-start(bf16[64,512]{1,0:T(8,128)(2,1)S(1)} %shard_map.76.refs_0_), channel_id=1, source_target_pairs={{0,12},{4,8},{8,4},{12,0},{16,28},{20,24},{24,20},{28,16},{1,13},{... | collective-permute-start | bytes 196616 | tf_op jit(solution)/shard_map/ppermute | solution.py:25
  98.3 5.5 %collective-permute-start.35 = (bf16[64,512]{1,0:T(8,128)(2,1)S(1)}, bf16[64,512]{1,0:T(8,128)(2,1)S(1)}, u32[]{:S(2)}, u32[]{:S(2)}) collective-permute-start(bf16[64,512]{1,0:T(8,128)(2,1)S(1)} %shard_map.76.refs_0_), channel_id=1, source_target_pairs={{0,4},{4,0},{8,12},{12,8},{16,20},{20,16},{24,28},{28,24},{1,5},{5... | collective-permute-start | bytes 196616 | tf_op jit(solution)/shard_map/ppermute | solution.py:25
  (7 other events, 12.3 us)
